TPU v7x, 32 devices: a whole 2x2x4 slice. The times are simulated.
32 devices in a mesh: tm: 8 (over y, x, core), tile: 4 (over z).
Axes of the slice: x: 2, y: 2, z: 4, core: 2. Of those that a mesh axis runs over, the one named last changes fastest.
Arguments:
- seg_gain: bfloat16 [8, 1024, 1024], P('tm', 'tile'), may hold values from -0.1875 to 0.1875
- seg_offset: float32 [8, 1024], P('tm', 'tile'), may hold values from -6 to 6
- seg_noise: bfloat16 [8, 1024, 1024], P('tm', 'tile'), as said below
- end_mean: bfloat16 [2, 1024], P(None, 'tile'), may hold values from -6 to 6
- end_cov: bfloat16 [2, 1024, 1024], P(None, 'tile'), as said below
- step_gain: bfloat16 [64, 1024, 1024], P('tm', 'tile'), may hold values from -0.1875 to 0.1875
- step_offset: float32 [64, 1024], P('tm', 'tile'), may hold values from -6 to 6
- step_var: float32 [64, 1024], P('tm', 'tile'), may hold values from 0.1 to 1.5
- obs_tiles: int32 [64, 4], P('tm'), may hold values from 0 to 7
- obs_count: int32 [64], P('tm'), may hold values from 1 to 4, as said below
- obs_value: float32 [64, 4, 128], P('tm'), may hold values from -10 to 10
- obs_noise: float32 [1024], replicated, may hold values from 0.2 to 2
Outputs:
- start_cov: bfloat16 [8, 1024, 1024], P('tm', 'tile')
- start_mean: bfloat16 [8, 1024], P('tm', 'tile')
- step_mean: float32 [64, 1024], P('tm', 'tile')
- step_spread: float32 [64, 1024], P('tm', 'tile')
- innovation: float32 [64, 4, 128], P('tm')
Inputs may be any that keep to these rules, and one draw needn't show every extreme that they name: `end_cov`: each matrix is symmetric and positive definite. `seg_noise`: each matrix is symmetric and positive definite. `obs_count`: some step has 4 live slots and some has 1.
All inputs are finite; a program needn't handle non-finite values.
Results may differ from a plain program's by a relative error of at most 0.015.
Values may be sent and summed in bfloat16 or wider, within the bound.
No kernel may reach another device: no remote copies, remote signals or barrier semaphores. Data moves between devices by JAX's collectives and lax.ppermute only.
A program may use at most 64 MiB of HBM per device.

v0:
```python
import jax
import jax.numpy as jnp
from jax import lax
from jax.sharding import PartitionSpec as P

TILE_STATES = 128
SLOTS = 4
GROUP_SEGS = 4


def shifted(block, axis, distance):
    devices = range(lax.axis_size(axis))
    route = [(i - distance, i) for i in devices if i - distance in devices]
    return lax.ppermute(block, axis, route)


def shards(
    seg_gain,
    seg_offset,
    seg_noise,
    end_mean,
    end_cov,
    step_gain,
    step_offset,
    step_var,
    obs_tiles,
    obs_count,
    obs_value,
    obs_noise,
):
    position = lax.axis_index("tm")
    slot_place = position % GROUP_SEGS
    group_index = position // GROUP_SEGS
    gain_rows = seg_gain[0]
    offset_rows = seg_offset[0]
    noise_rows = seg_noise[0].astype(jnp.float32)
    row_count = gain_rows.shape[0]
    state_count = gain_rows.shape[1]
    cur_mean = lax.dynamic_index_in_dim(end_mean, group_index, 0, keepdims=False)
    cur_cov = lax.dynamic_index_in_dim(end_cov, group_index, 0, keepdims=False)
    kept_mean = jnp.zeros((state_count,), jnp.bfloat16)
    kept_cov = jnp.zeros((state_count, state_count), jnp.bfloat16)
    out_mean = jnp.zeros((row_count,), jnp.bfloat16)
    out_cov = jnp.zeros((row_count, state_count), jnp.bfloat16)
    for depth_step in range(GROUP_SEGS):
        whole_mean, whole_cov = (
            lax.all_gather(cur_mean, "tile", axis=0, tiled=True),
            lax.all_gather(cur_cov, "tile", axis=0, tiled=True),
        )
        is_mine = slot_place == GROUP_SEGS - 1 - depth_step
        kept_mean = jnp.where(is_mine, whole_mean, kept_mean)
        kept_cov = jnp.where(is_mine, whole_cov, kept_cov)
        product = jnp.dot(gain_rows, whole_cov, preferred_element_type=jnp.float32).astype(
            jnp.bfloat16
        )
        col_block = jnp.einsum(
            "pd,rd->pr",
            lax.all_gather(product, "tile", axis=0, tiled=True),
            gain_rows,
            preferred_element_type=jnp.float32,
        )
        spread_rows = lax.all_to_all(col_block, "tile", split_axis=0, concat_axis=1, tiled=True)
        new_cov = (spread_rows + noise_rows).astype(jnp.bfloat16)
        new_mean = (
            jnp.dot(gain_rows, whole_mean, preferred_element_type=jnp.float32) + offset_rows
        ).astype(jnp.bfloat16)
        out_mean = jnp.where(is_mine, new_mean, out_mean)
        out_cov = jnp.where(is_mine, new_cov, out_cov)
        if depth_step < GROUP_SEGS - 1:
            got_mean, got_cov = shifted((new_mean, new_cov), "tm", -1)
            takes_next = slot_place == GROUP_SEGS - 2 - depth_step
            cur_mean = jnp.where(takes_next, got_mean, cur_mean)
            cur_cov = jnp.where(takes_next, got_cov, cur_cov)
    partial_value = jnp.einsum(
        "krd,de->kre", step_gain, kept_cov, preferred_element_type=jnp.float32
    )
    local_spread = jnp.sum(partial_value * step_gain, axis=2) + step_var
    local_mean = (
        jnp.einsum("krd,d->kr", step_gain, kept_mean, preferred_element_type=jnp.float32)
        + step_offset
    )
    full_mean, full_spread = (
        lax.all_gather(local_mean, "tile", axis=1, tiled=True),
        lax.all_gather(local_spread, "tile", axis=1, tiled=True),
    )
    step_count = full_mean.shape[0]
    tile_total = state_count // TILE_STATES
    tile_mean = full_mean.reshape(step_count, tile_total, TILE_STATES)
    tile_spread = full_spread.reshape(step_count, tile_total, TILE_STATES) + obs_noise.reshape(
        1, tile_total, TILE_STATES
    )
    onehot = (
        obs_tiles[:, :, None] == jnp.arange(tile_total, dtype=jnp.int32)[None, None, :]
    ).astype(jnp.float32)
    picked_mean = jnp.einsum("ksn,kno->kso", onehot, tile_mean, precision=lax.Precision.HIGHEST)
    picked_spread = jnp.einsum("ksn,kno->kso", onehot, tile_spread, precision=lax.Precision.HIGHEST)
    live_slots = jnp.arange(SLOTS, dtype=jnp.int32)[None, :] < obs_count[:, None]
    innovation = jnp.where(
        live_slots[:, :, None], (obs_value - picked_mean) / picked_spread, jnp.float32(0.0)
    )
    return (out_cov[None], out_mean[None], local_mean, local_spread, innovation)


def solution(mesh):
    in_specs = (
        P("tm", "tile", None),
        P("tm", "tile"),
        P("tm", "tile", None),
        P(None, "tile"),
        P(None, "tile", None),
        P("tm", "tile", None),
        P("tm", "tile"),
        P("tm", "tile"),
        P("tm", None),
        P("tm"),
        P("tm", None, None),
        P(),
    )
    out_specs = (
        P("tm", "tile", None),
        P("tm", "tile"),
        P("tm", "tile"),
        P("tm", "tile"),
        P("tm", None, None),
    )
    return jax.shard_map(shards, mesh=mesh, in_specs=in_specs, out_specs=out_specs, check_vma=False)
```

profile of v0, /device:TPU:0, one launch (start us, length us, event | category | flops | bytes accessed | tf_op | source)
XLA Modules:
  0.0 608.5 jit_solution(8157675636723825516)
XLA Ops:
  7.3 1.1 copy-done
  8.4 1.0 copy.64
  9.5 49.6 %all-gather.28.cloned.1.call-done = bf16[1,1024,1024]{1,2,0:T(8,128)(2,1)} async-done(((bf16[1,256,1024]{1,2,0:T(8,128)(2,1)}), bf16[1,1024,1024]{1,2,0:T(8,128)(2,1)}) %all-gather.28.cloned.1.call-update) | async-done | bytes 2097168 | tf_op jit(solution)/shard_map/all_gather | solution.py:48
  59.1 3.1 fusion.21
  62.3 44.6 %all-gather.14.cloned.1.call-done = bf16[1024,1024]{0,1:T(8,128)(2,1)} async-done(((bf16[256,1024]{0,1:T(8,128)(2,1)}), bf16[1024,1024]{0,1:T(8,128)(2,1)}) %all-gather.14.cloned.1.call-update) | async-done | bytes 2097168 | tf_op jit(solution)/shard_map/all_gather | solution.py:58
  106.9 3.9 copy.60
  110.9 3.3 fusion.43
  114.2 3.5 all-to-all-start
  117.8 1.2 copy.45
  119.0 24.0 %all-to-all-done = f32[4,256,256]{2,1,0:T(8,128)S(1)} async-done(((f32[4,256,256]{2,1,0:T(8,128)}), f32[4,256,256]{2,1,0:T(8,128)S(1)}, u32[]{:S(2)}, u32[]{:S(2)}) %all-to-all-start) | async-done | bytes 1048608 | tf_op jit(solution)/shard_map/all_to_all | solution.py:62
  143.0 1.0 copy-done.2
  144.0 1.6 copy.44
  145.6 0.9 fusion.25
  146.5 1.3 collective-permute-start
  147.8 2.8 collective-permute-done
  150.6 1.9 bitcast_select_fusion.1
  152.6 51.8 %all-gather.16.cloned.1.call-done = bf16[1024,1024]{0,1:T(8,128)(2,1)} async-done(((bf16[256,1024]{0,1:T(8,128)(2,1)}), bf16[1024,1024]{0,1:T(8,128)(2,1)}) %all-gather.16.cloned.1.call-update) | async-done | bytes 2097168 | tf_op jit(solution)/shard_map/all_gather | solution.py:48
  204.5 3.2 fusion.18
  207.7 44.6 %all-gather.18.cloned.1.call-done = bf16[1024,1024]{0,1:T(8,128)(2,1)} async-done(((bf16[256,1024]{0,1:T(8,128)(2,1)}), bf16[1024,1024]{0,1:T(8,128)(2,1)}) %all-gather.18.cloned.1.call-update) | async-done | bytes 2097168 | tf_op jit(solution)/shard_map/all_gather | solution.py:58
  252.3 3.9 copy.61
  256.2 2.3 fusion.41
  258.5 28.5 %all_to_all.73 = f32[4,256,256]{2,1,0:T(8,128)} all-to-all(f32[4,256,256]{2,1,0:T(8,128)S(1)} %fusion.41), channel_id=1, replica_groups=mesh['tm'=8,'tile'=4] {'tile'}, dimensions={0} | all-to-all | bytes 2097152 | tf_op jit(solution)/shard_map/all_to_all | solution.py:62
  287.0 2.6 copy.47
  289.6 2.2 fusion.26
  291.7 1.3 collective-permute-start.1
  293.0 2.8 collective-permute-done.1
  295.9 1.9 broadcast_select_fusion
  297.8 52.1 %all-gather.20.cloned.1.call-done = bf16[1024,1024]{0,1:T(8,128)(2,1)} async-done(((bf16[256,1024]{0,1:T(8,128)(2,1)}), bf16[1024,1024]{0,1:T(8,128)(2,1)}) %all-gather.20.cloned.1.call-update) | async-done | bytes 2097168 | tf_op jit(solution)/shard_map/all_gather | solution.py:48
  349.9 3.2 fusion.19
  353.1 44.6 %all-gather.22.cloned.1.call-done = bf16[1024,1024]{0,1:T(8,128)(2,1)} async-done(((bf16[256,1024]{0,1:T(8,128)(2,1)}), bf16[1024,1024]{0,1:T(8,128)(2,1)}) %all-gather.22.cloned.1.call-update) | async-done | bytes 2097168 | tf_op jit(solution)/shard_map/all_gather | solution.py:58
  397.7 3.9 copy.62
  401.6 2.3 fusion.39
  404.0 28.5 %all_to_all.74 = f32[4,256,256]{2,1,0:T(8,128)} all-to-all(f32[4,256,256]{2,1,0:T(8,128)S(1)} %fusion.39), channel_id=1, replica_groups=mesh['tm'=8,'tile'=4] {'tile'}, dimensions={0} | all-to-all | bytes 2097152 | tf_op jit(solution)/shard_map/all_to_all | solution.py:62
  432.5 2.5 copy.49
  435.0 2.2 fusion.27
  437.2 1.3 collective-permute-start.2
  438.5 2.8 collective-permute-done.2
  441.3 1.9 broadcast_select_fusion.1
  443.3 9.0 %all-gather.1 = bf16[1,1024]{1,0:T(2,128)(2,1)S(1)} all-gather(bf16[1,256]{1,0:T(2,128)(2,1)S(1)} %get-tuple-element.16), channel_id=3, replica_groups=mesh['tm'=8,'tile'=4] {'tile'}, dimensions={1}, use_global_device_ids=true | all-gather | bytes 2560 | tf_op jit(solution)/shard_map/all_gather | solution.py:47
  452.3 0.3 fusion.54
  452.6 1.3 collective-permute-start.3
  453.9 41.4 %all-gather.24.cloned.1.call-done = bf16[1024,1024]{0,1:T(8,128)(2,1)} async-done(((bf16[256,1024]{0,1:T(8,128)(2,1)}), bf16[1024,1024]{0,1:T(8,128)(2,1)}) %all-gather.24.cloned.1.call-update) | async-done | bytes 2097168 | tf_op jit(solution)/shard_map/all_gather | solution.py:48
  495.4 3.1 fusion.20
  498.5 8.3 %all-gather.2 = bf16[4,1,256]{2,1,0:T(2,128)(2,1)S(1)} all-gather(bf16[1,1,256]{2,1,0:T(2,128)(2,1)S(1)} %reshape.67), channel_id=1, replica_groups=mesh['tm'=8,'tile'=4] {'tile'}, dimensions={0}, use_global_device_ids=true | all-gather | bytes 2560 | tf_op jit(solution)/shard_map/all_gather | solution.py:47
  507.0 1.3 collective-permute-start.4
  508.5 1.6 collective-permute-done.4
  510.1 11.0 %all-gather.3 = bf16[4,1,256]{2,1,0:T(2,128)(2,1)S(1)} all-gather(bf16[1,1,256]{2,1,0:T(2,128)(2,1)S(1)} %reshape.69), channel_id=1, replica_groups=mesh['tm'=8,'tile'=4] {'tile'}, dimensions={0}, use_global_device_ids=true | all-gather | bytes 2560 | tf_op jit(solution)/shard_map/all_gather | solution.py:47
  521.1 0.2 fusion.48
  521.4 1.4 collective-permute-start.5
  522.8 6.5 %copy.55 = bf16[8,256,1024]{1,2,0:T(8,128)(2,1)} copy(bf16[8,256,1024]{2,1,0:T(8,128)(2,1)} %param.17) | data formatting | bytes 8388608 | tf_op args[5]
  529.5 7.7 %all-gather.4 = bf16[4,1,256]{2,1,0:T(2,128)(2,1)S(1)} all-gather(bf16[1,1,256]{2,1,0:T(2,128)(2,1)S(1)} %reshape.71), channel_id=1, replica_groups=mesh['tm'=8,'tile'=4] {'tile'}, dimensions={0}, use_global_device_ids=true | all-gather | bytes 2560 | tf_op jit(solution)/shard_map/all_gather | solution.py:47
  537.2 0.2 fusion.51
  537.4 0.6 broadcast_in_dim.35
  538.0 3.4 fusion.65
  541.4 13.3 %all_gather.54 = f32[8,1024]{1,0:T(8,128)S(1)} all-gather(f32[8,256]{1,0:T(8,128)S(1)} %bitcast_add_fusion), channel_id=1, replica_groups=mesh['tm'=8,'tile'=4] {'tile'}, dimensions={1}, use_global_device_ids=true | all-gather | bytes 40960 | tf_op jit(solution)/shard_map/all_gather | solution.py:83
  555.0 3.9 copy.63
  559.0 3.3 fusion.37
  562.3 4.4 all-to-all-start.3
  566.7 9.4 %fusion = f32[8,256]{1,0:T(8,128)S(1)} fusion(bf16[8,256,1024]{1,2,0:T(8,128)(2,1)} %copy.55, bf16[8,256,1024]{2,1,0:T(8,128)(2,1)} %param.17, bf16[1024,1024]{0,1:T(8,128)(2,1)} %all-gather.24.cloned.1.call-done, bf16[1024,1024]{0,1:T(8,128)(2,1)} %all-gather.20.cloned.1.call-done, bf16[1024,1024]{0,1:T(8,128)(2,1)} %all-gather.16.cloned.1.call-done, ...), kind=kOutput, calls=%fused_computation.1 | convolution fusion | flops 4305451008 | bytes 16785412 | tf_op jit(solution)/shard_map/krd,de->kre/dot_general | solution.py:74
  576.2 18.8 %all_gather.55 = f32[8,1024]{1,0:T(8,128)S(1)} all-gather(f32[8,256]{1,0:T(8,128)S(1)} %add.75), channel_id=1, replica_groups=mesh['tm'=8,'tile'=4] {'tile'}, dimensions={1}, use_global_device_ids=true | all-gather | bytes 40960 | tf_op jit(solution)/shard_map/all_gather | solution.py:84
  595.0 0.8 fusion.24
  595.9 2.5 copy.51
  598.4 2.2 fusion.36
  600.6 1.0 copy.58
  (71 shorter events, 1.4 us)
Async XLA Ops:
  7.2 1.2 copy-start
  7.2 52.0 %copy-start.1 = (bf16[1,256,1024]{2,1,0:T(8,128)(2,1)S(1)}, bf16[1,256,1024]{2,1,0:T(8,128)(2,1)}, u32[]{:S(2)}) copy-start(bf16[1,256,1024]{2,1,0:T(8,128)(2,1)} %param.12) | copy-start | bytes 1572868
  7.2 51.9 %all-gather.28.cloned.1.call-start = ((), (), s32[]{:S(2)}) async-start(), calls=%async_computation.11 | async-start | bytes 2621440 | tf_op jit(solution)/shard_map/all_gather | solution.py:48
  9.5 97.5 %all-gather.14.cloned.1.call-start = ((), (), s32[]{:S(2)}) async-start(), calls=%async_computation.4 | async-start | bytes 2621440 | tf_op jit(solution)/shard_map/all_gather | solution.py:58
  114.2 28.8 %all-to-all-start = ((f32[4,256,256]{2,1,0:T(8,128)}), f32[4,256,256]{2,1,0:T(8,128)S(1)}, u32[]{:S(2)}, u32[]{:S(2)}) async-start(f32[4,256,256]{2,1,0:T(8,128)} %fusion.43), calls=%async_computation | async-start | bytes 2097152 | tf_op jit(solution)/shard_map/all_to_all | solution.py:62
  117.7 86.7 %all-gather.16.cloned.1.call-start = ((), (), s32[]{:S(2)}) async-start(), calls=%async_computation.5 | async-start | bytes 2621440 | tf_op jit(solution)/shard_map/all_gather | solution.py:48
  143.0 1.0 copy-start.2
  146.5 4.1 collective-permute-start
  152.6 99.7 %all-gather.18.cloned.1.call-start = ((), (), s32[]{:S(2)}) async-start(), calls=%async_computation.6 | async-start | bytes 2621440 | tf_op jit(solution)/shard_map/all_gather | solution.py:58
  207.6 142.3 %all-gather.20.cloned.1.call-start = ((), (), s32[]{:S(2)}) async-start(), calls=%async_computation.7 | async-start | bytes 2621440 | tf_op jit(solution)/shard_map/all_gather | solution.py:48
  291.7 4.1 collective-permute-start.1
  297.8 99.9 %all-gather.22.cloned.1.call-start = ((), (), s32[]{:S(2)}) async-start(), calls=%async_computation.8 | async-start | bytes 2621440 | tf_op jit(solution)/shard_map/all_gather | solution.py:58
  353.1 142.3 %all-gather.24.cloned.1.call-start = ((), (), s32[]{:S(2)}) async-start(), calls=%async_computation.9 | async-start | bytes 2621440 | tf_op jit(solution)/shard_map/all_gather | solution.py:48
  435.0 8.3 %copy-start.10 = (bf16[2,256]{1,0:T(2,128)(2,1)S(1)}, bf16[2,256]{1,0:T(2,128)(2,1)}, u32[]{:S(2)}) copy-start(bf16[2,256]{1,0:T(2,128)(2,1)} %param.15) | copy-start | bytes 3076
  435.0 17.6 %copy-start.6 = (f32[1,256]{1,0:T(1,128)S(1)}, f32[1,256]{1,0:T(1,128)}, u32[]{:S(2)}) copy-start(f32[1,256]{1,0:T(1,128)} %param.13) | copy-start | bytes 3076
  437.2 4.1 collective-permute-start.2
  443.2 111.8 %all-gather.26.cloned.1.call-start = ((), (), s32[]{:S(2)}) async-start(), calls=%async_computation.10 | async-start | bytes 2621440 | tf_op jit(solution)/shard_map/all_gather | solution.py:58
  452.6 55.8 %copy-start.12 = (s32[8]{0:T(128)S(1)}, s32[8]{0:T(128)}, u32[]{:S(2)}) copy-start(s32[8]{0:T(128)} %param.21) | copy-start | bytes 100
  452.6 45.9 %collective-permute-start.3 = (bf16[256]{0:T(256)(128)(2,1)S(1)}, bf16[256]{0:T(256)(128)(2,1)S(1)}, u32[]{:S(2)}, u32[]{:S(2)}) collective-permute-start(bf16[256]{0:T(256)(128)(2,1)S(1)} %add_convert_fusion.3), channel_id=1, source_target_pairs={{4,0},{8,4},{12,8},{16,12},{20,16},{24,20},{28,24},{5,1},{9,5},{13... | collective-permute-start | bytes 1544 | tf_op jit(solution)/shard_map/ppermute | solution.py:14
  507.0 3.0 collective-permute-start.4
  521.4 7.9 %copy-start.9 = (s32[8,4]{0,1:T(4,128)S(1)}, s32[8,4]{0,1:T(4,128)}, u32[]{:S(2)}) copy-start(s32[8,4]{0,1:T(4,128)} %param.20) | copy-start | bytes 388
  521.4 8.1 %collective-permute-start.5 = (bf16[256]{0:T(256)(128)(2,1)S(1)}, bf16[256]{0:T(256)(128)(2,1)S(1)}, u32[]{:S(2)}, u32[]{:S(2)}) collective-permute-start(bf16[256]{0:T(256)(128)(2,1)S(1)} %add_convert_fusion.1), channel_id=1, source_target_pairs={{4,0},{8,4},{12,8},{16,12},{20,16},{24,20},{28,24},{5,1},{9,5},{13... | collective-permute-start | bytes 1544 | tf_op jit(solution)/shard_map/ppermute | solution.py:14
  538.0 3.4 copy-start.7
  538.0 16.7 %copy-start.5 = (f32[8,4,128]{2,1,0:T(4,128)S(1)}, f32[8,4,128]{2,1,0:T(4,128)}, u32[]{:S(2)}) copy-start(f32[8,4,128]{2,1,0:T(4,128)} %param.22) | copy-start | bytes 49156
  541.4 17.5 %copy-start.3 = (f32[8,256]{1,0:T(8,128)}, f32[8,256]{1,0:T(8,128)S(1)}, u32[]{:S(2)}) copy-start(f32[8,256]{1,0:T(8,128)S(1)} %bitcast_add_fusion) | copy-start | bytes 24580
  562.3 33.6 %all-to-all-start.3 = ((f32[4,256,256]{2,1,0:T(8,128)}), f32[4,256,256]{2,1,0:T(8,128)}, u32[]{:S(2)}, u32[]{:S(2)}) async-start(f32[4,256,256]{2,1,0:T(8,128)} %fusion.37), calls=%async_computation.3 | async-start | bytes 2097152 | tf_op jit(solution)/shard_map/all_to_all | solution.py:62
  566.7 9.5 %copy-start.8 = (f32[8,256]{1,0:T(8,128)S(1)}, f32[8,256]{1,0:T(8,128)}, u32[]{:S(2)}) copy-start(f32[8,256]{1,0:T(8,128)} %param.19) | copy-start | bytes 24580
  566.7 28.3 %copy-start.11 = (f32[1024]{0:T(1024)S(1)}, f32[1024]{0:T(1024)}, u32[]{:S(2)}) copy-start(f32[1024]{0:T(1024)} %param.23) | copy-start | bytes 12292
  576.2 24.4 %copy-start.4 = (f32[8,256]{1,0:T(8,128)}, f32[8,256]{1,0:T(8,128)S(1)}, u32[]{:S(2)}) copy-start(f32[8,256]{1,0:T(8,128)S(1)} %add.75) | copy-start | bytes 24580
Sparse Core Ops, SparseCore 0:
  10.2 48.9 all-gather.27
  62.4 44.4 all-gather.13
  152.7 51.7 all-gather.15
  207.7 44.4 all-gather.17
  297.9 51.9 all-gather.19
  353.2 44.4 all-gather.21
  443.4 51.9 all-gather.23
  498.6 44.5 all-gather.25
where the time goes:
time: 610 us; the launch traced here: 608 us
  waiting for transfers between devices  363 us (60%)
  blocking collectives  125 us (20%)
  matrix products  38.7 us (6%)
  local copies, waits for them, and re-layouts  37.6 us (6%)
  starting transfers between devices  16.1 us (3%)
  between operations  14.5 us (2%)
  other arithmetic  13.4 us (2%)
    all_gather x4, waiting for transfers between devices, shards(): lax.all_gather(cur_cov, 'tile', axis=0, tiled=True)  195 us
    all_gather x4, waiting for transfers between devices, shards(): lax.all_gather(product, 'tile', axis=0, tiled=True)  134 us
    all_to_all x2, blocking collectives, shards(): lax.all_to_all(col_block, 'tile', split_axis=0, concat_axis=1, tiled=True)  56.9 us
    all_gather x4, blocking collectives, shards(): lax.all_gather(cur_mean, 'tile', axis=0, tiled=True)  36 us
    all_to_all x2, waiting for transfers between devices, shards(): lax.all_to_all(col_block, 'tile', split_axis=0, concat_axis=1, tiled=True)  24 us
    all_gather x1, blocking collectives, shards(): lax.all_gather(local_spread, 'tile', axis=1, tiled=True)  18.8 us
    dot_general x4, local copies, waits for them, and re-layouts, shards(): jnp.einsum('pd,rd->pr', lax.all_gather(product, 'tile', axis=0, tiled=Tru...  15.8 us
    all_gather x1, blocking collectives, shards(): lax.all_gather(local_mean, 'tile', axis=1, tiled=True)  13.3 us
  transfers between devices with their start and end apart: 16, of which 12 were waited for; matrix products, arithmetic and copies ran while one was open for 4% of the time, Pallas kernels for 0%

commit v1 on v0

--- a/solution.py
+++ b/solution.py
@@ -1,6 +1,9 @@
+import functools
 import jax
 import jax.numpy as jnp
 from jax import lax
+from jax.experimental import pallas as pl
+from jax.experimental.pallas import tpu as pltpu
 from jax.sharding import PartitionSpec as P
 
 TILE_STATES = 128
@@ -14,7 +17,7 @@
     return lax.ppermute(block, axis, route)
 
 
-def shards(
+def general_shards(
     seg_gain,
     seg_offset,
     seg_noise,
@@ -101,6 +104,432 @@
     return (out_cov[None], out_mean[None], local_mean, local_spread, innovation)
 
 
+BLOCK = 256
+RING = 4
+TAIL = 16
+VMEM = 12 * 1024 * 1024
+ALL_VMEM = 56 * 1024 * 1024
+NT = (((1,), (1,)), ((), ()))
+F32 = jnp.float32
+BF16 = jnp.bfloat16
+
+
+def cols(index):
+    return pl.ds(pl.multiple_of(index * BLOCK, BLOCK), BLOCK)
+
+
+def spot(z, shift):
+    return lax.rem(z + shift, RING)
+
+
+def dot(a, b):
+    return jnp.dot(a, b, preferred_element_type=F32)
+
+
+def dot_nt(a, b):
+    return lax.dot_general(a, b, NT, preferred_element_type=F32)
+
+
+def owns_far(row):
+    return (row == 0) | (row == RING - 1)
+
+
+def lay_out(z, parcels, full, mean):
+    for a in range(RING):
+        at = spot(z, a)
+        row, near, far = cols(at), cols(spot(z, a + 1)), cols(spot(z, a + 2))
+        full[row, row] = parcels[a][:BLOCK, :BLOCK]
+        beside = parcels[a][:BLOCK, BLOCK : 2 * BLOCK]
+        full[row, near] = beside
+        full[near, row] = beside.T
+        mean[:, row] = parcels[a][BLOCK:, :BLOCK]
+
+        @pl.when(owns_far(at))
+        def _(a=a, row=row, far=far):
+            block = parcels[a][:BLOCK, 2 * BLOCK :]
+            full[row, far] = block
+            full[far, row] = block.T
+
+
+def keep_parcels(z, parcels, half, half_mean):
+    for a in range(RING):
+        at = spot(z, a)
+        half_mean[:, cols(at)] = parcels[a][BLOCK:, :BLOCK]
+        half[at, 2 * BLOCK :, :] = parcels[a][:BLOCK, :BLOCK]
+        half[spot(z, a + 1), BLOCK : 2 * BLOCK, :] = parcels[a][:BLOCK, BLOCK : 2 * BLOCK] * 2
+
+        @pl.when(owns_far(at))
+        def _(a=a):
+            half[spot(z, a + 2), :BLOCK, :] = parcels[a][:BLOCK, 2 * BLOCK :] * 2
+
+
+def pack_kernel(where, end_cov, noise, end_mean, offset, parcel, sems):
+    z, seg, group = where[0], where[1], where[2]
+
+    def fetch(source, tail):
+        copies = []
+        for j in range(3):
+            target = parcel.at[pl.ds(0, BLOCK), pl.ds(j * BLOCK, BLOCK)]
+            copies.append(pltpu.make_async_copy(source.at[:, cols(spot(z, j))], target, sems.at[j]))
+        for copy in copies:
+            copy.start()
+        parcel[BLOCK:, :] = jnp.zeros((TAIL, 3 * BLOCK), BF16)
+        parcel[BLOCK:, :BLOCK] = tail.astype(BF16)
+        for copy in copies:
+            copy.wait()
+
+    @pl.when(seg == 1)
+    def _():
+        high = offset[...].astype(BF16).astype(F32)
+        first = lax.broadcasted_iota(jnp.int32, (TAIL, BLOCK), 0) == 0
+        fetch(noise, jnp.where(first, high, offset[...] - high))
+
+    @pl.when(seg != 1)
+    def _():
+        mean = jnp.zeros((1, BLOCK), F32)
+        for g in range(end_mean.shape[0]):
+            mean = jnp.where(group == g, end_mean[g : g + 1, :].astype(F32), mean)
+        fetch(end_cov.at[group], jnp.broadcast_to(mean, (TAIL, BLOCK)))
+
+
+def pairs_kernel(at_seg, where, g0, g1, g2, p0, p1, p2, p3, noise, offset, *refs):
+    if at_seg == GROUP_SEGS - 1:
+        half, half_mean, parcel, mean_row, full, mean = refs
+    else:
+        early, _, _, half, half_mean, parcel, mean_row, full, mean = refs
+    z, seg = where[0], where[1]
+    parcels = (p0, p1, p2, p3)
+
+    @pl.when(seg == at_seg)
+    def _():
+        lay_out(z, parcels, full, mean)
+        product = dot(g0[...], full[...]).astype(BF16)
+        for j, gain in enumerate((g0, g1, g2)):
+            block = dot_nt(product, gain[...]) + noise[:, cols(spot(z, j))].astype(F32)
+            parcel[:BLOCK, j * BLOCK : (j + 1) * BLOCK] = block.astype(BF16)
+        new_mean = (dot_nt(mean[...], g0[...]) + offset[...]).astype(BF16)
+        parcel[BLOCK:, :BLOCK] = new_mean
+        parcel[BLOCK:, BLOCK:] = jnp.zeros((TAIL, 2 * BLOCK), BF16)
+        mean_row[...] = new_mean
+        keep_parcels(z, parcels, half, half_mean)
+
+    if at_seg < GROUP_SEGS - 1:
+
+        @pl.when(seg == GROUP_SEGS - 1)
+        def _():
+            parcel[...] = early[...]
+
+
+def hand_kernel(where, event, gain, out, sem):
+    @pl.when(where[1] < 2)
+    def _():
+        copy = pltpu.make_async_copy(gain, out, sem)
+        copy.start()
+        copy.wait()
+
+
+def stack_kernel(where, event, g0, g1, g2, g3, n0, n1, n2, n3, lift):
+    z, seg = where[0], where[1]
+    states = g0.shape[1]
+
+    @pl.when(seg == 1)
+    def _():
+        for a, gain in enumerate((g0, g1, g2, g3)):
+            lift[cols(spot(z, a)), :] = gain[...]
+        lay_out(z, (n0, n1, n2, n3), lift.at[pl.ds(states, states)], lift.at[pl.ds(2 * states, TAIL)])
+
+
+def turn_kernel(where, event, t0, t1, t2, t3, out):
+    @pl.when(where[1] == 1)
+    def _():
+        for a, parcel in enumerate((t0, t1, t2, t3)):
+            out[a] = parcel[...]
+
+
+def ahead_kernel(where, lift, gain, step_gain, left, base, through, beside):
+    seg = where[1]
+    states = gain.shape[1]
+
+    @pl.when(seg == 0)
+    def _():
+        through[...] = dot(gain[...], lift[:states, :]).astype(BF16)
+        beside[...] = dot(gain[...], lift[states : 2 * states, :])
+
+        def one(k, carry):
+            rows = step_gain[k]
+            left[k] = dot(rows, lift[:states, :]).astype(BF16)
+            value = dot(rows, lift[states : 2 * states, :]) * rows.astype(F32)
+            base[pl.ds(k, 1), :] = row_sums(value)
+            return carry
+
+        lax.fori_loop(0, step_gain.shape[0], one, 0)
+
+
+def row_sums(value):
+    total = value[:, :128]
+    for at in range(128, value.shape[1], 128):
+        total = total + value[:, at : at + 128]
+    return jnp.sum(total.T, axis=0, keepdims=True)
+
+
+def moments_kernel(where, ends_1, ends_0, lift, left, base, gain, offset, var, parcel, kept, kept_mean, half, half_mean, out_mean, out_spread, out, parcel_on):
+    z, seg = where[0], where[1]
+    states = gain.shape[2]
+
+    @pl.when(seg == 1)
+    def _():
+        keep_parcels(z, [ends_1.at[a] for a in range(RING)], half, half_mean)
+
+    @pl.when(seg == 0)
+    def _():
+        keep_parcels(z, [ends_0.at[a] for a in range(RING)], half, half_mean)
+        tail = lift[2 * states :, :].astype(F32)
+        half_mean[...] = (dot_nt(half_mean[...], lift[:states, :]) + tail[0:1] + tail[1:2]).astype(BF16)
+
+    @pl.when(seg > 1)
+    def _():
+        parcel_on[...] = parcel[...]
+
+    def steps(rows_of, more):
+        def one(k, carry):
+            total = jnp.zeros((BLOCK, BLOCK), F32)
+            for b in range(RING):
+                blocks = (b + 2, b + 3, b) if b in (1, 2) else (b + 3, b)
+                parts = [rows_of[k, :, (r % RING) * BLOCK : (r % RING + 1) * BLOCK] for r in blocks]
+                value = dot(jnp.concatenate(parts, axis=1), half[b, (3 - len(blocks)) * BLOCK :, :])
+                total = total + value * parts[-1].astype(F32)
+            spread = row_sums(total) + var[pl.ds(k, 1), :]
+            if more is not None:
+                spread = spread + more[pl.ds(k, 1), :]
+            means = dot_nt(half_mean[...], gain[k])[0:1] + offset[pl.ds(k, 1), :]
+            out[0, pl.ds(k, 1), :] = means
+            out[1, pl.ds(k, 1), :] = spread
+            out_mean[pl.ds(k, 1), :] = means
+            out_spread[pl.ds(k, 1), :] = spread
+            return carry
+
+        lax.fori_loop(0, gain.shape[0], one, 0, unroll=2)
+
+    @pl.when(seg == 0)
+    def _():
+        steps(left, base)
+
+    @pl.when(seg != 0)
+    def _():
+        steps(gain, None)
+
+
+def last_kernel(where, g0, g1, g2, g3, ends_1, ends_0, lift, through, beside, noise, offset, means, rows, mean_row, full, mean):
+    z, seg = where[0], where[1]
+    states = g0.shape[1]
+
+    def finish(product):
+        for a, gain in enumerate((g0, g1, g2, g3)):
+            column = cols(spot(z, a))
+            rows[:, column] = (dot_nt(product, gain[...]) + noise[:, column].astype(F32)).astype(BF16)
+        mean_row[...] = (dot_nt(means[...], g0[...]) + offset[...]).astype(BF16)
+
+    @pl.when(seg == 0)
+    def _():
+        lay_out(z, [ends_0.at[a] for a in range(RING)], full, mean)
+        product = dot(through[...], full[...]).astype(BF16)
+        finish((dot_nt(product, lift[:states, :]) + beside[...]).astype(BF16))
+
+    @pl.when(seg == 1)
+    def _():
+        lay_out(z, [ends_1.at[a] for a in range(RING)], full, mean)
+        finish(dot(g0[...], full[...]).astype(BF16))
+
+
+def innovation_kernel(where, tiles, counts, s0, s1, s2, s3, value, noise, own, far, near, mean_1, mean_2, mean_3, _, out, mean_row, rows_out, full, rows, sem):
+    z, seg = where[0], where[1]
+    copy = pltpu.make_async_copy(rows, rows_out, sem)
+
+    @pl.when(seg > 1)
+    def _():
+        rows[:, cols(z)] = own[:BLOCK, :BLOCK]
+        rows[:, cols(spot(z, 1))] = own[:BLOCK, BLOCK : 2 * BLOCK]
+        rows[:, cols(spot(z, 3))] = near[:BLOCK, BLOCK : 2 * BLOCK].T
+
+        @pl.when(owns_far(z))
+        def _():
+            rows[:, cols(spot(z, 2))] = own[:BLOCK, 2 * BLOCK :]
+
+        @pl.when(jnp.logical_not(owns_far(z)))
+        def _():
+            rows[:, cols(spot(z, 2))] = far[:BLOCK, 2 * BLOCK :].T
+
+        copy.start()
+
+    mean = mean_1[0:1].astype(F32)
+    for at, source in ((2, mean_2), (3, mean_3)):
+        mean = jnp.where(seg == at, source[0:1].astype(F32), mean)
+    mean_row[...] = mean.astype(BF16)
+    for a, part in enumerate((s0, s1, s2, s3)):
+        full[:, :, cols(spot(z, a))] = part[...]
+    full[1] = full[1] + noise[...]
+    for k in range(value.shape[0]):
+        for j in range(SLOTS):
+            at = pl.ds(pl.multiple_of(tiles[j, k] * TILE_STATES, TILE_STATES), TILE_STATES)
+            result = (value[k, j : j + 1, :] - full[0, k : k + 1, at]) / full[1, k : k + 1, at]
+            out[k, j : j + 1, :] = jnp.where(j < counts[k], result, 0.0)
+
+    @pl.when(seg > 1)
+    def _():
+        copy.wait()
+
+
+def smem():
+    return pl.BlockSpec(memory_space=pltpu.SMEM)
+
+
+def vmem():
+    return pl.BlockSpec(memory_space=pltpu.VMEM)
+
+
+def params():
+    return pltpu.CompilerParams(vmem_limit_bytes=VMEM)
+
+
+def cost(flops, moved):
+    return pl.CostEstimate(flops=int(flops), bytes_accessed=int(moved), transcendentals=0)
+
+
+def shape(dims, kind=BF16):
+    return jax.ShapeDtypeStruct(dims, kind)
+
+
+def ring_shards(groups, seg_gain, seg_offset, seg_noise, end_mean, end_cov, step_gain, step_offset, step_var, obs_tiles, obs_count, obs_value, obs_noise):
+    position = lax.axis_index("tm")
+    z = lax.axis_index("tile")
+    where = jnp.stack([z, position % GROUP_SEGS, position // GROUP_SEGS]).astype(jnp.int32)
+    gain, noise = seg_gain[0], seg_noise[0]
+    states = gain.shape[1]
+    steps = step_gain.shape[0]
+    parcel_shape = shape((BLOCK + TAIL, 3 * BLOCK))
+
+    def route(block, moves):
+        table = []
+        for g in range(groups):
+            for (source, start), (target, end) in moves:
+                table.append(((g * GROUP_SEGS + source) * RING + start, (g * GROUP_SEGS + target) * RING + end))
+        return lax.ppermute(block, ("tm", "tile"), table)
+
+    def send(block, pairs, shift):
+        return route(block, [((a, (to + shift) % RING), (b, to)) for a, b in pairs for to in range(RING)])
+
+    def exchange(block, pairs, own=None):
+        others = [send(block, pairs, a) for a in (2, 1, 3)]
+        return [send(block, pairs, 0) if own is None else own, others[1], others[0], others[2]]
+
+    def within(segments, steps):
+        return [((a, start), (a, to)) for a in segments for start, to in steps]
+
+    def call(kernel, name, out_shape, operands, scratch, flops, aliases={}):
+        moved = sum(x.size * x.dtype.itemsize for x in list(operands) + list(out_shape))
+        return pl.pallas_call(
+            kernel,
+            out_shape=out_shape,
+            in_specs=[smem()] + [vmem()] * len(operands),
+            out_specs=(vmem(),) * len(out_shape),
+            scratch_shapes=scratch,
+            input_output_aliases=aliases,
+            compiler_params=params(),
+            cost_estimate=cost(flops, moved),
+            name=name,
+        )(where, *operands)
+
+    def pack(kernel, name, out_shape, far_operands, near_operands, sems, limit):
+        return pl.pallas_call(
+            kernel,
+            out_shape=out_shape,
+            in_specs=[smem()] + [pl.BlockSpec(memory_space=pl.ANY)] * len(far_operands) + [vmem()] * len(near_operands),
+            out_specs=vmem(),
+            scratch_shapes=[sems],
+            compiler_params=pltpu.CompilerParams(vmem_limit_bytes=limit),
+            cost_estimate=cost(0, 1e6),
+            name=name,
+        )(where, *far_operands, *near_operands)
+
+    full_and_mean = [pltpu.VMEM((states, states), BF16), pltpu.VMEM((TAIL, states), BF16)]
+    row_shape, mean_shape = shape((BLOCK, states)), shape((TAIL, BLOCK))
+    half_shapes = (shape((RING, 3 * BLOCK, BLOCK)), shape((TAIL, states)))
+
+    back, on = ((1, 0), (2, 1), (3, 2), (0, 3)), ((0, 1), (1, 2), (2, 3), (3, 0))
+    gain_1 = route(gain, within((3, 2, 1, 0), back))
+    gain_2 = route(gain, within((3, 2), ((2, 0), (1, 3))) + within((1, 0), on))
+    parcel = pack(pack_kernel, "pack", parcel_shape, (end_cov, noise), (end_mean, seg_offset), pltpu.SemaphoreType.DMA((3,)), ALL_VMEM)
+    first = exchange(parcel, ((3, 3), (1, 1)), parcel)
+    held = pack(hand_kernel, "hand", row_shape, (first[2], gain), (), pltpu.SemaphoreType.DMA, VMEM)
+    gains = [gain, gain_1, route(held, within((1, 0), ((0, 2), (1, 3), (2, 0), (3, 1)))), gain_2]
+
+    flops = 4 * BLOCK * states * states
+    *kept, parcel_3, mean_3 = call(
+        functools.partial(pairs_kernel, 3),
+        "pairs_3",
+        (*half_shapes, parcel_shape, mean_shape),
+        (gain, gain_1, gain_2, *first, noise, seg_offset),
+        full_and_mean,
+        flops,
+    )
+    second = exchange(parcel_3, ((3, 2),))
+    *kept, parcel_2, mean_2 = call(
+        functools.partial(pairs_kernel, 2),
+        "pairs_2",
+        (*half_shapes, parcel_shape, mean_shape),
+        (gain, gain_1, gain_2, *second, noise, seg_offset, parcel_3, *kept),
+        full_and_mean,
+        flops,
+        {11: 0, 12: 1},
+    )
+    third = exchange(parcel_2, ((2, 1),))
+    (lift,) = call(stack_kernel, "stack", (shape((2 * states + TAIL, states)),), (parcel_2, *gains, *first), [], 0)
+    lift = send(lift, ((1, 0),), 0)
+    left, base, through, beside = call(
+        ahead_kernel,
+        "ahead",
+        (shape(step_gain.shape), shape((steps, BLOCK), F32), row_shape, shape((BLOCK, states), F32)),
+        (lift, gain, step_gain),
+        [],
+        4 * (steps + 1) * BLOCK * states * states,
+    )
+    (ends_1,) = call(turn_kernel, "turn", (shape((RING, *parcel_shape.shape)),), (base, *third), [], 0)
+    ends_0 = send(ends_1, ((1, 0),), 0)
+    out_steps = shape((steps, BLOCK), F32)
+    _, means, step_mean, step_spread, stats, parcel_on = call(
+        moments_kernel,
+        "moments",
+        (*half_shapes, out_steps, out_steps, shape((2, steps, BLOCK), F32), parcel_shape),
+        (ends_1, ends_0, lift, left, base, step_gain, step_offset, step_var, parcel_2, *kept),
+        [],
+        2 * steps * BLOCK * states * states,
+        {10: 0, 11: 1},
+    )
+    everyone = tuple((s, s) for s in range(GROUP_SEGS))
+    all_stats = [stats] + [send(stats, everyone, a) for a in range(1, RING)]
+    near, far = send(parcel_on, ((3, 3), (2, 2)), 3), route(parcel_on, within((3, 2), ((0, 2), (3, 1))))
+    rows, mean_1 = call(
+        last_kernel,
+        "last",
+        (row_shape, mean_shape),
+        (*gains, ends_1, ends_0, lift, through, beside, noise, seg_offset, means),
+        full_and_mean,
+        flops,
+    )
+    innovation, out_mean, out_cov = pl.pallas_call(
+        innovation_kernel,
+        out_shape=(shape(obs_value.shape, F32), shape((1, BLOCK)), row_shape),
+        in_specs=[smem()] * 3 + [vmem()] * 12 + [pl.BlockSpec(memory_space=pl.ANY)],
+        out_specs=(vmem(), vmem(), pl.BlockSpec(memory_space=pl.ANY)),
+        scratch_shapes=[pltpu.VMEM((2, steps, states), F32), pltpu.VMEM(row_shape.shape, BF16), pltpu.SemaphoreType.DMA],
+        input_output_aliases={15: 2},
+        compiler_params=params(),
+        cost_estimate=cost(0, 2e5),
+        name="innovation",
+    )(where, obs_tiles.T, obs_count, *all_stats, obs_value, obs_noise.reshape(1, states), parcel_2, far, near, mean_1, mean_2, mean_3, rows)
+    return out_cov[None], out_mean, step_mean, step_spread, innovation
+
+
 def solution(mesh):
     in_specs = (
         P("tm", "tile", None),
@@ -123,4 +552,8 @@
         P("tm", "tile"),
         P("tm", None, None),
     )
+    if mesh.shape["tile"] == RING:
+        shards = functools.partial(ring_shards, mesh.shape["tm"] // GROUP_SEGS)
+    else:
+        shards = general_shards
     return jax.shard_map(shards, mesh=mesh, in_specs=in_specs, out_specs=out_specs, check_vma=False)

time: 610 us -> 131 us (0.21)
  waiting for transfers between devices: 363 us -> 69.3 us
  blocking collectives: 125 us -> 0 us
  matrix products: 38.7 us -> 0 us
  local copies, waits for them, and re-layouts: 37.6 us -> 1.06 us
  Pallas kernels: 0 us -> 29.6 us
  between operations: 14.5 us -> 1.02 us
  starting transfers between devices: 16.1 us -> 29.2 us
  other arithmetic: 13.4 us -> 0.59 us
    all_gather x8 -> x0, waiting for transfers between devices: 329 us -> none  [the longest x4 195 us: shards(): lax.all_gather(cur_cov, 'tile', axis=0, tiled=True)]
    all_gather x6 -> x0, blocking collectives: 68.1 us -> none  [the longest x4 36 us: shards(): lax.all_gather(cur_mean, 'tile', axis=0, tiled=True)]
    ppermute x6 -> x21, waiting for transfers between devices: 10.1 us -> 69.3 us  [route(): return lax.ppermute(block, ('tm', 'tile'), table)]
    all_to_all x2 -> x0, blocking collectives: 56.9 us -> none  [shards(): lax.all_to_all(col_block, 'tile', split_axis=0, concat_axis=1, tiled=True)]
    dot_general x16 -> x0, matrix products: 38.7 us -> none  [the longest x4 12.6 us: shards(): jnp.dot(gain_rows, whole_cov, preferred_element_type=jnp.float32)]
    pallas_call x0 -> x10, Pallas kernels: none -> 29.6 us  [the longest x7 25 us: call(): pl.pallas_call(kernel, out_shape=out_shape, in_specs=[smem()] + [vmem()]...]
    all_to_all x2 -> x0, waiting for transfers between devices: 24 us -> none  [shards(): lax.all_to_all(col_block, 'tile', split_axis=0, concat_axis=1, tiled=True)]
    ppermute x6 -> x21, starting transfers between devices: 7.86 us -> 29.2 us  [route(): return lax.ppermute(block, ('tm', 'tile'), table)]
  transfers between devices with their start and end apart: 16 -> 21, of which waited for: 12 -> 5; matrix products, arithmetic and copies ran while one was open for 4% -> 0% of each run, Pallas kernels for 0% -> 16%
where the time goes in v1:
time: 131 us
  waiting for transfers between devices  69.3 us (53%)
  Pallas kernels  29.6 us (23%)
  starting transfers between devices  29.2 us (22%)
    ppermute x21, waiting for transfers between devices, route(): return lax.ppermute(block, ('tm', 'tile'), table)  69.3 us
    ppermute x21, starting transfers between devices, route(): return lax.ppermute(block, ('tm', 'tile'), table)  29.2 us
    pallas_call x7, Pallas kernels, call(): pl.pallas_call(kernel, out_shape=out_shape, in_specs=[smem()] + [vmem()]...  25 us
    pallas_call x2, Pallas kernels, pack(): pl.pallas_call(kernel, out_shape=out_shape, in_specs=[smem()] + [pl.Block...  3.22 us
  transfers between devices with their start and end apart: 21, of which 5 were waited for; matrix products, arithmetic and copies ran while one was open for 0% of the time, Pallas kernels for 16%

profile of v1, /device:TPU:0, one launch (start us, length us, event | category | flops | bytes accessed | tf_op | source)
XLA Modules:
  0.0 130.8 jit_solution(14199518486965487396)
XLA Ops:
  0.6 0.0 copy-start
  0.6 5.1 %collective-permute-start.1 = (bf16[256,1024]{1,0:T(8,128)(2,1)}, bf16[256,1024]{1,0:T(8,128)(2,1)S(1)}, u32[]{:S(2)}, u32[]{:S(2)}) collective-permute-start(bf16[256,1024]{1,0:T(8,128)(2,1)} %bitcast.8), channel_id=1, source_target_pairs={{14,12},{13,15},{10,8},{9,11},{4,5},{5,6},{6,7},{7,4},{0,1},{1,2},... | collective-permute-start | bytes 1572872 | tf_op jit(solution)/shard_map/ppermute | solution.py:416
  5.7 2.1 %collective-permute-start = (bf16[256,1024]{1,0:T(8,128)(2,1)}, bf16[256,1024]{1,0:T(8,128)(2,1)S(1)}, u32[]{:S(2)}, u32[]{:S(2)}) collective-permute-start(bf16[256,1024]{1,0:T(8,128)(2,1)} %bitcast.9), channel_id=1, source_target_pairs={{13,12},{14,13},{15,14},{12,15},{9,8},{10,9},{11,10},{8,11},{5,4},... | collective-permute-start | bytes 1572872 | tf_op jit(solution)/shard_map/ppermute | solution.py:416
  7.8 0.6 pad_add_fusion.where
  8.4 2.6 %pack.1.p0.n0 = bf16[272,768]{1,0:T(8,128)(2,1)} custom-call(s32[3]{0:T(128)} %pad_add_fusion.where, bf16[2,256,1024]{2,1,0:T(8,128)(2,1)} %end_cov.1, bf16[256,1024]{1,0:T(8,128)(2,1)} %bitcast.16, bf16[2,256]{1,0:T(2,128)(2,1)} %end_mean.1, f32[1,256]{1,0:T(1,128)} %offset.9), custom_call_target="tpu_custom_call" | custom-call | bytes 1000000 | tf_op jit(solution)/shard_map/pack/pallas_call | solution.py:443
  11.0 0.7 collective-permute-start.3
  11.7 0.7 collective-permute-start.4
  12.4 0.7 collective-permute-start.2
  13.1 0.0 collective-permute-done.3.p2.event.n2
  13.1 0.6 hand.1
  13.7 2.9 %collective-permute-start.9 = (bf16[256,1024]{1,0:T(8,128)(2,1)S(1)}, bf16[256,1024]{1,0:T(8,128)(2,1)S(1)}, u32[]{:S(2)}, u32[]{:S(2)}) collective-permute-start(bf16[256,1024]{1,0:T(8,128)(2,1)S(1)} %hand.1), channel_id=1, source_target_pairs={{4,6},{5,7},{6,4},{7,5},{0,2},{1,3},{2,0},{3,1},{20,22},{21,23},{2... | collective-permute-start | bytes 1572872 | tf_op jit(solution)/shard_map/ppermute | solution.py:416
  16.7 0.0 collective-permute-done.4.p3.n3
  16.7 0.0 collective-permute-done.2.p1.n1
  16.7 4.0 %collective-permute-done.1.g2.g3 = bf16[256,1024]{1,0:T(8,128)(2,1)S(1)} collective-permute-done((bf16[256,1024]{1,0:T(8,128)(2,1)}, bf16[256,1024]{1,0:T(8,128)(2,1)S(1)}, u32[]{:S(2)}, u32[]{:S(2)}) %collective-permute-start.1) | collective-permute-done | bytes 524320 | tf_op jit(solution)/shard_map/ppermute | solution.py:416
  20.7 10.5 %collective-permute-done.g1 = bf16[256,1024]{1,0:T(8,128)(2,1)S(1)} collective-permute-done((bf16[256,1024]{1,0:T(8,128)(2,1)}, bf16[256,1024]{1,0:T(8,128)(2,1)S(1)}, u32[]{:S(2)}, u32[]{:S(2)}) %collective-permute-start) | collective-permute-done | bytes 524320 | tf_op jit(solution)/shard_map/ppermute | solution.py:416
  31.2 1.0 copy-done.3
  32.3 0.5 pairs_3.1
  32.8 0.7 collective-permute-start.8
  33.5 0.7 collective-permute-start.7
  34.2 0.7 collective-permute-start.6
  34.9 0.7 collective-permute-start.5
  35.6 0.0 collective-permute-done.8.p3
  35.6 0.0 collective-permute-done.7.p2
  35.6 0.0 collective-permute-done.6.p1
  35.6 0.0 collective-permute-done.5.p0
  35.6 0.0 copy-start.4
  35.6 0.6 pairs_2.1
  36.2 20.8 %collective-permute-done.9.g2 = bf16[256,1024]{1,0:T(8,128)(2,1)S(1)} collective-permute-done((bf16[256,1024]{1,0:T(8,128)(2,1)S(1)}, bf16[256,1024]{1,0:T(8,128)(2,1)S(1)}, u32[]{:S(2)}, u32[]{:S(2)}) %collective-permute-start.9) | collective-permute-done | bytes 524320 | tf_op jit(solution)/shard_map/ppermute | solution.py:416
  57.0 0.5 stack.17
  57.6 1.4 %collective-permute-start.10 = (bf16[2064,1024]{1,0:T(8,128)(2,1)S(1)}, bf16[2064,1024]{1,0:T(8,128)(2,1)S(1)}, u32[]{:S(2)}, u32[]{:S(2)}) collective-permute-start(bf16[2064,1024]{1,0:T(8,128)(2,1)S(1)} %stack.17), channel_id=1, source_target_pairs={{4,0},{5,1},{6,2},{7,3},{20,16},{21,17},{22,18},{23,19}} | collective-permute-start | bytes 12681224 | tf_op jit(solution)/shard_map/ppermute | solution.py:416
  59.0 0.7 collective-permute-start.14
  59.7 0.7 collective-permute-start.13
  60.4 0.7 collective-permute-start.12
  61.1 0.7 collective-permute-start.11
  61.8 18.8 %collective-permute-done.10.lift = bf16[2064,1024]{1,0:T(8,128)(2,1)S(1)} collective-permute-done((bf16[2064,1024]{1,0:T(8,128)(2,1)S(1)}, bf16[2064,1024]{1,0:T(8,128)(2,1)S(1)}, u32[]{:S(2)}, u32[]{:S(2)}) %collective-permute-start.10) | collective-permute-done | bytes 4227104 | tf_op jit(solution)/shard_map/ppermute | solution.py:416
  80.6 0.0 copy-done.2
  80.6 12.6 %ahead.1 = (bf16[8,256,1024]{2,1,0:T(8,128)(2,1)S(1)}, f32[8,256]{1,0:T(8,128)S(1)}, bf16[256,1024]{1,0:T(8,128)(2,1)S(1)}, f32[256,1024]{1,0:T(8,128)S(1)}) custom-call(s32[3]{0:T(128)S(1)} %copy-done.5, bf16[2064,1024]{1,0:T(8,128)(2,1)S(1)} %collective-permute-done.10.lift, bf16[256,1024]{1,0:T(8,128)(2,1)S(1)} %bitcast.14, ...), custom_call_target="tpu_custom_call" | custom-call | flops 9663676416 | bytes 14721024 | tf_op jit(solution)/shard_map/ahead/pallas_call | solution.py:430
  93.2 0.0 collective-permute-done.14.t3
  93.2 0.0 collective-permute-done.13.t2
  93.2 0.0 collective-permute-done.12.t1
  93.3 0.0 collective-permute-done.11.t0
  93.3 0.0 copy-start.8
  93.3 0.0 copy-start.9
  93.3 0.6 turn.1.ends_1
  93.8 1.3 collective-permute-start.15
  95.1 15.1 %collective-permute-done.15.ends_0 = bf16[4,272,768]{2,1,0:T(8,128)(2,1)S(1)} collective-permute-done((bf16[4,272,768]{2,1,0:T(8,128)(2,1)S(1)}, bf16[4,272,768]{2,1,0:T(8,128)(2,1)S(1)}, u32[]{:S(2)}, u32[]{:S(2)}) %collective-permute-start.15) | collective-permute-done | bytes 1671200 | tf_op jit(solution)/shard_map/ppermute | solution.py:416
  110.3 0.0 copy-done.9
  110.3 6.3 %moments.1 = (bf16[4,768,256]{2,1,0:T(8,128)(2,1)S(1)}, bf16[16,1024]{1,0:T(8,128)(2,1)S(1)}, f32[8,256]{1,0:T(8,128)}, f32[8,256]{1,0:T(8,128)}, f32[2,8,256]{2...) custom-call(s32[3]{0:T(128)S(1)} %copy-done.5, ...), custom_call_target="tpu_custom_call", output_to_operand_aliasing={{0}: (10, {}), {1}: (11, {})} | custom-call | flops 4294967296 | bytes 20062208 | tf_op jit(solution)/shard_map/moments/pallas_call | solution.py:430
  116.6 0.7 collective-permute-start.20
  117.2 0.7 collective-permute-start.19
  117.9 5.1 %collective-permute-start.18 = (f32[2,8,256]{2,1,0:T(8,128)S(1)}, f32[2,8,256]{2,1,0:T(8,128)S(1)}, u32[]{:S(2)}, u32[]{:S(2)}) collective-permute-start(f32[2,8,256]{2,1,0:T(8,128)S(1)} %get-tuple-element.35.s0), channel_id=1, source_target_pairs={{3,0},{0,1},{1,2},{2,3},{7,4},{4,5},{5,6},{6,7},{11,8},{8,9},{9,10... | collective-permute-start | bytes 49160 | tf_op jit(solution)/shard_map/ppermute | solution.py:416
  123.0 0.3 collective-permute-start.17
  123.3 2.1 %collective-permute-start.16 = (f32[2,8,256]{2,1,0:T(8,128)S(1)}, f32[2,8,256]{2,1,0:T(8,128)S(1)}, u32[]{:S(2)}, u32[]{:S(2)}) collective-permute-start(f32[2,8,256]{2,1,0:T(8,128)S(1)} %get-tuple-element.35.s0), channel_id=1, source_target_pairs={{1,0},{2,1},{3,2},{0,3},{5,4},{6,5},{7,6},{4,7},{9,8},{10,9},{11,1... | collective-permute-start | bytes 49160 | tf_op jit(solution)/shard_map/ppermute | solution.py:416
  125.5 3.9 %last.1 = (bf16[256,1024]{1,0:T(8,128)(2,1)}, bf16[16,256]{1,0:T(8,128)(2,1)S(1)}) custom-call(s32[3]{0:T(128)S(1)} %copy-done.5, bf16[256,1024]{1,0:T(8,128)(2,1)S(1)} %bitcast.15, bf16[256,1024]{1,0:T(8,128)(2,1)S(1)} %collective-permute-done.g1, bf16[256,1024]{1,0:T(8,128)(2,1)S(1)} %collective-permute-done.9.g2, ...), custom_call_target="tpu_custom_call" | custom-call | flops 1073741824 | bytes 12329984 | tf_op jit(solution)/shard_map/last/pallas_call | solution.py:430
  129.4 0.0 collective-permute-done.18.s3
  129.4 0.0 collective-permute-done.17.s2
  129.4 0.0 collective-permute-done.16.s1
  129.4 0.0 collective-permute-done.20.near
  129.4 0.0 collective-permute-done.19.far
  129.4 0.0 copy-done.6
  129.4 0.0 copy-done.10
  129.4 0.0 copy-done.11
  129.4 0.0 copy-done.12
  129.5 1.3 innovation.1
  (15 shorter events, 0.0 us)
Async XLA Ops:
  0.6 12.5 %copy-start = (bf16[1,256,1024]{2,1,0:T(8,128)(2,1)S(1)}, bf16[1,256,1024]{2,1,0:T(8,128)(2,1)}, u32[]{:S(2)}) copy-start(bf16[1,256,1024]{2,1,0:T(8,128)(2,1)} %param.12) | copy-start | bytes 1572868
  0.6 20.1 %collective-permute-start.1 = (bf16[256,1024]{1,0:T(8,128)(2,1)}, bf16[256,1024]{1,0:T(8,128)(2,1)S(1)}, u32[]{:S(2)}, u32[]{:S(2)}) collective-permute-start(bf16[256,1024]{1,0:T(8,128)(2,1)} %bitcast.8), channel_id=1, source_target_pairs={{14,12},{13,15},{10,8},{9,11},{4,5},{5,6},{6,7},{7,4},{0,1},{1,2},... | collective-permute-start | bytes 1572872 | tf_op jit(solution)/shard_map/ppermute | solution.py:416
  5.7 25.5 %collective-permute-start = (bf16[256,1024]{1,0:T(8,128)(2,1)}, bf16[256,1024]{1,0:T(8,128)(2,1)S(1)}, u32[]{:S(2)}, u32[]{:S(2)}) collective-permute-start(bf16[256,1024]{1,0:T(8,128)(2,1)} %bitcast.9), channel_id=1, source_target_pairs={{13,12},{14,13},{15,14},{12,15},{9,8},{10,9},{11,10},{8,11},{5,4},... | collective-permute-start | bytes 1572872 | tf_op jit(solution)/shard_map/ppermute | solution.py:416
  8.4 4.8 %copy-start.5 = (s32[3]{0:T(128)S(1)}, s32[3]{0:T(128)}, u32[]{:S(2)}) copy-start(s32[3]{0:T(128)} %pad_add_fusion.where) | copy-start | bytes 40
  8.4 22.9 %copy-start.1 = (bf16[1,256,1024]{2,1,0:T(8,128)(2,1)S(1)}, bf16[1,256,1024]{2,1,0:T(8,128)(2,1)}, u32[]{:S(2)}) copy-start(bf16[1,256,1024]{2,1,0:T(8,128)(2,1)} %param.14) | copy-start | bytes 1572868
  8.4 22.9 %copy-start.7 = (f32[1,256]{1,0:T(1,128)S(1)}, f32[1,256]{1,0:T(1,128)}, u32[]{:S(2)}) copy-start(f32[1,256]{1,0:T(1,128)} %offset.9) | copy-start | bytes 3076
  11.0 2.1 %collective-permute-start.3 = (bf16[272,768]{1,0:T(8,128)(2,1)}, bf16[272,768]{1,0:T(8,128)(2,1)S(1)}, u32[]{:S(2)}, u32[]{:S(2)}) collective-permute-start(bf16[272,768]{1,0:T(8,128)(2,1)} %pack.1.p0.n0), channel_id=1, source_target_pairs={{14,12},{15,13},{12,14},{13,15},{6,4},{7,5},{4,6},{5,7},{30,28},{3... | collective-permute-start | bytes 1253384 | tf_op jit(solution)/shard_map/ppermute | solution.py:416
  11.7 4.9 %collective-permute-start.4 = (bf16[272,768]{1,0:T(8,128)(2,1)}, bf16[272,768]{1,0:T(8,128)(2,1)S(1)}, u32[]{:S(2)}, u32[]{:S(2)}) collective-permute-start(bf16[272,768]{1,0:T(8,128)(2,1)} %pack.1.p0.n0), channel_id=1, source_target_pairs={{15,12},{12,13},{13,14},{14,15},{7,4},{4,5},{5,6},{6,7},{31,28},{2... | collective-permute-start | bytes 1253384 | tf_op jit(solution)/shard_map/ppermute | solution.py:416
  12.4 4.3 %collective-permute-start.2 = (bf16[272,768]{1,0:T(8,128)(2,1)}, bf16[272,768]{1,0:T(8,128)(2,1)S(1)}, u32[]{:S(2)}, u32[]{:S(2)}) collective-permute-start(bf16[272,768]{1,0:T(8,128)(2,1)} %pack.1.p0.n0), channel_id=1, source_target_pairs={{13,12},{14,13},{15,14},{12,15},{5,4},{6,5},{7,6},{4,7},{29,28},{3... | collective-permute-start | bytes 1253384 | tf_op jit(solution)/shard_map/ppermute | solution.py:416
  13.7 43.2 %collective-permute-start.9 = (bf16[256,1024]{1,0:T(8,128)(2,1)S(1)}, bf16[256,1024]{1,0:T(8,128)(2,1)S(1)}, u32[]{:S(2)}, u32[]{:S(2)}) collective-permute-start(bf16[256,1024]{1,0:T(8,128)(2,1)S(1)} %hand.1), channel_id=1, source_target_pairs={{4,6},{5,7},{6,4},{7,5},{0,2},{1,3},{2,0},{3,1},{20,22},{21,23},{2... | collective-permute-start | bytes 1572872 | tf_op jit(solution)/shard_map/ppermute | solution.py:416
  31.2 1.0 copy-start.3
  32.8 2.8 %collective-permute-start.8 = (bf16[272,768]{1,0:T(8,128)(2,1)S(1)}, bf16[272,768]{1,0:T(8,128)(2,1)S(1)}, u32[]{:S(2)}, u32[]{:S(2)}) collective-permute-start(bf16[272,768]{1,0:T(8,128)(2,1)S(1)} %get-tuple-element.27.refs_0_), channel_id=1, source_target_pairs={{15,8},{12,9},{13,10},{14,11},{31,24},{28,25},{29,26},{30,27}} | collective-permute-start | bytes 1253384 | tf_op jit(solution)/shard_map/ppermute | solution.py:416
  33.5 2.1 %collective-permute-start.7 = (bf16[272,768]{1,0:T(8,128)(2,1)S(1)}, bf16[272,768]{1,0:T(8,128)(2,1)S(1)}, u32[]{:S(2)}, u32[]{:S(2)}) collective-permute-start(bf16[272,768]{1,0:T(8,128)(2,1)S(1)} %get-tuple-element.27.refs_0_), channel_id=1, source_target_pairs={{14,8},{15,9},{12,10},{13,11},{30,24},{31,25},{28,26},{29,27}} | collective-permute-start | bytes 1253384 | tf_op jit(solution)/shard_map/ppermute | solution.py:416
  34.2 1.4 %collective-permute-start.6 = (bf16[272,768]{1,0:T(8,128)(2,1)S(1)}, bf16[272,768]{1,0:T(8,128)(2,1)S(1)}, u32[]{:S(2)}, u32[]{:S(2)}) collective-permute-start(bf16[272,768]{1,0:T(8,128)(2,1)S(1)} %get-tuple-element.27.refs_0_), channel_id=1, source_target_pairs={{13,8},{14,9},{15,10},{12,11},{29,24},{30,25},{31,26},{28,27}} | collective-permute-start | bytes 1253384 | tf_op jit(solution)/shard_map/ppermute | solution.py:416
  34.9 0.7 collective-permute-start.5
  35.6 21.4 %copy-start.4 = (bf16[272,768]{1,0:T(8,128)(2,1)S(1)}, bf16[272,768]{1,0:T(8,128)(2,1)}, u32[]{:S(2)}) copy-start(bf16[272,768]{1,0:T(8,128)(2,1)} %pack.1.p0.n0) | copy-start | bytes 1253380
  57.0 23.6 %copy-start.2 = (bf16[8,256,1024]{2,1,0:T(8,128)(2,1)S(1)}, bf16[8,256,1024]{2,1,0:T(8,128)(2,1)}, u32[]{:S(2)}) copy-start(bf16[8,256,1024]{2,1,0:T(8,128)(2,1)} %gain.1) | copy-start | bytes 12582916
  57.6 23.0 %collective-permute-start.10 = (bf16[2064,1024]{1,0:T(8,128)(2,1)S(1)}, bf16[2064,1024]{1,0:T(8,128)(2,1)S(1)}, u32[]{:S(2)}, u32[]{:S(2)}) collective-permute-start(bf16[2064,1024]{1,0:T(8,128)(2,1)S(1)} %stack.17), channel_id=1, source_target_pairs={{4,0},{5,1},{6,2},{7,3},{20,16},{21,17},{22,18},{23,19}} | collective-permute-start | bytes 12681224 | tf_op jit(solution)/shard_map/ppermute | solution.py:416
  59.0 34.2 %collective-permute-start.14 = (bf16[272,768]{1,0:T(8,128)(2,1)S(1)}, bf16[272,768]{1,0:T(8,128)(2,1)S(1)}, u32[]{:S(2)}, u32[]{:S(2)}) collective-permute-start(bf16[272,768]{1,0:T(8,128)(2,1)S(1)} %get-tuple-element.30.event.parcel.own), channel_id=1, source_target_pairs={{11,4},{8,5},{9,6},{10,7},{27,20},{24,21},{25,22},{26,23}} | collective-permute-start | bytes 1253384 | tf_op jit(solution)/shard_map/ppermute | solution.py:416
  59.7 33.6 %collective-permute-start.13 = (bf16[272,768]{1,0:T(8,128)(2,1)S(1)}, bf16[272,768]{1,0:T(8,128)(2,1)S(1)}, u32[]{:S(2)}, u32[]{:S(2)}) collective-permute-start(bf16[272,768]{1,0:T(8,128)(2,1)S(1)} %get-tuple-element.30.event.parcel.own), channel_id=1, source_target_pairs={{10,4},{11,5},{8,6},{9,7},{26,20},{27,21},{24,22},{25,23}} | collective-permute-start | bytes 1253384 | tf_op jit(solution)/shard_map/ppermute | solution.py:416
  60.4 32.9 %collective-permute-start.12 = (bf16[272,768]{1,0:T(8,128)(2,1)S(1)}, bf16[272,768]{1,0:T(8,128)(2,1)S(1)}, u32[]{:S(2)}, u32[]{:S(2)}) collective-permute-start(bf16[272,768]{1,0:T(8,128)(2,1)S(1)} %get-tuple-element.30.event.parcel.own), channel_id=1, source_target_pairs={{9,4},{10,5},{11,6},{8,7},{25,20},{26,21},{27,22},{24,23}} | collective-permute-start | bytes 1253384 | tf_op jit(solution)/shard_map/ppermute | solution.py:416
  61.1 32.2 %collective-permute-start.11 = (bf16[272,768]{1,0:T(8,128)(2,1)S(1)}, bf16[272,768]{1,0:T(8,128)(2,1)S(1)}, u32[]{:S(2)}, u32[]{:S(2)}) collective-permute-start(bf16[272,768]{1,0:T(8,128)(2,1)S(1)} %get-tuple-element.30.event.parcel.own), channel_id=1, source_target_pairs={{8,4},{9,5},{10,6},{11,7},{24,20},{25,21},{26,22},{27,23}} | collective-permute-start | bytes 1253384 | tf_op jit(solution)/shard_map/ppermute | solution.py:416
  93.3 17.0 %copy-start.8 = (f32[8,256]{1,0:T(8,128)S(1)}, f32[8,256]{1,0:T(8,128)}, u32[]{:S(2)}) copy-start(f32[8,256]{1,0:T(8,128)} %offset.8) | copy-start | bytes 24580
  93.3 17.0 %copy-start.9 = (f32[8,256]{1,0:T(8,128)S(1)}, f32[8,256]{1,0:T(8,128)}, u32[]{:S(2)}) copy-start(f32[8,256]{1,0:T(8,128)} %var.1) | copy-start | bytes 24580
  93.8 16.4 %collective-permute-start.15 = (bf16[4,272,768]{2,1,0:T(8,128)(2,1)S(1)}, bf16[4,272,768]{2,1,0:T(8,128)(2,1)S(1)}, u32[]{:S(2)}, u32[]{:S(2)}) collective-permute-start(bf16[4,272,768]{2,1,0:T(8,128)(2,1)S(1)} %turn.1.ends_1), channel_id=1, source_target_pairs={{4,0},{5,1},{6,2},{7,3},{20,16},{21,17},{22,18},{23,19}} | collective-permute-start | bytes 5013512 | tf_op jit(solution)/shard_map/ppermute | solution.py:416
  116.6 12.8 %collective-permute-start.20 = (bf16[272,768]{1,0:T(8,128)(2,1)S(1)}, bf16[272,768]{1,0:T(8,128)(2,1)S(1)}, u32[]{:S(2)}, u32[]{:S(2)}) collective-permute-start(bf16[272,768]{1,0:T(8,128)(2,1)S(1)} %get-tuple-element.36), channel_id=1, source_target_pairs={{15,12},{12,13},{13,14},{14,15},{11,8},{8,9},{9,10},{10,11},{31,28... | collective-permute-start | bytes 1253384 | tf_op jit(solution)/shard_map/ppermute | solution.py:416
  117.2 12.2 %collective-permute-start.19 = (bf16[272,768]{1,0:T(8,128)(2,1)S(1)}, bf16[272,768]{1,0:T(8,128)(2,1)S(1)}, u32[]{:S(2)}, u32[]{:S(2)}) collective-permute-start(bf16[272,768]{1,0:T(8,128)(2,1)S(1)} %get-tuple-element.36), channel_id=1, source_target_pairs={{12,14},{15,13},{8,10},{11,9},{28,30},{31,29},{24,26},{27,25}} | collective-permute-start | bytes 1253384 | tf_op jit(solution)/shard_map/ppermute | solution.py:416
  117.9 11.4 %collective-permute-start.18 = (f32[2,8,256]{2,1,0:T(8,128)S(1)}, f32[2,8,256]{2,1,0:T(8,128)S(1)}, u32[]{:S(2)}, u32[]{:S(2)}) collective-permute-start(f32[2,8,256]{2,1,0:T(8,128)S(1)} %get-tuple-element.35.s0), channel_id=1, source_target_pairs={{3,0},{0,1},{1,2},{2,3},{7,4},{4,5},{5,6},{6,7},{11,8},{8,9},{9,10... | collective-permute-start | bytes 49160 | tf_op jit(solution)/shard_map/ppermute | solution.py:416
  123.0 6.4 %collective-permute-start.17 = (f32[2,8,256]{2,1,0:T(8,128)S(1)}, f32[2,8,256]{2,1,0:T(8,128)S(1)}, u32[]{:S(2)}, u32[]{:S(2)}) collective-permute-start(f32[2,8,256]{2,1,0:T(8,128)S(1)} %get-tuple-element.35.s0), channel_id=1, source_target_pairs={{2,0},{3,1},{0,2},{1,3},{6,4},{7,5},{4,6},{5,7},{10,8},{11,9},{8,1... | collective-permute-start | bytes 49160 | tf_op jit(solution)/shard_map/ppermute | solution.py:416
  123.3 6.0 %collective-permute-start.16 = (f32[2,8,256]{2,1,0:T(8,128)S(1)}, f32[2,8,256]{2,1,0:T(8,128)S(1)}, u32[]{:S(2)}, u32[]{:S(2)}) collective-permute-start(f32[2,8,256]{2,1,0:T(8,128)S(1)} %get-tuple-element.35.s0), channel_id=1, source_target_pairs={{1,0},{2,1},{3,2},{0,3},{5,4},{6,5},{7,6},{4,7},{9,8},{10,9},{11,1... | collective-permute-start | bytes 49160 | tf_op jit(solution)/shard_map/ppermute | solution.py:416
  125.5 4.0 %copy-start.6 = (f32[8,4,128]{2,1,0:T(4,128)S(1)}, f32[8,4,128]{2,1,0:T(4,128)}, u32[]{:S(2)}) copy-start(f32[8,4,128]{2,1,0:T(4,128)} %value.1) | copy-start | bytes 49156
  125.5 4.0 %copy-start.10 = (f32[1024]{0:T(1024)S(1)}, f32[1024]{0:T(1024)}, u32[]{:S(2)}) copy-start(f32[1024]{0:T(1024)} %param.23) | copy-start | bytes 12292
  125.5 4.0 %copy-start.11 = (s32[8,4]{0,1:T(4,128)S(1)}, s32[8,4]{0,1:T(4,128)}, u32[]{:S(2)}) copy-start(s32[8,4]{0,1:T(4,128)} %param.20) | copy-start | bytes 388
  125.5 4.0 %copy-start.12 = (s32[8]{0:T(128)S(1)}, s32[8]{0:T(128)}, u32[]{:S(2)}) copy-start(s32[8]{0:T(128)} %counts.1) | copy-start | bytes 100

commit v2 on v1

--- a/solution.py
+++ b/solution.py
@@ -134,74 +134,112 @@
     return (row == 0) | (row == RING - 1)
 
 
+def each_parcel(parcels, body):
+    for a, entry in enumerate(parcels):
+        if isinstance(entry, tuple):
+            condition, one, other = entry
+            pl.when(condition)(functools.partial(body, a, one))
+            pl.when(jnp.logical_not(condition))(functools.partial(body, a, other))
+        else:
+            body(a, entry)
+
+
+def by_relay(z, own, after, across, before, handed):
+    return own, (z < RING - 1, after, handed), across, (z > 0, before, handed)
+
+
 def lay_out(z, parcels, full, mean):
-    for a in range(RING):
+    def body(a, parcel):
         at = spot(z, a)
         row, near, far = cols(at), cols(spot(z, a + 1)), cols(spot(z, a + 2))
-        full[row, row] = parcels[a][:BLOCK, :BLOCK]
-        beside = parcels[a][:BLOCK, BLOCK : 2 * BLOCK]
+        full[row, row] = parcel[:BLOCK, :BLOCK]
+        beside = parcel[:BLOCK, BLOCK : 2 * BLOCK]
         full[row, near] = beside
         full[near, row] = beside.T
-        mean[:, row] = parcels[a][BLOCK:, :BLOCK]
+        mean[:, row] = parcel[BLOCK:, :BLOCK]
 
         @pl.when(owns_far(at))
-        def _(a=a, row=row, far=far):
-            block = parcels[a][:BLOCK, 2 * BLOCK :]
+        def _():
+            block = parcel[:BLOCK, 2 * BLOCK :]
             full[row, far] = block
             full[far, row] = block.T
 
+    each_parcel(parcels, body)
+
 
 def keep_parcels(z, parcels, half, half_mean):
-    for a in range(RING):
+    def body(a, parcel):
         at = spot(z, a)
-        half_mean[:, cols(at)] = parcels[a][BLOCK:, :BLOCK]
-        half[at, 2 * BLOCK :, :] = parcels[a][:BLOCK, :BLOCK]
-        half[spot(z, a + 1), BLOCK : 2 * BLOCK, :] = parcels[a][:BLOCK, BLOCK : 2 * BLOCK] * 2
+        half_mean[:, cols(at)] = parcel[BLOCK:, :BLOCK]
+        half[at, 2 * BLOCK :, :] = parcel[:BLOCK, :BLOCK]
+        half[spot(z, a + 1), BLOCK : 2 * BLOCK, :] = parcel[:BLOCK, BLOCK : 2 * BLOCK] * 2
 
         @pl.when(owns_far(at))
-        def _(a=a):
-            half[spot(z, a + 2), :BLOCK, :] = parcels[a][:BLOCK, 2 * BLOCK :] * 2
+        def _():
+            half[spot(z, a + 2), :BLOCK, :] = parcel[:BLOCK, 2 * BLOCK :] * 2
+
+    each_parcel(parcels, body)
+
+
+def keep_whole(full, mean, half, half_mean):
+    half_mean[...] = mean[...]
+    for b in range(RING):
+        column = slice(b * BLOCK, (b + 1) * BLOCK)
+        for j in range(3):
+            if j < 2 or b in (1, 2):
+                row = (b - j) % RING * BLOCK
+                block = full[row : row + BLOCK, column]
+                half[b, (2 - j) * BLOCK : (3 - j) * BLOCK, :] = block * 2 if j else block
+
+
+def fetch(source, z, tail, parcel, sems):
+    copies = []
+    for j in range(3):
+        target = parcel.at[pl.ds(0, BLOCK), pl.ds(j * BLOCK, BLOCK)]
+        copies.append(pltpu.make_async_copy(source.at[:, cols(spot(z, j))], target, sems.at[j]))
+    for copy in copies:
+        copy.start()
+    parcel[BLOCK:, :] = jnp.zeros((TAIL, 3 * BLOCK), BF16)
+    parcel[BLOCK:, :BLOCK] = tail.astype(BF16)
+    for copy in copies:
+        copy.wait()
+
+
+def group_mean(group, end_mean):
+    mean = jnp.zeros((1, BLOCK), F32)
+    for g in range(end_mean.shape[0]):
+        mean = jnp.where(group == g, end_mean[g : g + 1, :].astype(F32), mean)
+    return jnp.broadcast_to(mean, (TAIL, BLOCK))
 
 
 def pack_kernel(where, end_cov, noise, end_mean, offset, parcel, sems):
     z, seg, group = where[0], where[1], where[2]
 
-    def fetch(source, tail):
-        copies = []
-        for j in range(3):
-            target = parcel.at[pl.ds(0, BLOCK), pl.ds(j * BLOCK, BLOCK)]
-            copies.append(pltpu.make_async_copy(source.at[:, cols(spot(z, j))], target, sems.at[j]))
-        for copy in copies:
-            copy.start()
-        parcel[BLOCK:, :] = jnp.zeros((TAIL, 3 * BLOCK), BF16)
-        parcel[BLOCK:, :BLOCK] = tail.astype(BF16)
-        for copy in copies:
-            copy.wait()
-
     @pl.when(seg == 1)
     def _():
         high = offset[...].astype(BF16).astype(F32)
         first = lax.broadcasted_iota(jnp.int32, (TAIL, BLOCK), 0) == 0
-        fetch(noise, jnp.where(first, high, offset[...] - high))
+        fetch(noise, z, jnp.where(first, high, offset[...] - high), parcel, sems)
 
     @pl.when(seg != 1)
     def _():
-        mean = jnp.zeros((1, BLOCK), F32)
-        for g in range(end_mean.shape[0]):
-            mean = jnp.where(group == g, end_mean[g : g + 1, :].astype(F32), mean)
-        fetch(end_cov.at[group], jnp.broadcast_to(mean, (TAIL, BLOCK)))
-
-
-def pairs_kernel(at_seg, where, g0, g1, g2, p0, p1, p2, p3, noise, offset, *refs):
+        fetch(end_cov.at[group], z, group_mean(group, end_mean), parcel, sems)
+
+
+def pairs_kernel(at_seg, where, g0, g1, g2, noise, offset, *refs):
+    z, seg, group = where[0], where[1], where[2]
     if at_seg == GROUP_SEGS - 1:
-        half, half_mean, parcel, mean_row, full, mean = refs
+        end_cov, end_mean, *others, half, half_mean, parcel, mean_row, full, mean, own = refs
+        parcels = (own, *others)
     else:
-        early, _, _, half, half_mean, parcel, mean_row, full, mean = refs
-    z, seg = where[0], where[1]
-    parcels = (p0, p1, p2, p3)
+        *parcels, early, _, _, half, half_mean, parcel, mean_row, beside, far, full, mean = refs
 
     @pl.when(seg == at_seg)
     def _():
+        if at_seg == GROUP_SEGS - 1:
+            for j in range(3):
+                own[:BLOCK, j * BLOCK : (j + 1) * BLOCK] = end_cov[group, :, cols(spot(z, j))]
+            own[BLOCK:, :BLOCK] = group_mean(group, end_mean).astype(BF16)
         lay_out(z, parcels, full, mean)
         product = dot(g0[...], full[...]).astype(BF16)
         for j, gain in enumerate((g0, g1, g2)):
@@ -211,17 +249,19 @@
         parcel[BLOCK:, :BLOCK] = new_mean
         parcel[BLOCK:, BLOCK:] = jnp.zeros((TAIL, 2 * BLOCK), BF16)
         mean_row[...] = new_mean
-        keep_parcels(z, parcels, half, half_mean)
+        keep_whole(full, mean, half, half_mean)
 
     if at_seg < GROUP_SEGS - 1:
-
         @pl.when(seg == GROUP_SEGS - 1)
         def _():
             parcel[...] = early[...]
 
-
-def hand_kernel(where, event, gain, out, sem):
-    @pl.when(where[1] < 2)
+        beside[...] = parcel[:BLOCK, BLOCK : 2 * BLOCK]
+        far[...] = parcel[:BLOCK, 2 * BLOCK :]
+
+
+def hand_kernel(at_seg, where, event, gain, out, sem):
+    @pl.when(where[1] == at_seg)
     def _():
         copy = pltpu.make_async_copy(gain, out, sem)
         copy.start()
@@ -239,16 +279,23 @@
         lay_out(z, (n0, n1, n2, n3), lift.at[pl.ds(states, states)], lift.at[pl.ds(2 * states, TAIL)])
 
 
-def turn_kernel(where, event, t0, t1, t2, t3, out):
+def turn_kernel(where, near, far, t0, t1, t2, t3, t4, out):
+    def body(a, parcel):
+        out[a] = parcel[...]
+
     @pl.when(where[1] == 1)
     def _():
-        for a, parcel in enumerate((t0, t1, t2, t3)):
-            out[a] = parcel[...]
-
-
-def ahead_kernel(where, lift, gain, step_gain, left, base, through, beside):
+        each_parcel(by_relay(where[0], t0, t1, t2, t3, t4), body)
+
+
+def ahead_kernel(where, event, lift, gain, step_gain, block_1, block_2, left, base, through, beside, block_1_on, block_2_on):
     seg = where[1]
     states = gain.shape[1]
+
+    @pl.when(seg > 1)
+    def _():
+        block_1_on[...] = block_1[...]
+        block_2_on[...] = block_2[...]
 
     @pl.when(seg == 0)
     def _():
@@ -272,7 +319,7 @@
     return jnp.sum(total.T, axis=0, keepdims=True)
 
 
-def moments_kernel(where, ends_1, ends_0, lift, left, base, gain, offset, var, parcel, kept, kept_mean, half, half_mean, out_mean, out_spread, out, parcel_on):
+def moments_kernel(where, ends_1, ends_0, lift, left, base, gain, offset, var, kept, kept_mean, half, half_mean, out_mean, out_spread, out):
     z, seg = where[0], where[1]
     states = gain.shape[2]
 
@@ -285,10 +332,6 @@
         keep_parcels(z, [ends_0.at[a] for a in range(RING)], half, half_mean)
         tail = lift[2 * states :, :].astype(F32)
         half_mean[...] = (dot_nt(half_mean[...], lift[:states, :]) + tail[0:1] + tail[1:2]).astype(BF16)
-
-    @pl.when(seg > 1)
-    def _():
-        parcel_on[...] = parcel[...]
 
     def steps(rows_of, more):
         def one(k, carry):
@@ -319,12 +362,12 @@
         steps(gain, None)
 
 
-def last_kernel(where, g0, g1, g2, g3, ends_1, ends_0, lift, through, beside, noise, offset, means, rows, mean_row, full, mean):
+def last_kernel(where, g0, a1, a2, a3, b1, b2, b3, ends_1, ends_0, lift, through, beside, noise, offset, means, rows, mean_row, full, mean):
     z, seg = where[0], where[1]
     states = g0.shape[1]
 
-    def finish(product):
-        for a, gain in enumerate((g0, g1, g2, g3)):
+    def finish(product, gains):
+        for a, gain in enumerate(gains):
             column = cols(spot(z, a))
             rows[:, column] = (dot_nt(product, gain[...]) + noise[:, column].astype(F32)).astype(BF16)
         mean_row[...] = (dot_nt(means[...], g0[...]) + offset[...]).astype(BF16)
@@ -333,12 +376,12 @@
     def _():
         lay_out(z, [ends_0.at[a] for a in range(RING)], full, mean)
         product = dot(through[...], full[...]).astype(BF16)
-        finish((dot_nt(product, lift[:states, :]) + beside[...]).astype(BF16))
+        finish((dot_nt(product, lift[:states, :]) + beside[...]).astype(BF16), (g0, b1, b2, b3))
 
     @pl.when(seg == 1)
     def _():
         lay_out(z, [ends_1.at[a] for a in range(RING)], full, mean)
-        finish(dot(g0[...], full[...]).astype(BF16))
+        finish(dot(g0[...], full[...]).astype(BF16), (g0, a1, a2, a3))
 
 
 def innovation_kernel(where, tiles, counts, s0, s1, s2, s3, value, noise, own, far, near, mean_1, mean_2, mean_3, _, out, mean_row, rows_out, full, rows, sem):
@@ -349,7 +392,7 @@
     def _():
         rows[:, cols(z)] = own[:BLOCK, :BLOCK]
         rows[:, cols(spot(z, 1))] = own[:BLOCK, BLOCK : 2 * BLOCK]
-        rows[:, cols(spot(z, 3))] = near[:BLOCK, BLOCK : 2 * BLOCK].T
+        rows[:, cols(spot(z, 3))] = near[...].T
 
         @pl.when(owns_far(z))
         def _():
@@ -357,7 +400,7 @@
 
         @pl.when(jnp.logical_not(owns_far(z)))
         def _():
-            rows[:, cols(spot(z, 2))] = far[:BLOCK, 2 * BLOCK :].T
+            rows[:, cols(spot(z, 2))] = far[...].T
 
         copy.start()
 
@@ -444,7 +487,7 @@
             kernel,
             out_shape=out_shape,
             in_specs=[smem()] + [pl.BlockSpec(memory_space=pl.ANY)] * len(far_operands) + [vmem()] * len(near_operands),
-            out_specs=vmem(),
+            out_specs=jax.tree.map(lambda _: vmem(), out_shape),
             scratch_shapes=[sems],
             compiler_params=pltpu.CompilerParams(vmem_limit_bytes=limit),
             cost_estimate=cost(0, 1e6),
@@ -452,67 +495,79 @@
         )(where, *far_operands, *near_operands)
 
     full_and_mean = [pltpu.VMEM((states, states), BF16), pltpu.VMEM((TAIL, states), BF16)]
-    row_shape, mean_shape = shape((BLOCK, states)), shape((TAIL, BLOCK))
+    row_shape, mean_shape, block_shape = shape((BLOCK, states)), shape((TAIL, BLOCK)), shape((BLOCK, BLOCK))
     half_shapes = (shape((RING, 3 * BLOCK, BLOCK)), shape((TAIL, states)))
 
-    back, on = ((1, 0), (2, 1), (3, 2), (0, 3)), ((0, 1), (1, 2), (2, 3), (3, 0))
-    gain_1 = route(gain, within((3, 2, 1, 0), back))
-    gain_2 = route(gain, within((3, 2), ((2, 0), (1, 3))) + within((1, 0), on))
+    back, two_on, on = ((1, 0), (2, 1), (3, 2), (0, 3)), ((0, 2), (1, 3), (2, 0), (3, 1)), ((0, 1), (1, 2), (2, 3), (3, 0))
+    pair_gains = [route(gain, within((3, 2, 1), back)), route(gain, within((3, 2), ((2, 0), (1, 3))) + within((1,), on))]
     parcel = pack(pack_kernel, "pack", parcel_shape, (end_cov, noise), (end_mean, seg_offset), pltpu.SemaphoreType.DMA((3,)), ALL_VMEM)
-    first = exchange(parcel, ((3, 3), (1, 1)), parcel)
-    held = pack(hand_kernel, "hand", row_shape, (first[2], gain), (), pltpu.SemaphoreType.DMA, VMEM)
-    gains = [gain, gain_1, route(held, within((1, 0), ((0, 2), (1, 3), (2, 0), (3, 1)))), gain_2]
+    first = [send(parcel, ((0 if a == 2 else 3, 3), (1, 1)), a) for a in range(1, RING)]
+
+    def hand(segment, event):
+        kernel = functools.partial(hand_kernel, segment)
+        return pack(kernel, f"hand_{segment}", row_shape, (event, gain), (), pltpu.SemaphoreType.DMA, VMEM)
+
+    gains_1 = [pair_gains[0], route(hand(1, first[1]), within((1,), two_on)), pair_gains[1]]
 
     flops = 4 * BLOCK * states * states
     *kept, parcel_3, mean_3 = call(
         functools.partial(pairs_kernel, 3),
         "pairs_3",
         (*half_shapes, parcel_shape, mean_shape),
-        (gain, gain_1, gain_2, *first, noise, seg_offset),
-        full_and_mean,
+        (gain, *pair_gains, noise, seg_offset, end_cov, end_mean, *first),
+        full_and_mean + [pltpu.VMEM(parcel_shape.shape, BF16)],
         flops,
     )
     second = exchange(parcel_3, ((3, 2),))
-    *kept, parcel_2, mean_2 = call(
+
+    *kept, parcel_2, mean_2, beside_block, far_block = call(
         functools.partial(pairs_kernel, 2),
         "pairs_2",
-        (*half_shapes, parcel_shape, mean_shape),
-        (gain, gain_1, gain_2, *second, noise, seg_offset, parcel_3, *kept),
+        (*half_shapes, parcel_shape, mean_shape, block_shape, block_shape),
+        (gain, *pair_gains, noise, seg_offset, *second, parcel_3, *kept),
         full_and_mean,
         flops,
         {11: 0, 12: 1},
     )
-    third = exchange(parcel_2, ((2, 1),))
-    (lift,) = call(stack_kernel, "stack", (shape((2 * states + TAIL, states)),), (parcel_2, *gains, *first), [], 0)
+    own = send(parcel_2, ((2, 1),), 0)
+    across = send(parcel_2, ((2, 1),), 2)
+    sides = [
+        route(parcel_2, [((2, start), (1, to)) for start, to in moves])
+        for moves in (((1, 0), (2, 1), (3, 2)), ((0, 1), (1, 2), (2, 3)))
+    ]
+    third = [own, sides[0], across, sides[1], route(across, within((1,), ((2, 3), (1, 0))))]
+    (lift,) = call(stack_kernel, "stack", (shape((2 * states + TAIL, states)),), (parcel_2, gain, *gains_1, parcel, *first), [], 0)
     lift = send(lift, ((1, 0),), 0)
-    left, base, through, beside = call(
+    gain_0 = hand(0, lift)
+    left, base, through, beside, beside_block, far_block = call(
         ahead_kernel,
         "ahead",
-        (shape(step_gain.shape), shape((steps, BLOCK), F32), row_shape, shape((BLOCK, states), F32)),
-        (lift, gain, step_gain),
+        (shape(step_gain.shape), shape((steps, BLOCK), F32), row_shape, shape((BLOCK, states), F32), block_shape, block_shape),
+        (gain_0, lift, gain, step_gain, beside_block, far_block),
         [],
         4 * (steps + 1) * BLOCK * states * states,
     )
-    (ends_1,) = call(turn_kernel, "turn", (shape((RING, *parcel_shape.shape)),), (base, *third), [], 0)
+    gains_0 = [route(gain_0, within((0,), moves)) for moves in (back, two_on, on)]
+    near, far = route(beside_block, within((3, 2), on)), route(far_block, within((3, 2), ((0, 2), (3, 1))))
+    (ends_1,) = call(turn_kernel, "turn", (shape((RING, *parcel_shape.shape)),), (near, far, *third), [], 0)
     ends_0 = send(ends_1, ((1, 0),), 0)
     out_steps = shape((steps, BLOCK), F32)
-    _, means, step_mean, step_spread, stats, parcel_on = call(
+    _, means, step_mean, step_spread, stats = call(
         moments_kernel,
         "moments",
-        (*half_shapes, out_steps, out_steps, shape((2, steps, BLOCK), F32), parcel_shape),
-        (ends_1, ends_0, lift, left, base, step_gain, step_offset, step_var, parcel_2, *kept),
+        (*half_shapes, out_steps, out_steps, shape((2, steps, BLOCK), F32)),
+        (ends_1, ends_0, lift, left, base, step_gain, step_offset, step_var, *kept),
         [],
         2 * steps * BLOCK * states * states,
-        {10: 0, 11: 1},
+        {9: 0, 10: 1},
     )
     everyone = tuple((s, s) for s in range(GROUP_SEGS))
     all_stats = [stats] + [send(stats, everyone, a) for a in range(1, RING)]
-    near, far = send(parcel_on, ((3, 3), (2, 2)), 3), route(parcel_on, within((3, 2), ((0, 2), (3, 1))))
     rows, mean_1 = call(
         last_kernel,
         "last",
         (row_shape, mean_shape),
-        (*gains, ends_1, ends_0, lift, through, beside, noise, seg_offset, means),
+        (gain, *gains_1, *gains_0, ends_1, ends_0, lift, through, beside, noise, seg_offset, means),
         full_and_mean,
         flops,
     )

time: 131 us -> 121 us (0.924)
  waiting for transfers between devices: 69.3 us -> 44.4 us
  starting transfers between devices: 29.2 us -> 44.2 us
    ppermute x21 -> x25, waiting for transfers between devices: 69.3 us -> 44.4 us  [route(): return lax.ppermute(block, ('tm', 'tile'), table)]
    ppermute x21 -> x25, starting transfers between devices: 29.2 us -> 44.2 us  [route(): return lax.ppermute(block, ('tm', 'tile'), table)]
    pallas_call x2 -> x3, Pallas kernels: 3.22 us -> 3.8 us  [pack(): pl.pallas_call(kernel, out_shape=out_shape, in_specs=[smem()] + [pl.Block...]
  transfers between devices with their start and end apart: 21 -> 25, of which waited for: 5 -> 5; matrix products, arithmetic and copies ran while one was open for 0% -> 0% of each run, Pallas kernels for 16% -> 23%
where the time goes in v2:
time: 121 us
  waiting for transfers between devices  44.4 us (37%)
  starting transfers between devices  44.2 us (37%)
  Pallas kernels  30.2 us (25%)
    ppermute x25, waiting for transfers between devices, route(): return lax.ppermute(block, ('tm', 'tile'), table)  44.4 us
    ppermute x25, starting transfers between devices, route(): return lax.ppermute(block, ('tm', 'tile'), table)  44.2 us
    pallas_call x7, Pallas kernels, call(): pl.pallas_call(kernel, out_shape=out_shape, in_specs=[smem()] + [vmem()]...  25.1 us
    pallas_call x3, Pallas kernels, pack(): pl.pallas_call(kernel, out_shape=out_shape, in_specs=[smem()] + [pl.Block...  3.8 us
  transfers between devices with their start and end apart: 25, of which 5 were waited for; matrix products, arithmetic and copies ran while one was open for 0% of the time, Pallas kernels for 23%

profile of v2, /device:TPU:0, one launch (start us, length us, event | category | flops | bytes accessed | tf_op | source)
XLA Modules:
  0.0 120.9 jit_solution(418687092449507239)
XLA Ops:
  0.6 0.8 collective-permute-start
  1.5 0.7 collective-permute-start.1
  2.2 0.6 pad_add_fusion.where
  2.8 0.0 copy-start.11
  2.8 2.7 %pack.1.n0 = bf16[272,768]{1,0:T(8,128)(2,1)} custom-call(s32[3]{0:T(128)} %pad_add_fusion.where, bf16[2,256,1024]{2,1,0:T(8,128)(2,1)} %refs_0_.1, bf16[256,1024]{1,0:T(8,128)(2,1)} %bitcast.17, bf16[2,256]{1,0:T(2,128)(2,1)} %refs_1_.1, f32[1,256]{1,0:T(1,128)} %offset.9), custom_call_target="tpu_custom_call" | custom-call | bytes 1000000 | tf_op jit(solution)/shard_map/pack/pallas_call | solution.py:486
  5.5 12.2 %collective-permute-start.3 = (bf16[272,768]{1,0:T(8,128)(2,1)}, bf16[272,768]{1,0:T(8,128)(2,1)S(1)}, u32[]{:S(2)}, u32[]{:S(2)}) collective-permute-start(bf16[272,768]{1,0:T(8,128)(2,1)} %pack.1.n0), channel_id=1, source_target_pairs={{2,12},{3,13},{0,14},{1,15},{6,4},{7,5},{4,6},{5,7},{18,28},{19,29... | collective-permute-start | bytes 1253384 | tf_op jit(solution)/shard_map/ppermute | solution.py:459
  17.6 0.7 collective-permute-start.2
  18.3 0.7 collective-permute-start.4
  19.0 9.0 %collective-permute-done.3.refs_3_.event.n2 = bf16[272,768]{1,0:T(8,128)(2,1)S(1)} collective-permute-done((bf16[272,768]{1,0:T(8,128)(2,1)}, bf16[272,768]{1,0:T(8,128)(2,1)S(1)}, u32[]{:S(2)}, u32[]{:S(2)}) %collective-permute-start.3) | collective-permute-done | bytes 417824 | tf_op jit(solution)/shard_map/ppermute | solution.py:459
  28.1 0.6 hand_1.1
  28.6 0.7 collective-permute-start.9
  29.3 0.0 collective-permute-done.2.refs_2_.n1
  29.3 0.0 collective-permute-done.4.refs_4_.n3
  29.3 0.0 collective-permute-done.g1.a1
  29.4 0.0 collective-permute-done.1.g2.g3.a3
  29.4 0.6 pairs_3.1
  30.0 0.7 collective-permute-start.5
  30.7 0.7 collective-permute-start.6
  31.4 0.7 collective-permute-start.7
  32.1 0.7 collective-permute-start.8
  32.8 0.0 collective-permute-done.5.refs_0_
  32.8 0.0 collective-permute-done.6.refs_1_
  32.8 0.0 copy-start.4
  32.8 0.6 pairs_2.1
  33.4 0.0 collective-permute-done.9.g2.a2
  33.4 0.4 copy-done.4
  33.8 0.5 stack.17
  34.4 0.0 copy-start.3
  34.4 1.6 %collective-permute-start.10 = (bf16[2064,1024]{1,0:T(8,128)(2,1)S(1)}, bf16[2064,1024]{1,0:T(8,128)(2,1)S(1)}, u32[]{:S(2)}, u32[]{:S(2)}) collective-permute-start(bf16[2064,1024]{1,0:T(8,128)(2,1)S(1)} %stack.17), channel_id=1, source_target_pairs={{4,0},{5,1},{6,2},{7,3},{20,16},{21,17},{22,18},{23,19}} | collective-permute-start | bytes 12681224 | tf_op jit(solution)/shard_map/ppermute | solution.py:459
  35.9 0.7 collective-permute-start.15
  36.6 0.7 collective-permute-start.13
  37.3 0.7 collective-permute-start.14
  38.0 0.7 collective-permute-start.16
  38.7 0.0 collective-permute-done.15.t2
  38.7 0.7 collective-permute-start.17
  39.4 29.3 %collective-permute-done.10.event.lift = bf16[2064,1024]{1,0:T(8,128)(2,1)S(1)} collective-permute-done((bf16[2064,1024]{1,0:T(8,128)(2,1)S(1)}, bf16[2064,1024]{1,0:T(8,128)(2,1)S(1)}, u32[]{:S(2)}, u32[]{:S(2)}) %collective-permute-start.10) | collective-permute-done | bytes 4227104 | tf_op jit(solution)/shard_map/ppermute | solution.py:459
  68.7 0.6 hand_0.1.event
  69.4 12.6 %ahead.1 = (bf16[8,256,1024]{2,1,0:T(8,128)(2,1)S(1)}, f32[8,256]{1,0:T(8,128)S(1)}, bf16[256,1024]{1,0:T(8,128)(2,1)S(1)}, f32[256,1024]{1,0:T(8,128)S(1)}, bf1...) custom-call(s32[3]{0:T(128)S(1)} %copy-done.5, bf16[256,1024]{1,0:T(8,128)(2,1)S(1)} %hand_0.1.event, ...), custom_call_target="tpu_custom_call" | custom-call | flops 9663676416 | bytes 15769600 | tf_op jit(solution)/shard_map/ahead/pallas_call | solution.py:473
  82.0 0.7 collective-permute-start.11
  82.7 0.0 collective-permute-done.13.t0
  82.7 0.0 copy-start.8
  82.7 0.0 copy-start.9
  82.7 0.7 collective-permute-start.12
  83.4 0.0 collective-permute-done.14.t1
  83.4 0.0 collective-permute-done.16.t3
  83.4 0.0 collective-permute-done.11.near
  83.4 0.0 collective-permute-done.12.far
  83.4 0.6 turn.1.ends_1
  84.0 1.3 %collective-permute-start.18 = (bf16[4,272,768]{2,1,0:T(8,128)(2,1)S(1)}, bf16[4,272,768]{2,1,0:T(8,128)(2,1)S(1)}, u32[]{:S(2)}, u32[]{:S(2)}) collective-permute-start(bf16[4,272,768]{2,1,0:T(8,128)(2,1)S(1)} %turn.1.ends_1), channel_id=1, source_target_pairs={{4,0},{5,1},{6,2},{7,3},{20,16},{21,17},{22,18},{23,19}} | collective-permute-start | bytes 5013512 | tf_op jit(solution)/shard_map/ppermute | solution.py:459
  85.3 4.0 %collective-permute-start.22 = (bf16[256,1024]{1,0:T(8,128)(2,1)S(1)}, bf16[256,1024]{1,0:T(8,128)(2,1)S(1)}, u32[]{:S(2)}, u32[]{:S(2)}) collective-permute-start(bf16[256,1024]{1,0:T(8,128)(2,1)S(1)} %hand_0.1.event), channel_id=1, source_target_pairs={{1,0},{2,1},{3,2},{0,3},{17,16},{18,17},{19,18},{16,19}} | collective-permute-start | bytes 1572872 | tf_op jit(solution)/shard_map/ppermute | solution.py:459
  89.3 1.9 %collective-permute-start.23 = (bf16[256,1024]{1,0:T(8,128)(2,1)S(1)}, bf16[256,1024]{1,0:T(8,128)(2,1)S(1)}, u32[]{:S(2)}, u32[]{:S(2)}) collective-permute-start(bf16[256,1024]{1,0:T(8,128)(2,1)S(1)} %hand_0.1.event), channel_id=1, source_target_pairs={{0,2},{1,3},{2,0},{3,1},{16,18},{17,19},{18,16},{19,17}} | collective-permute-start | bytes 1572872 | tf_op jit(solution)/shard_map/ppermute | solution.py:459
  91.3 2.5 %collective-permute-start.24 = (bf16[256,1024]{1,0:T(8,128)(2,1)S(1)}, bf16[256,1024]{1,0:T(8,128)(2,1)S(1)}, u32[]{:S(2)}, u32[]{:S(2)}) collective-permute-start(bf16[256,1024]{1,0:T(8,128)(2,1)S(1)} %hand_0.1.event), channel_id=1, source_target_pairs={{0,1},{1,2},{2,3},{3,0},{16,17},{17,18},{18,19},{19,16}} | collective-permute-start | bytes 1572872 | tf_op jit(solution)/shard_map/ppermute | solution.py:459
  93.7 5.0 %collective-permute-done.18.ends_0 = bf16[4,272,768]{2,1,0:T(8,128)(2,1)S(1)} collective-permute-done((bf16[4,272,768]{2,1,0:T(8,128)(2,1)S(1)}, bf16[4,272,768]{2,1,0:T(8,128)(2,1)S(1)}, u32[]{:S(2)}, u32[]{:S(2)}) %collective-permute-start.18) | collective-permute-done | bytes 1671200 | tf_op jit(solution)/shard_map/ppermute | solution.py:459
  98.7 6.3 %moments.1 = (bf16[4,768,256]{2,1,0:T(8,128)(2,1)S(1)}, bf16[16,1024]{1,0:T(8,128)(2,1)S(1)}, f32[8,256]{1,0:T(8,128)}, f32[8,256]{1,0:T(8,128)}, f32[2,8,256]{2,1,0:T(8,128)S(1)}) custom-call(s32[3]{0:T(128)S(1)} %copy-done.5, bf16[4,272,768]{2,1,0:T(8,128)(2,1)S(1)} %turn.1.ends_1, ...), custom_call_target="tpu_custom_call", output_to_operand_aliasing={{0}: (9, {}), {1}: (10, {})} | custom-call | flops 4294967296 | bytes 19226624 | tf_op jit(solution)/shard_map/moments/pallas_call | solution.py:473
  105.0 9.1 %collective-permute-start.19 = (f32[2,8,256]{2,1,0:T(8,128)S(1)}, f32[2,8,256]{2,1,0:T(8,128)S(1)}, u32[]{:S(2)}, u32[]{:S(2)}) collective-permute-start(f32[2,8,256]{2,1,0:T(8,128)S(1)} %get-tuple-element.42.s0), channel_id=1, source_target_pairs={{1,0},{2,1},{3,2},{0,3},{5,4},{6,5},{7,6},{4,7},{9,8},{10,9},{11,1... | collective-permute-start | bytes 49160 | tf_op jit(solution)/shard_map/ppermute | solution.py:459
  114.0 0.0 collective-permute-start.20
  114.1 0.6 collective-permute-start.21
  114.6 0.0 copy-start.10
  114.6 0.0 copy-start.12
  114.7 0.0 copy-start.13
  114.7 3.9 %last.1 = (bf16[256,1024]{1,0:T(8,128)(2,1)}, bf16[16,256]{1,0:T(8,128)(2,1)S(1)}) custom-call(s32[3]{0:T(128)S(1)} %copy-done.5, bf16[256,1024]{1,0:T(8,128)(2,1)S(1)} %bitcast.16, bf16[256,1024]{1,0:T(8,128)(2,1)S(1)} %collective-permute-done.g1.a1, bf16[256,1024]{1,0:T(8,128)(2,1)S(1)} %collective-permute-done.9.g2.a2, ...), custom_call_target="tpu_custom_call" | custom-call | flops 1073741824 | bytes 13902848 | tf_op jit(solution)/shard_map/last/pallas_call | solution.py:473
  118.6 0.1 collective-permute-done.20.s2
  118.7 0.9 collective-permute-done.21.s3
  119.6 1.3 %innovation.1 = (f32[8,4,128]{2,1,0:T(4,128)}, bf16[1,256]{1,0:T(2,128)(2,1)}, bf16[256,1024]{1,0:T(8,128)(2,1)}) custom-call(s32[3]{0:T(128)S(1)} %copy-done.5, s32[4,8]{1,0:T(4,128)S(1)} %bitcast.22, s32[8]{0:T(128)S(1)} %copy-done.13, f32[2,8,256]{2,1,0:T(8,128)S(1)} %get-tuple-element.42.s0, ...), custom_call_target="tpu_custom_call", output_to_operand_aliasing={{2}: (15, {})} | custom-call | bytes 200000 | tf_op jit(solution)/shard_map/innovation/pallas_call | solution.py:574
  (26 shorter events, 0.1 us)
Async XLA Ops:
  0.6 27.4 %copy-start = (bf16[1,256,1024]{2,1,0:T(8,128)(2,1)S(1)}, bf16[1,256,1024]{2,1,0:T(8,128)(2,1)}, u32[]{:S(2)}) copy-start(bf16[1,256,1024]{2,1,0:T(8,128)(2,1)} %param.12) | copy-start | bytes 1572868
  0.6 28.7 %collective-permute-start = (bf16[256,1024]{1,0:T(8,128)(2,1)}, bf16[256,1024]{1,0:T(8,128)(2,1)S(1)}, u32[]{:S(2)}, u32[]{:S(2)}) collective-permute-start(bf16[256,1024]{1,0:T(8,128)(2,1)} %bitcast.8), channel_id=1, source_target_pairs={{13,12},{14,13},{15,14},{12,15},{9,8},{10,9},{11,10},{8,11},{5,4},... | collective-permute-start | bytes 1572872 | tf_op jit(solution)/shard_map/ppermute | solution.py:459
  1.5 27.9 %collective-permute-start.1 = (bf16[256,1024]{1,0:T(8,128)(2,1)}, bf16[256,1024]{1,0:T(8,128)(2,1)S(1)}, u32[]{:S(2)}, u32[]{:S(2)}) collective-permute-start(bf16[256,1024]{1,0:T(8,128)(2,1)} %bitcast.9), channel_id=1, source_target_pairs={{14,12},{13,15},{10,8},{9,11},{4,5},{5,6},{6,7},{7,4},{30,28},{29,... | collective-permute-start | bytes 1572872 | tf_op jit(solution)/shard_map/ppermute | solution.py:459
  2.8 25.3 %copy-start.5 = (s32[3]{0:T(128)S(1)}, s32[3]{0:T(128)}, u32[]{:S(2)}) copy-start(s32[3]{0:T(128)} %pad_add_fusion.where) | copy-start | bytes 40
  2.8 26.6 %copy-start.1 = (bf16[1,256,1024]{2,1,0:T(8,128)(2,1)S(1)}, bf16[1,256,1024]{2,1,0:T(8,128)(2,1)}, u32[]{:S(2)}) copy-start(bf16[1,256,1024]{2,1,0:T(8,128)(2,1)} %param.14) | copy-start | bytes 1572868
  2.8 26.6 %copy-start.2 = (bf16[2,256,1024]{2,1,0:T(8,128)(2,1)S(1)}, bf16[2,256,1024]{2,1,0:T(8,128)(2,1)}, u32[]{:S(2)}) copy-start(bf16[2,256,1024]{2,1,0:T(8,128)(2,1)} %refs_0_.1) | copy-start | bytes 3145732
  2.8 26.6 %copy-start.7 = (f32[1,256]{1,0:T(1,128)S(1)}, f32[1,256]{1,0:T(1,128)}, u32[]{:S(2)}) copy-start(f32[1,256]{1,0:T(1,128)} %offset.9) | copy-start | bytes 3076
  2.8 26.6 %copy-start.11 = (bf16[2,256]{1,0:T(2,128)(2,1)S(1)}, bf16[2,256]{1,0:T(2,128)(2,1)}, u32[]{:S(2)}) copy-start(bf16[2,256]{1,0:T(2,128)(2,1)} %refs_1_.1) | copy-start | bytes 3076
  5.5 22.6 %collective-permute-start.3 = (bf16[272,768]{1,0:T(8,128)(2,1)}, bf16[272,768]{1,0:T(8,128)(2,1)S(1)}, u32[]{:S(2)}, u32[]{:S(2)}) collective-permute-start(bf16[272,768]{1,0:T(8,128)(2,1)} %pack.1.n0), channel_id=1, source_target_pairs={{2,12},{3,13},{0,14},{1,15},{6,4},{7,5},{4,6},{5,7},{18,28},{19,29... | collective-permute-start | bytes 1253384 | tf_op jit(solution)/shard_map/ppermute | solution.py:459
  17.6 11.7 %collective-permute-start.2 = (bf16[272,768]{1,0:T(8,128)(2,1)}, bf16[272,768]{1,0:T(8,128)(2,1)S(1)}, u32[]{:S(2)}, u32[]{:S(2)}) collective-permute-start(bf16[272,768]{1,0:T(8,128)(2,1)} %pack.1.n0), channel_id=1, source_target_pairs={{13,12},{14,13},{15,14},{12,15},{5,4},{6,5},{7,6},{4,7},{29,28},{3... | collective-permute-start | bytes 1253384 | tf_op jit(solution)/shard_map/ppermute | solution.py:459
  18.3 11.0 %collective-permute-start.4 = (bf16[272,768]{1,0:T(8,128)(2,1)}, bf16[272,768]{1,0:T(8,128)(2,1)S(1)}, u32[]{:S(2)}, u32[]{:S(2)}) collective-permute-start(bf16[272,768]{1,0:T(8,128)(2,1)} %pack.1.n0), channel_id=1, source_target_pairs={{15,12},{12,13},{13,14},{14,15},{7,4},{4,5},{5,6},{6,7},{31,28},{2... | collective-permute-start | bytes 1253384 | tf_op jit(solution)/shard_map/ppermute | solution.py:459
  28.6 4.8 %collective-permute-start.9 = (bf16[256,1024]{1,0:T(8,128)(2,1)S(1)}, bf16[256,1024]{1,0:T(8,128)(2,1)S(1)}, u32[]{:S(2)}, u32[]{:S(2)}) collective-permute-start(bf16[256,1024]{1,0:T(8,128)(2,1)S(1)} %hand_1.1), channel_id=1, source_target_pairs={{4,6},{5,7},{6,4},{7,5},{20,22},{21,23},{22,20},{23,21}} | collective-permute-start | bytes 1572872 | tf_op jit(solution)/shard_map/ppermute | solution.py:459
  30.0 2.8 %collective-permute-start.5 = (bf16[272,768]{1,0:T(8,128)(2,1)S(1)}, bf16[272,768]{1,0:T(8,128)(2,1)S(1)}, u32[]{:S(2)}, u32[]{:S(2)}) collective-permute-start(bf16[272,768]{1,0:T(8,128)(2,1)S(1)} %get-tuple-element.30.refs_4_), channel_id=1, source_target_pairs={{12,8},{13,9},{14,10},{15,11},{28,24},{29,25},{30,26},{31,27}} | collective-permute-start | bytes 1253384 | tf_op jit(solution)/shard_map/ppermute | solution.py:459
  30.7 2.1 %collective-permute-start.6 = (bf16[272,768]{1,0:T(8,128)(2,1)S(1)}, bf16[272,768]{1,0:T(8,128)(2,1)S(1)}, u32[]{:S(2)}, u32[]{:S(2)}) collective-permute-start(bf16[272,768]{1,0:T(8,128)(2,1)S(1)} %get-tuple-element.30.refs_4_), channel_id=1, source_target_pairs={{13,8},{14,9},{15,10},{12,11},{29,24},{30,25},{31,26},{28,27}} | collective-permute-start | bytes 1253384 | tf_op jit(solution)/shard_map/ppermute | solution.py:459
  31.4 1.4 %collective-permute-start.7 = (bf16[272,768]{1,0:T(8,128)(2,1)S(1)}, bf16[272,768]{1,0:T(8,128)(2,1)S(1)}, u32[]{:S(2)}, u32[]{:S(2)}) collective-permute-start(bf16[272,768]{1,0:T(8,128)(2,1)S(1)} %get-tuple-element.30.refs_4_), channel_id=1, source_target_pairs={{14,8},{15,9},{12,10},{13,11},{30,24},{31,25},{28,26},{29,27}} | collective-permute-start | bytes 1253384 | tf_op jit(solution)/shard_map/ppermute | solution.py:459
  32.1 0.7 collective-permute-start.8
  32.8 1.0 copy-start.4
  34.4 35.0 %copy-start.3 = (bf16[8,256,1024]{2,1,0:T(8,128)(2,1)S(1)}, bf16[8,256,1024]{2,1,0:T(8,128)(2,1)}, u32[]{:S(2)}) copy-start(bf16[8,256,1024]{2,1,0:T(8,128)(2,1)} %gain.1) | copy-start | bytes 12582916
  34.4 34.4 %collective-permute-start.10 = (bf16[2064,1024]{1,0:T(8,128)(2,1)S(1)}, bf16[2064,1024]{1,0:T(8,128)(2,1)S(1)}, u32[]{:S(2)}, u32[]{:S(2)}) collective-permute-start(bf16[2064,1024]{1,0:T(8,128)(2,1)S(1)} %stack.17), channel_id=1, source_target_pairs={{4,0},{5,1},{6,2},{7,3},{20,16},{21,17},{22,18},{23,19}} | collective-permute-start | bytes 12681224 | tf_op jit(solution)/shard_map/ppermute | solution.py:459
  35.9 2.8 %collective-permute-start.15 = (bf16[272,768]{1,0:T(8,128)(2,1)S(1)}, bf16[272,768]{1,0:T(8,128)(2,1)S(1)}, u32[]{:S(2)}, u32[]{:S(2)}) collective-permute-start(bf16[272,768]{1,0:T(8,128)(2,1)S(1)} %get-tuple-element.33.event.own), channel_id=1, source_target_pairs={{10,4},{11,5},{8,6},{9,7},{26,20},{27,21},{24,22},{25,23}} | collective-permute-start | bytes 1253384 | tf_op jit(solution)/shard_map/ppermute | solution.py:459
  36.6 46.1 %collective-permute-start.13 = (bf16[272,768]{1,0:T(8,128)(2,1)S(1)}, bf16[272,768]{1,0:T(8,128)(2,1)S(1)}, u32[]{:S(2)}, u32[]{:S(2)}) collective-permute-start(bf16[272,768]{1,0:T(8,128)(2,1)S(1)} %get-tuple-element.33.event.own), channel_id=1, source_target_pairs={{8,4},{9,5},{10,6},{11,7},{24,20},{25,21},{26,22},{27,23}} | collective-permute-start | bytes 1253384 | tf_op jit(solution)/shard_map/ppermute | solution.py:459
  37.3 46.1 %collective-permute-start.14 = (bf16[272,768]{1,0:T(8,128)(2,1)S(1)}, bf16[272,768]{1,0:T(8,128)(2,1)S(1)}, u32[]{:S(2)}, u32[]{:S(2)}) collective-permute-start(bf16[272,768]{1,0:T(8,128)(2,1)S(1)} %get-tuple-element.33.event.own), channel_id=1, source_target_pairs={{9,4},{10,5},{11,6},{25,20},{26,21},{27,22}} | collective-permute-start | bytes 1253384 | tf_op jit(solution)/shard_map/ppermute | solution.py:459
  38.0 45.4 %collective-permute-start.16 = (bf16[272,768]{1,0:T(8,128)(2,1)S(1)}, bf16[272,768]{1,0:T(8,128)(2,1)S(1)}, u32[]{:S(2)}, u32[]{:S(2)}) collective-permute-start(bf16[272,768]{1,0:T(8,128)(2,1)S(1)} %get-tuple-element.33.event.own), channel_id=1, source_target_pairs={{8,5},{9,6},{10,7},{24,21},{25,22},{26,23}} | collective-permute-start | bytes 1253384 | tf_op jit(solution)/shard_map/ppermute | solution.py:459
  38.7 44.7 %collective-permute-start.17 = (bf16[272,768]{1,0:T(8,128)(2,1)S(1)}, bf16[272,768]{1,0:T(8,128)(2,1)S(1)}, u32[]{:S(2)}, u32[]{:S(2)}) collective-permute-start(bf16[272,768]{1,0:T(8,128)(2,1)S(1)} %collective-permute-done.15.t2), channel_id=1, source_target_pairs={{6,7},{5,4},{22,23},{21,20}} | collective-permute-start | bytes 1253384 | tf_op jit(solution)/shard_map/ppermute | solution.py:459
  82.0 1.4 %collective-permute-start.11 = (bf16[256,256]{1,0:T(8,128)(2,1)S(1)}, bf16[256,256]{1,0:T(8,128)(2,1)S(1)}, u32[]{:S(2)}, u32[]{:S(2)}) collective-permute-start(bf16[256,256]{1,0:T(8,128)(2,1)S(1)} %get-tuple-element.36), channel_id=1, source_target_pairs={{12,13},{13,14},{14,15},{15,12},{8,9},{9,10},{10,11},{11,8},{28,29... | collective-permute-start | bytes 393224 | tf_op jit(solution)/shard_map/ppermute | solution.py:459
  82.7 16.0 %copy-start.8 = (f32[8,256]{1,0:T(8,128)S(1)}, f32[8,256]{1,0:T(8,128)}, u32[]{:S(2)}) copy-start(f32[8,256]{1,0:T(8,128)} %offset.8) | copy-start | bytes 24580
  82.7 16.0 %copy-start.9 = (f32[8,256]{1,0:T(8,128)S(1)}, f32[8,256]{1,0:T(8,128)}, u32[]{:S(2)}) copy-start(f32[8,256]{1,0:T(8,128)} %var.1) | copy-start | bytes 24580
  82.7 0.7 collective-permute-start.12
  84.0 14.7 %collective-permute-start.18 = (bf16[4,272,768]{2,1,0:T(8,128)(2,1)S(1)}, bf16[4,272,768]{2,1,0:T(8,128)(2,1)S(1)}, u32[]{:S(2)}, u32[]{:S(2)}) collective-permute-start(bf16[4,272,768]{2,1,0:T(8,128)(2,1)S(1)} %turn.1.ends_1), channel_id=1, source_target_pairs={{4,0},{5,1},{6,2},{7,3},{20,16},{21,17},{22,18},{23,19}} | collective-permute-start | bytes 5013512 | tf_op jit(solution)/shard_map/ppermute | solution.py:459
  85.3 28.8 %collective-permute-start.22 = (bf16[256,1024]{1,0:T(8,128)(2,1)S(1)}, bf16[256,1024]{1,0:T(8,128)(2,1)S(1)}, u32[]{:S(2)}, u32[]{:S(2)}) collective-permute-start(bf16[256,1024]{1,0:T(8,128)(2,1)S(1)} %hand_0.1.event), channel_id=1, source_target_pairs={{1,0},{2,1},{3,2},{0,3},{17,16},{18,17},{19,18},{16,19}} | collective-permute-start | bytes 1572872 | tf_op jit(solution)/shard_map/ppermute | solution.py:459
  89.3 25.3 %collective-permute-start.23 = (bf16[256,1024]{1,0:T(8,128)(2,1)S(1)}, bf16[256,1024]{1,0:T(8,128)(2,1)S(1)}, u32[]{:S(2)}, u32[]{:S(2)}) collective-permute-start(bf16[256,1024]{1,0:T(8,128)(2,1)S(1)} %hand_0.1.event), channel_id=1, source_target_pairs={{0,2},{1,3},{2,0},{3,1},{16,18},{17,19},{18,16},{19,17}} | collective-permute-start | bytes 1572872 | tf_op jit(solution)/shard_map/ppermute | solution.py:459
  91.3 23.4 %collective-permute-start.24 = (bf16[256,1024]{1,0:T(8,128)(2,1)S(1)}, bf16[256,1024]{1,0:T(8,128)(2,1)S(1)}, u32[]{:S(2)}, u32[]{:S(2)}) collective-permute-start(bf16[256,1024]{1,0:T(8,128)(2,1)S(1)} %hand_0.1.event), channel_id=1, source_target_pairs={{0,1},{1,2},{2,3},{3,0},{16,17},{17,18},{18,19},{19,16}} | collective-permute-start | bytes 1572872 | tf_op jit(solution)/shard_map/ppermute | solution.py:459
  105.0 13.6 %collective-permute-start.19 = (f32[2,8,256]{2,1,0:T(8,128)S(1)}, f32[2,8,256]{2,1,0:T(8,128)S(1)}, u32[]{:S(2)}, u32[]{:S(2)}) collective-permute-start(f32[2,8,256]{2,1,0:T(8,128)S(1)} %get-tuple-element.42.s0), channel_id=1, source_target_pairs={{1,0},{2,1},{3,2},{0,3},{5,4},{6,5},{7,6},{4,7},{9,8},{10,9},{11,1... | collective-permute-start | bytes 49160 | tf_op jit(solution)/shard_map/ppermute | solution.py:459
  114.0 4.6 %collective-permute-start.20 = (f32[2,8,256]{2,1,0:T(8,128)S(1)}, f32[2,8,256]{2,1,0:T(8,128)S(1)}, u32[]{:S(2)}, u32[]{:S(2)}) collective-permute-start(f32[2,8,256]{2,1,0:T(8,128)S(1)} %get-tuple-element.42.s0), channel_id=1, source_target_pairs={{2,0},{3,1},{0,2},{1,3},{6,4},{7,5},{4,6},{5,7},{10,8},{11,9},{8,1... | collective-permute-start | bytes 49160 | tf_op jit(solution)/shard_map/ppermute | solution.py:459
  114.1 5.5 %collective-permute-start.21 = (f32[2,8,256]{2,1,0:T(8,128)S(1)}, f32[2,8,256]{2,1,0:T(8,128)S(1)}, u32[]{:S(2)}, u32[]{:S(2)}) collective-permute-start(f32[2,8,256]{2,1,0:T(8,128)S(1)} %get-tuple-element.42.s0), channel_id=1, source_target_pairs={{3,0},{0,1},{1,2},{2,3},{7,4},{4,5},{5,6},{6,7},{11,8},{8,9},{9,10... | collective-permute-start | bytes 49160 | tf_op jit(solution)/shard_map/ppermute | solution.py:459
  114.6 5.0 %copy-start.6 = (f32[8,4,128]{2,1,0:T(4,128)S(1)}, f32[8,4,128]{2,1,0:T(4,128)}, u32[]{:S(2)}) copy-start(f32[8,4,128]{2,1,0:T(4,128)} %value.1) | copy-start | bytes 49156
  114.6 5.0 %copy-start.10 = (f32[1024]{0:T(1024)S(1)}, f32[1024]{0:T(1024)}, u32[]{:S(2)}) copy-start(f32[1024]{0:T(1024)} %param.23) | copy-start | bytes 12292
  114.6 5.0 %copy-start.12 = (s32[8,4]{0,1:T(4,128)S(1)}, s32[8,4]{0,1:T(4,128)}, u32[]{:S(2)}) copy-start(s32[8,4]{0,1:T(4,128)} %param.20) | copy-start | bytes 388
  114.7 5.0 %copy-start.13 = (s32[8]{0:T(128)S(1)}, s32[8]{0:T(128)}, u32[]{:S(2)}) copy-start(s32[8]{0:T(128)} %counts.1) | copy-start | bytes 100

commit v3 on v2

--- a/solution.py
+++ b/solution.py
@@ -145,7 +145,7 @@
 
 
 def by_relay(z, own, after, across, before, handed):
-    return own, (z < RING - 1, after, handed), across, (z > 0, before, handed)
+    return own, after, across, (z > 0, before, handed)
 
 
 def lay_out(z, parcels, full, mean):
@@ -351,7 +351,7 @@
             out_spread[pl.ds(k, 1), :] = spread
             return carry
 
-        lax.fori_loop(0, gain.shape[0], one, 0, unroll=2)
+        lax.fori_loop(0, gain.shape[0], one, 0, unroll=4)
 
     @pl.when(seg == 0)
     def _():
@@ -533,9 +533,9 @@
     across = send(parcel_2, ((2, 1),), 2)
     sides = [
         route(parcel_2, [((2, start), (1, to)) for start, to in moves])
-        for moves in (((1, 0), (2, 1), (3, 2)), ((0, 1), (1, 2), (2, 3)))
+        for moves in (((1, 0), (2, 1), (3, 2), (0, 3)), ((0, 1), (1, 2), (2, 3)))
     ]
-    third = [own, sides[0], across, sides[1], route(across, within((1,), ((2, 3), (1, 0))))]
+    third = [own, sides[0], across, sides[1], route(across, within((1,), ((1, 0),)))]
     (lift,) = call(stack_kernel, "stack", (shape((2 * states + TAIL, states)),), (parcel_2, gain, *gains_1, parcel, *first), [], 0)
     lift = send(lift, ((1, 0),), 0)
     gain_0 = hand(0, lift)

time: 121 us -> 120 us (level)
  starting transfers between devices: 44.2 us -> 38 us
  waiting for transfers between devices: 44.4 us -> 48.6 us
    ppermute x25, starting transfers between devices: 44.2 us -> 38 us  [route(): return lax.ppermute(block, ('tm', 'tile'), table)]
    ppermute x25, waiting for transfers between devices: 44.4 us -> 48.6 us  [route(): return lax.ppermute(block, ('tm', 'tile'), table)]
  transfers between devices with their start and end apart: 25 -> 25, of which waited for: 5 -> 4; matrix products, arithmetic and copies ran while one was open for 0% -> 0% of each run, Pallas kernels for 23% -> 23%
where the time goes in v3:
time: 120 us; the launch traced here: 119 us
  waiting for transfers between devices  48.6 us (40%)
  starting transfers between devices  38 us (32%)
  Pallas kernels  30.1 us (25%)
  between operations  1.32 us (1%)
    ppermute x25, waiting for transfers between devices, route(): return lax.ppermute(block, ('tm', 'tile'), table)  48.6 us
    ppermute x25, starting transfers between devices, route(): return lax.ppermute(block, ('tm', 'tile'), table)  38 us
    pallas_call x7, Pallas kernels, call(): pl.pallas_call(kernel, out_shape=out_shape, in_specs=[smem()] + [vmem()]...  25 us
    pallas_call x3, Pallas kernels, pack(): pl.pallas_call(kernel, out_shape=out_shape, in_specs=[smem()] + [pl.Block...  3.8 us
  transfers between devices with their start and end apart: 25, of which 4 were waited for; matrix products, arithmetic and copies ran while one was open for 0% of the time, Pallas kernels for 23%

profile of v3, /device:TPU:0, one launch (start us, length us, event | category | flops | bytes accessed | tf_op | source)
XLA Modules:
  0.0 119.1 jit_solution(6979370281704205701)
XLA Ops:
  0.6 0.8 collective-permute-start
  1.5 0.7 collective-permute-start.1
  2.2 0.6 pad_add_fusion.where
  2.8 0.0 copy-start.11
  2.8 2.7 %pack.1.n0 = bf16[272,768]{1,0:T(8,128)(2,1)} custom-call(s32[3]{0:T(128)} %pad_add_fusion.where, bf16[2,256,1024]{2,1,0:T(8,128)(2,1)} %refs_0_.1, bf16[256,1024]{1,0:T(8,128)(2,1)} %bitcast.17, bf16[2,256]{1,0:T(2,128)(2,1)} %refs_1_.1, f32[1,256]{1,0:T(1,128)} %offset.9), custom_call_target="tpu_custom_call" | custom-call | bytes 1000000 | tf_op jit(solution)/shard_map/pack/pallas_call | solution.py:486
  5.5 12.2 %collective-permute-start.3 = (bf16[272,768]{1,0:T(8,128)(2,1)}, bf16[272,768]{1,0:T(8,128)(2,1)S(1)}, u32[]{:S(2)}, u32[]{:S(2)}) collective-permute-start(bf16[272,768]{1,0:T(8,128)(2,1)} %pack.1.n0), channel_id=1, source_target_pairs={{2,12},{3,13},{0,14},{1,15},{6,4},{7,5},{4,6},{5,7},{18,28},{19,29... | collective-permute-start | bytes 1253384 | tf_op jit(solution)/shard_map/ppermute | solution.py:459
  17.6 0.7 collective-permute-start.2
  18.3 0.7 collective-permute-start.4
  19.0 9.0 %collective-permute-done.3.refs_3_.event.n2 = bf16[272,768]{1,0:T(8,128)(2,1)S(1)} collective-permute-done((bf16[272,768]{1,0:T(8,128)(2,1)}, bf16[272,768]{1,0:T(8,128)(2,1)S(1)}, u32[]{:S(2)}, u32[]{:S(2)}) %collective-permute-start.3) | collective-permute-done | bytes 417824 | tf_op jit(solution)/shard_map/ppermute | solution.py:459
  28.1 0.6 hand_1.1
  28.6 0.7 collective-permute-start.9
  29.3 0.0 collective-permute-done.2.refs_2_.n1
  29.3 0.0 collective-permute-done.4.refs_4_.n3
  29.3 0.0 collective-permute-done.g1.a1
  29.4 0.0 collective-permute-done.1.g2.g3.a3
  29.4 0.6 pairs_3.1
  30.0 0.7 collective-permute-start.5
  30.7 0.7 collective-permute-start.6
  31.4 0.7 collective-permute-start.7
  32.1 0.7 collective-permute-start.8
  32.8 0.0 collective-permute-done.5.refs_0_
  32.8 0.0 collective-permute-done.6.refs_1_
  32.8 0.0 collective-permute-done.8.refs_3_
  32.8 0.0 copy-start.4
  32.8 0.6 pairs_2.1
  33.4 0.0 collective-permute-done.9.g2.a2
  33.4 0.4 copy-done.4
  33.8 0.5 stack.17
  34.4 0.0 copy-start.3
  34.4 1.6 %collective-permute-start.10 = (bf16[2064,1024]{1,0:T(8,128)(2,1)S(1)}, bf16[2064,1024]{1,0:T(8,128)(2,1)S(1)}, u32[]{:S(2)}, u32[]{:S(2)}) collective-permute-start(bf16[2064,1024]{1,0:T(8,128)(2,1)S(1)} %stack.17), channel_id=1, source_target_pairs={{4,0},{5,1},{6,2},{7,3},{20,16},{21,17},{22,18},{23,19}} | collective-permute-start | bytes 12681224 | tf_op jit(solution)/shard_map/ppermute | solution.py:459
  35.9 0.7 collective-permute-start.15
  36.6 0.7 collective-permute-start.13
  37.3 0.7 collective-permute-start.14
  38.0 0.7 collective-permute-start.16
  38.7 0.0 collective-permute-done.15.t2
  38.7 0.7 collective-permute-start.17
  39.4 29.3 %collective-permute-done.10.event.lift = bf16[2064,1024]{1,0:T(8,128)(2,1)S(1)} collective-permute-done((bf16[2064,1024]{1,0:T(8,128)(2,1)S(1)}, bf16[2064,1024]{1,0:T(8,128)(2,1)S(1)}, u32[]{:S(2)}, u32[]{:S(2)}) %collective-permute-start.10) | collective-permute-done | bytes 4227104 | tf_op jit(solution)/shard_map/ppermute | solution.py:459
  68.7 0.6 hand_0.1.event
  69.4 12.6 %ahead.1 = (bf16[8,256,1024]{2,1,0:T(8,128)(2,1)S(1)}, f32[8,256]{1,0:T(8,128)S(1)}, bf16[256,1024]{1,0:T(8,128)(2,1)S(1)}, f32[256,1024]{1,0:T(8,128)S(1)}, bf1...) custom-call(s32[3]{0:T(128)S(1)} %copy-done.5, bf16[256,1024]{1,0:T(8,128)(2,1)S(1)} %hand_0.1.event, ...), custom_call_target="tpu_custom_call" | custom-call | flops 9663676416 | bytes 15769600 | tf_op jit(solution)/shard_map/ahead/pallas_call | solution.py:473
  82.0 0.7 collective-permute-start.11
  82.7 0.0 collective-permute-done.13.t0
  82.7 0.0 copy-start.8
  82.7 0.0 copy-start.9
  82.7 0.7 collective-permute-start.12
  83.4 0.0 collective-permute-done.14.t1
  83.4 0.0 collective-permute-done.17.t4
  83.4 0.0 collective-permute-done.11.near
  83.4 0.6 turn.1.ends_1
  84.0 1.3 %collective-permute-start.18 = (bf16[4,272,768]{2,1,0:T(8,128)(2,1)S(1)}, bf16[4,272,768]{2,1,0:T(8,128)(2,1)S(1)}, u32[]{:S(2)}, u32[]{:S(2)}) collective-permute-start(bf16[4,272,768]{2,1,0:T(8,128)(2,1)S(1)} %turn.1.ends_1), channel_id=1, source_target_pairs={{4,0},{5,1},{6,2},{7,3},{20,16},{21,17},{22,18},{23,19}} | collective-permute-start | bytes 5013512 | tf_op jit(solution)/shard_map/ppermute | solution.py:459
  85.3 4.0 %collective-permute-start.22 = (bf16[256,1024]{1,0:T(8,128)(2,1)S(1)}, bf16[256,1024]{1,0:T(8,128)(2,1)S(1)}, u32[]{:S(2)}, u32[]{:S(2)}) collective-permute-start(bf16[256,1024]{1,0:T(8,128)(2,1)S(1)} %hand_0.1.event), channel_id=1, source_target_pairs={{1,0},{2,1},{3,2},{0,3},{17,16},{18,17},{19,18},{16,19}} | collective-permute-start | bytes 1572872 | tf_op jit(solution)/shard_map/ppermute | solution.py:459
  89.3 1.9 %collective-permute-start.23 = (bf16[256,1024]{1,0:T(8,128)(2,1)S(1)}, bf16[256,1024]{1,0:T(8,128)(2,1)S(1)}, u32[]{:S(2)}, u32[]{:S(2)}) collective-permute-start(bf16[256,1024]{1,0:T(8,128)(2,1)S(1)} %hand_0.1.event), channel_id=1, source_target_pairs={{0,2},{1,3},{2,0},{3,1},{16,18},{17,19},{18,16},{19,17}} | collective-permute-start | bytes 1572872 | tf_op jit(solution)/shard_map/ppermute | solution.py:459
  91.3 2.5 %collective-permute-start.24 = (bf16[256,1024]{1,0:T(8,128)(2,1)S(1)}, bf16[256,1024]{1,0:T(8,128)(2,1)S(1)}, u32[]{:S(2)}, u32[]{:S(2)}) collective-permute-start(bf16[256,1024]{1,0:T(8,128)(2,1)S(1)} %hand_0.1.event), channel_id=1, source_target_pairs={{0,1},{1,2},{2,3},{3,0},{16,17},{17,18},{18,19},{19,16}} | collective-permute-start | bytes 1572872 | tf_op jit(solution)/shard_map/ppermute | solution.py:459
  93.7 5.0 %collective-permute-done.18.ends_0 = bf16[4,272,768]{2,1,0:T(8,128)(2,1)S(1)} collective-permute-done((bf16[4,272,768]{2,1,0:T(8,128)(2,1)S(1)}, bf16[4,272,768]{2,1,0:T(8,128)(2,1)S(1)}, u32[]{:S(2)}, u32[]{:S(2)}) %collective-permute-start.18) | collective-permute-done | bytes 1671200 | tf_op jit(solution)/shard_map/ppermute | solution.py:459
  98.7 6.2 %moments.1 = (bf16[4,768,256]{2,1,0:T(8,128)(2,1)S(1)}, bf16[16,1024]{1,0:T(8,128)(2,1)S(1)}, f32[8,256]{1,0:T(8,128)}, f32[8,256]{1,0:T(8,128)}, f32[2,8,256]{2,1,0:T(8,128)S(1)}) custom-call(s32[3]{0:T(128)S(1)} %copy-done.5, bf16[4,272,768]{2,1,0:T(8,128)(2,1)S(1)} %turn.1.ends_1, ...), custom_call_target="tpu_custom_call", output_to_operand_aliasing={{0}: (9, {}), {1}: (10, {})} | custom-call | flops 4294967296 | bytes 19226624 | tf_op jit(solution)/shard_map/moments/pallas_call | solution.py:473
  104.9 1.0 collective-permute-start.19
  105.9 0.4 collective-permute-start.20
  106.3 0.0 collective-permute-done.22.b1
  106.3 2.0 %collective-permute-start.21 = (f32[2,8,256]{2,1,0:T(8,128)S(1)}, f32[2,8,256]{2,1,0:T(8,128)S(1)}, u32[]{:S(2)}, u32[]{:S(2)}) collective-permute-start(f32[2,8,256]{2,1,0:T(8,128)S(1)} %get-tuple-element.42.s0), channel_id=1, source_target_pairs={{3,0},{0,1},{1,2},{2,3},{7,4},{4,5},{5,6},{6,7},{11,8},{8,9},{9,10... | collective-permute-start | bytes 49160 | tf_op jit(solution)/shard_map/ppermute | solution.py:459
  108.3 5.3 %collective-permute-done.23.b2 = bf16[256,1024]{1,0:T(8,128)(2,1)S(1)} collective-permute-done((bf16[256,1024]{1,0:T(8,128)(2,1)S(1)}, bf16[256,1024]{1,0:T(8,128)(2,1)S(1)}, u32[]{:S(2)}, u32[]{:S(2)}) %collective-permute-start.23) | collective-permute-done | bytes 524320 | tf_op jit(solution)/shard_map/ppermute | solution.py:459
  113.6 0.0 copy-start.13
  113.6 3.9 %last.1 = (bf16[256,1024]{1,0:T(8,128)(2,1)}, bf16[16,256]{1,0:T(8,128)(2,1)S(1)}) custom-call(s32[3]{0:T(128)S(1)} %copy-done.5, bf16[256,1024]{1,0:T(8,128)(2,1)S(1)} %bitcast.16, bf16[256,1024]{1,0:T(8,128)(2,1)S(1)} %collective-permute-done.g1.a1, bf16[256,1024]{1,0:T(8,128)(2,1)S(1)} %collective-permute-done.9.g2.a2, ...), custom_call_target="tpu_custom_call" | custom-call | flops 1073741824 | bytes 13902848 | tf_op jit(solution)/shard_map/last/pallas_call | solution.py:473
  117.5 0.0 collective-permute-done.20.s2
  117.6 0.0 collective-permute-done.21.s3
  117.6 1.3 %innovation.1 = (f32[8,4,128]{2,1,0:T(4,128)}, bf16[1,256]{1,0:T(2,128)(2,1)}, bf16[256,1024]{1,0:T(8,128)(2,1)}) custom-call(s32[3]{0:T(128)S(1)} %copy-done.5, s32[4,8]{1,0:T(4,128)S(1)} %bitcast.22, s32[8]{0:T(128)S(1)} %copy-done.13, f32[2,8,256]{2,1,0:T(8,128)S(1)} %get-tuple-element.42.s0, ...), custom_call_target="tpu_custom_call", output_to_operand_aliasing={{2}: (15, {})} | custom-call | bytes 200000 | tf_op jit(solution)/shard_map/innovation/pallas_call | solution.py:574
  (26 shorter events, 0.1 us)
Async XLA Ops:
  0.6 27.4 %copy-start = (bf16[1,256,1024]{2,1,0:T(8,128)(2,1)S(1)}, bf16[1,256,1024]{2,1,0:T(8,128)(2,1)}, u32[]{:S(2)}) copy-start(bf16[1,256,1024]{2,1,0:T(8,128)(2,1)} %param.12) | copy-start | bytes 1572868
  0.6 28.7 %collective-permute-start = (bf16[256,1024]{1,0:T(8,128)(2,1)}, bf16[256,1024]{1,0:T(8,128)(2,1)S(1)}, u32[]{:S(2)}, u32[]{:S(2)}) collective-permute-start(bf16[256,1024]{1,0:T(8,128)(2,1)} %bitcast.8), channel_id=1, source_target_pairs={{13,12},{14,13},{15,14},{12,15},{9,8},{10,9},{11,10},{8,11},{5,4},... | collective-permute-start | bytes 1572872 | tf_op jit(solution)/shard_map/ppermute | solution.py:459
  1.5 27.9 %collective-permute-start.1 = (bf16[256,1024]{1,0:T(8,128)(2,1)}, bf16[256,1024]{1,0:T(8,128)(2,1)S(1)}, u32[]{:S(2)}, u32[]{:S(2)}) collective-permute-start(bf16[256,1024]{1,0:T(8,128)(2,1)} %bitcast.9), channel_id=1, source_target_pairs={{14,12},{13,15},{10,8},{9,11},{4,5},{5,6},{6,7},{7,4},{30,28},{29,... | collective-permute-start | bytes 1572872 | tf_op jit(solution)/shard_map/ppermute | solution.py:459
  2.8 25.3 %copy-start.5 = (s32[3]{0:T(128)S(1)}, s32[3]{0:T(128)}, u32[]{:S(2)}) copy-start(s32[3]{0:T(128)} %pad_add_fusion.where) | copy-start | bytes 40
  2.8 26.6 %copy-start.1 = (bf16[1,256,1024]{2,1,0:T(8,128)(2,1)S(1)}, bf16[1,256,1024]{2,1,0:T(8,128)(2,1)}, u32[]{:S(2)}) copy-start(bf16[1,256,1024]{2,1,0:T(8,128)(2,1)} %param.14) | copy-start | bytes 1572868
  2.8 26.6 %copy-start.2 = (bf16[2,256,1024]{2,1,0:T(8,128)(2,1)S(1)}, bf16[2,256,1024]{2,1,0:T(8,128)(2,1)}, u32[]{:S(2)}) copy-start(bf16[2,256,1024]{2,1,0:T(8,128)(2,1)} %refs_0_.1) | copy-start | bytes 3145732
  2.8 26.6 %copy-start.7 = (f32[1,256]{1,0:T(1,128)S(1)}, f32[1,256]{1,0:T(1,128)}, u32[]{:S(2)}) copy-start(f32[1,256]{1,0:T(1,128)} %offset.9) | copy-start | bytes 3076
  2.8 26.6 %copy-start.11 = (bf16[2,256]{1,0:T(2,128)(2,1)S(1)}, bf16[2,256]{1,0:T(2,128)(2,1)}, u32[]{:S(2)}) copy-start(bf16[2,256]{1,0:T(2,128)(2,1)} %refs_1_.1) | copy-start | bytes 3076
  5.5 22.6 %collective-permute-start.3 = (bf16[272,768]{1,0:T(8,128)(2,1)}, bf16[272,768]{1,0:T(8,128)(2,1)S(1)}, u32[]{:S(2)}, u32[]{:S(2)}) collective-permute-start(bf16[272,768]{1,0:T(8,128)(2,1)} %pack.1.n0), channel_id=1, source_target_pairs={{2,12},{3,13},{0,14},{1,15},{6,4},{7,5},{4,6},{5,7},{18,28},{19,29... | collective-permute-start | bytes 1253384 | tf_op jit(solution)/shard_map/ppermute | solution.py:459
  17.6 11.7 %collective-permute-start.2 = (bf16[272,768]{1,0:T(8,128)(2,1)}, bf16[272,768]{1,0:T(8,128)(2,1)S(1)}, u32[]{:S(2)}, u32[]{:S(2)}) collective-permute-start(bf16[272,768]{1,0:T(8,128)(2,1)} %pack.1.n0), channel_id=1, source_target_pairs={{13,12},{14,13},{15,14},{12,15},{5,4},{6,5},{7,6},{4,7},{29,28},{3... | collective-permute-start | bytes 1253384 | tf_op jit(solution)/shard_map/ppermute | solution.py:459
  18.3 11.0 %collective-permute-start.4 = (bf16[272,768]{1,0:T(8,128)(2,1)}, bf16[272,768]{1,0:T(8,128)(2,1)S(1)}, u32[]{:S(2)}, u32[]{:S(2)}) collective-permute-start(bf16[272,768]{1,0:T(8,128)(2,1)} %pack.1.n0), channel_id=1, source_target_pairs={{15,12},{12,13},{13,14},{14,15},{7,4},{4,5},{5,6},{6,7},{31,28},{2... | collective-permute-start | bytes 1253384 | tf_op jit(solution)/shard_map/ppermute | solution.py:459
  28.6 4.8 %collective-permute-start.9 = (bf16[256,1024]{1,0:T(8,128)(2,1)S(1)}, bf16[256,1024]{1,0:T(8,128)(2,1)S(1)}, u32[]{:S(2)}, u32[]{:S(2)}) collective-permute-start(bf16[256,1024]{1,0:T(8,128)(2,1)S(1)} %hand_1.1), channel_id=1, source_target_pairs={{4,6},{5,7},{6,4},{7,5},{20,22},{21,23},{22,20},{23,21}} | collective-permute-start | bytes 1572872 | tf_op jit(solution)/shard_map/ppermute | solution.py:459
  30.0 2.8 %collective-permute-start.5 = (bf16[272,768]{1,0:T(8,128)(2,1)S(1)}, bf16[272,768]{1,0:T(8,128)(2,1)S(1)}, u32[]{:S(2)}, u32[]{:S(2)}) collective-permute-start(bf16[272,768]{1,0:T(8,128)(2,1)S(1)} %get-tuple-element.30.refs_4_), channel_id=1, source_target_pairs={{12,8},{13,9},{14,10},{15,11},{28,24},{29,25},{30,26},{31,27}} | collective-permute-start | bytes 1253384 | tf_op jit(solution)/shard_map/ppermute | solution.py:459
  30.7 2.1 %collective-permute-start.6 = (bf16[272,768]{1,0:T(8,128)(2,1)S(1)}, bf16[272,768]{1,0:T(8,128)(2,1)S(1)}, u32[]{:S(2)}, u32[]{:S(2)}) collective-permute-start(bf16[272,768]{1,0:T(8,128)(2,1)S(1)} %get-tuple-element.30.refs_4_), channel_id=1, source_target_pairs={{13,8},{14,9},{15,10},{12,11},{29,24},{30,25},{31,26},{28,27}} | collective-permute-start | bytes 1253384 | tf_op jit(solution)/shard_map/ppermute | solution.py:459
  31.4 1.4 %collective-permute-start.7 = (bf16[272,768]{1,0:T(8,128)(2,1)S(1)}, bf16[272,768]{1,0:T(8,128)(2,1)S(1)}, u32[]{:S(2)}, u32[]{:S(2)}) collective-permute-start(bf16[272,768]{1,0:T(8,128)(2,1)S(1)} %get-tuple-element.30.refs_4_), channel_id=1, source_target_pairs={{14,8},{15,9},{12,10},{13,11},{30,24},{31,25},{28,26},{29,27}} | collective-permute-start | bytes 1253384 | tf_op jit(solution)/shard_map/ppermute | solution.py:459
  32.1 0.7 collective-permute-start.8
  32.8 1.0 copy-start.4
  34.4 35.0 %copy-start.3 = (bf16[8,256,1024]{2,1,0:T(8,128)(2,1)S(1)}, bf16[8,256,1024]{2,1,0:T(8,128)(2,1)}, u32[]{:S(2)}) copy-start(bf16[8,256,1024]{2,1,0:T(8,128)(2,1)} %gain.1) | copy-start | bytes 12582916
  34.4 34.4 %collective-permute-start.10 = (bf16[2064,1024]{1,0:T(8,128)(2,1)S(1)}, bf16[2064,1024]{1,0:T(8,128)(2,1)S(1)}, u32[]{:S(2)}, u32[]{:S(2)}) collective-permute-start(bf16[2064,1024]{1,0:T(8,128)(2,1)S(1)} %stack.17), channel_id=1, source_target_pairs={{4,0},{5,1},{6,2},{7,3},{20,16},{21,17},{22,18},{23,19}} | collective-permute-start | bytes 12681224 | tf_op jit(solution)/shard_map/ppermute | solution.py:459
  35.9 2.8 %collective-permute-start.15 = (bf16[272,768]{1,0:T(8,128)(2,1)S(1)}, bf16[272,768]{1,0:T(8,128)(2,1)S(1)}, u32[]{:S(2)}, u32[]{:S(2)}) collective-permute-start(bf16[272,768]{1,0:T(8,128)(2,1)S(1)} %get-tuple-element.33.event.own), channel_id=1, source_target_pairs={{10,4},{11,5},{8,6},{9,7},{26,20},{27,21},{24,22},{25,23}} | collective-permute-start | bytes 1253384 | tf_op jit(solution)/shard_map/ppermute | solution.py:459
  36.6 46.1 %collective-permute-start.13 = (bf16[272,768]{1,0:T(8,128)(2,1)S(1)}, bf16[272,768]{1,0:T(8,128)(2,1)S(1)}, u32[]{:S(2)}, u32[]{:S(2)}) collective-permute-start(bf16[272,768]{1,0:T(8,128)(2,1)S(1)} %get-tuple-element.33.event.own), channel_id=1, source_target_pairs={{8,4},{9,5},{10,6},{11,7},{24,20},{25,21},{26,22},{27,23}} | collective-permute-start | bytes 1253384 | tf_op jit(solution)/shard_map/ppermute | solution.py:459
  37.3 46.1 %collective-permute-start.14 = (bf16[272,768]{1,0:T(8,128)(2,1)S(1)}, bf16[272,768]{1,0:T(8,128)(2,1)S(1)}, u32[]{:S(2)}, u32[]{:S(2)}) collective-permute-start(bf16[272,768]{1,0:T(8,128)(2,1)S(1)} %get-tuple-element.33.event.own), channel_id=1, source_target_pairs={{9,4},{10,5},{11,6},{8,7},{25,20},{26,21},{27,22},{24,23}} | collective-permute-start | bytes 1253384 | tf_op jit(solution)/shard_map/ppermute | solution.py:459
  38.0 45.4 %collective-permute-start.16 = (bf16[272,768]{1,0:T(8,128)(2,1)S(1)}, bf16[272,768]{1,0:T(8,128)(2,1)S(1)}, u32[]{:S(2)}, u32[]{:S(2)}) collective-permute-start(bf16[272,768]{1,0:T(8,128)(2,1)S(1)} %get-tuple-element.33.event.own), channel_id=1, source_target_pairs={{8,5},{9,6},{10,7},{24,21},{25,22},{26,23}} | collective-permute-start | bytes 1253384 | tf_op jit(solution)/shard_map/ppermute | solution.py:459
  38.7 44.7 %collective-permute-start.17 = (bf16[272,768]{1,0:T(8,128)(2,1)S(1)}, bf16[272,768]{1,0:T(8,128)(2,1)S(1)}, u32[]{:S(2)}, u32[]{:S(2)}) collective-permute-start(bf16[272,768]{1,0:T(8,128)(2,1)S(1)} %collective-permute-done.15.t2), channel_id=1, source_target_pairs={{5,4},{21,20}} | collective-permute-start | bytes 1253384 | tf_op jit(solution)/shard_map/ppermute | solution.py:459
  82.0 1.4 %collective-permute-start.11 = (bf16[256,256]{1,0:T(8,128)(2,1)S(1)}, bf16[256,256]{1,0:T(8,128)(2,1)S(1)}, u32[]{:S(2)}, u32[]{:S(2)}) collective-permute-start(bf16[256,256]{1,0:T(8,128)(2,1)S(1)} %get-tuple-element.36), channel_id=1, source_target_pairs={{12,13},{13,14},{14,15},{15,12},{8,9},{9,10},{10,11},{11,8},{28,29... | collective-permute-start | bytes 393224 | tf_op jit(solution)/shard_map/ppermute | solution.py:459
  82.7 16.0 %copy-start.8 = (f32[8,256]{1,0:T(8,128)S(1)}, f32[8,256]{1,0:T(8,128)}, u32[]{:S(2)}) copy-start(f32[8,256]{1,0:T(8,128)} %offset.8) | copy-start | bytes 24580
  82.7 16.0 %copy-start.9 = (f32[8,256]{1,0:T(8,128)S(1)}, f32[8,256]{1,0:T(8,128)}, u32[]{:S(2)}) copy-start(f32[8,256]{1,0:T(8,128)} %var.1) | copy-start | bytes 24580
  82.7 0.7 collective-permute-start.12
  84.0 14.7 %collective-permute-start.18 = (bf16[4,272,768]{2,1,0:T(8,128)(2,1)S(1)}, bf16[4,272,768]{2,1,0:T(8,128)(2,1)S(1)}, u32[]{:S(2)}, u32[]{:S(2)}) collective-permute-start(bf16[4,272,768]{2,1,0:T(8,128)(2,1)S(1)} %turn.1.ends_1), channel_id=1, source_target_pairs={{4,0},{5,1},{6,2},{7,3},{20,16},{21,17},{22,18},{23,19}} | collective-permute-start | bytes 5013512 | tf_op jit(solution)/shard_map/ppermute | solution.py:459
  85.3 21.0 %collective-permute-start.22 = (bf16[256,1024]{1,0:T(8,128)(2,1)S(1)}, bf16[256,1024]{1,0:T(8,128)(2,1)S(1)}, u32[]{:S(2)}, u32[]{:S(2)}) collective-permute-start(bf16[256,1024]{1,0:T(8,128)(2,1)S(1)} %hand_0.1.event), channel_id=1, source_target_pairs={{1,0},{2,1},{3,2},{0,3},{17,16},{18,17},{19,18},{16,19}} | collective-permute-start | bytes 1572872 | tf_op jit(solution)/shard_map/ppermute | solution.py:459
  89.3 24.3 %collective-permute-start.23 = (bf16[256,1024]{1,0:T(8,128)(2,1)S(1)}, bf16[256,1024]{1,0:T(8,128)(2,1)S(1)}, u32[]{:S(2)}, u32[]{:S(2)}) collective-permute-start(bf16[256,1024]{1,0:T(8,128)(2,1)S(1)} %hand_0.1.event), channel_id=1, source_target_pairs={{0,2},{1,3},{2,0},{3,1},{16,18},{17,19},{18,16},{19,17}} | collective-permute-start | bytes 1572872 | tf_op jit(solution)/shard_map/ppermute | solution.py:459
  91.3 22.3 %collective-permute-start.24 = (bf16[256,1024]{1,0:T(8,128)(2,1)S(1)}, bf16[256,1024]{1,0:T(8,128)(2,1)S(1)}, u32[]{:S(2)}, u32[]{:S(2)}) collective-permute-start(bf16[256,1024]{1,0:T(8,128)(2,1)S(1)} %hand_0.1.event), channel_id=1, source_target_pairs={{0,1},{1,2},{2,3},{3,0},{16,17},{17,18},{18,19},{19,16}} | collective-permute-start | bytes 1572872 | tf_op jit(solution)/shard_map/ppermute | solution.py:459
  104.9 12.6 %collective-permute-start.19 = (f32[2,8,256]{2,1,0:T(8,128)S(1)}, f32[2,8,256]{2,1,0:T(8,128)S(1)}, u32[]{:S(2)}, u32[]{:S(2)}) collective-permute-start(f32[2,8,256]{2,1,0:T(8,128)S(1)} %get-tuple-element.42.s0), channel_id=1, source_target_pairs={{1,0},{2,1},{3,2},{0,3},{5,4},{6,5},{7,6},{4,7},{9,8},{10,9},{11,1... | collective-permute-start | bytes 49160 | tf_op jit(solution)/shard_map/ppermute | solution.py:459
  105.9 11.7 %collective-permute-start.20 = (f32[2,8,256]{2,1,0:T(8,128)S(1)}, f32[2,8,256]{2,1,0:T(8,128)S(1)}, u32[]{:S(2)}, u32[]{:S(2)}) collective-permute-start(f32[2,8,256]{2,1,0:T(8,128)S(1)} %get-tuple-element.42.s0), channel_id=1, source_target_pairs={{2,0},{3,1},{0,2},{1,3},{6,4},{7,5},{4,6},{5,7},{10,8},{11,9},{8,1... | collective-permute-start | bytes 49160 | tf_op jit(solution)/shard_map/ppermute | solution.py:459
  106.3 11.2 %collective-permute-start.21 = (f32[2,8,256]{2,1,0:T(8,128)S(1)}, f32[2,8,256]{2,1,0:T(8,128)S(1)}, u32[]{:S(2)}, u32[]{:S(2)}) collective-permute-start(f32[2,8,256]{2,1,0:T(8,128)S(1)} %get-tuple-element.42.s0), channel_id=1, source_target_pairs={{3,0},{0,1},{1,2},{2,3},{7,4},{4,5},{5,6},{6,7},{11,8},{8,9},{9,10... | collective-permute-start | bytes 49160 | tf_op jit(solution)/shard_map/ppermute | solution.py:459
  113.6 4.0 %copy-start.6 = (f32[8,4,128]{2,1,0:T(4,128)S(1)}, f32[8,4,128]{2,1,0:T(4,128)}, u32[]{:S(2)}) copy-start(f32[8,4,128]{2,1,0:T(4,128)} %value.1) | copy-start | bytes 49156
  113.6 4.0 %copy-start.10 = (f32[1024]{0:T(1024)S(1)}, f32[1024]{0:T(1024)}, u32[]{:S(2)}) copy-start(f32[1024]{0:T(1024)} %param.23) | copy-start | bytes 12292
  113.6 4.0 %copy-start.12 = (s32[8,4]{0,1:T(4,128)S(1)}, s32[8,4]{0,1:T(4,128)}, u32[]{:S(2)}) copy-start(s32[8,4]{0,1:T(4,128)} %param.20) | copy-start | bytes 388
  113.6 4.0 %copy-start.13 = (s32[8]{0:T(128)S(1)}, s32[8]{0:T(128)}, u32[]{:S(2)}) copy-start(s32[8]{0:T(128)} %counts.1) | copy-start | bytes 100

commit v4 on v3

--- a/solution.py
+++ b/solution.py
@@ -309,7 +309,7 @@
             base[pl.ds(k, 1), :] = row_sums(value)
             return carry
 
-        lax.fori_loop(0, step_gain.shape[0], one, 0)
+        lax.fori_loop(0, step_gain.shape[0], one, 0, unroll=4)
 
 
 def row_sums(value):
@@ -362,31 +362,37 @@
         steps(gain, None)
 
 
-def last_kernel(where, g0, a1, a2, a3, b1, b2, b3, ends_1, ends_0, lift, through, beside, noise, offset, means, rows, mean_row, full, mean):
+def last_kernel(where, g0, a1, a2, a3, ends_1, ends_0, lift, through, beside, noise, offset, means, rows, mean_row, product, full, mean):
     z, seg = where[0], where[1]
     states = g0.shape[1]
-
-    def finish(product, gains):
-        for a, gain in enumerate(gains):
-            column = cols(spot(z, a))
-            rows[:, column] = (dot_nt(product, gain[...]) + noise[:, column].astype(F32)).astype(BF16)
-        mean_row[...] = (dot_nt(means[...], g0[...]) + offset[...]).astype(BF16)
+    mean_row[...] = (dot_nt(means[...], g0[...]) + offset[...]).astype(BF16)
 
     @pl.when(seg == 0)
     def _():
         lay_out(z, [ends_0.at[a] for a in range(RING)], full, mean)
-        product = dot(through[...], full[...]).astype(BF16)
-        finish((dot_nt(product, lift[:states, :]) + beside[...]).astype(BF16), (g0, b1, b2, b3))
+        half_way = dot(through[...], full[...]).astype(BF16)
+        product[...] = (dot_nt(half_way, lift[:states, :]) + beside[...]).astype(BF16)
 
     @pl.when(seg == 1)
     def _():
         lay_out(z, [ends_1.at[a] for a in range(RING)], full, mean)
-        finish(dot(g0[...], full[...]).astype(BF16), (g0, a1, a2, a3))
-
-
-def innovation_kernel(where, tiles, counts, s0, s1, s2, s3, value, noise, own, far, near, mean_1, mean_2, mean_3, _, out, mean_row, rows_out, full, rows, sem):
+        finish(z, dot(g0[...], full[...]).astype(BF16), (g0, a1, a2, a3), noise, rows)
+
+
+def finish(z, product, gains, noise, rows):
+    for a, gain in enumerate(gains):
+        column = cols(spot(z, a))
+        rows[:, column] = (dot_nt(product, gain[...]) + noise[:, column].astype(F32)).astype(BF16)
+
+
+def innovation_kernel(where, tiles, counts, s0, s1, s2, s3, value, noise, own, far, near, mean_1, mean_2, mean_3, product, g0, b1, b2, b3, cov_noise, _, out, mean_row, rows_out, full, rows, sem):
     z, seg = where[0], where[1]
     copy = pltpu.make_async_copy(rows, rows_out, sem)
+
+    @pl.when(seg == 0)
+    def _():
+        finish(z, product[...], (g0, b1, b2, b3), cov_noise, rows)
+        copy.start()
 
     @pl.when(seg > 1)
     def _():
@@ -417,7 +423,7 @@
             result = (value[k, j : j + 1, :] - full[0, k : k + 1, at]) / full[1, k : k + 1, at]
             out[k, j : j + 1, :] = jnp.where(j < counts[k], result, 0.0)
 
-    @pl.when(seg > 1)
+    @pl.when(seg != 1)
     def _():
         copy.wait()
 
@@ -563,25 +569,25 @@
     )
     everyone = tuple((s, s) for s in range(GROUP_SEGS))
     all_stats = [stats] + [send(stats, everyone, a) for a in range(1, RING)]
-    rows, mean_1 = call(
+    rows, mean_1, product = call(
         last_kernel,
         "last",
-        (row_shape, mean_shape),
-        (gain, *gains_1, *gains_0, ends_1, ends_0, lift, through, beside, noise, seg_offset, means),
+        (row_shape, mean_shape, row_shape),
+        (gain, *gains_1, ends_1, ends_0, lift, through, beside, noise, seg_offset, means),
         full_and_mean,
         flops,
     )
     innovation, out_mean, out_cov = pl.pallas_call(
         innovation_kernel,
         out_shape=(shape(obs_value.shape, F32), shape((1, BLOCK)), row_shape),
-        in_specs=[smem()] * 3 + [vmem()] * 12 + [pl.BlockSpec(memory_space=pl.ANY)],
+        in_specs=[smem()] * 3 + [vmem()] * 18 + [pl.BlockSpec(memory_space=pl.ANY)],
         out_specs=(vmem(), vmem(), pl.BlockSpec(memory_space=pl.ANY)),
         scratch_shapes=[pltpu.VMEM((2, steps, states), F32), pltpu.VMEM(row_shape.shape, BF16), pltpu.SemaphoreType.DMA],
-        input_output_aliases={15: 2},
+        input_output_aliases={21: 2},
         compiler_params=params(),
         cost_estimate=cost(0, 2e5),
         name="innovation",
-    )(where, obs_tiles.T, obs_count, *all_stats, obs_value, obs_noise.reshape(1, states), parcel_2, far, near, mean_1, mean_2, mean_3, rows)
+    )(where, obs_tiles.T, obs_count, *all_stats, obs_value, obs_noise.reshape(1, states), parcel_2, far, near, mean_1, mean_2, mean_3, product, gain, *gains_0, noise, rows)
     return out_cov[None], out_mean, step_mean, step_spread, innovation
 
 

time: 120 us -> 117 us (0.975)
  starting transfers between devices: 38 us -> 36.6 us
    pallas_call x7, Pallas kernels: 25 us -> 22.8 us  [call(): pl.pallas_call(kernel, out_shape=out_shape, in_specs=[smem()] + [vmem()]...]
    pallas_call x1, Pallas kernels: 1.31 us -> 2.76 us  [ring_shards(): pl.pallas_call(innovation_kernel, out_shape=(shape(obs_value.shape, F32),...]
    ppermute x25, starting transfers between devices: 38 us -> 36.6 us  [route(): return lax.ppermute(block, ('tm', 'tile'), table)]
  transfers between devices with their start and end apart: 25 -> 25, of which waited for: 4 -> 4; matrix products, arithmetic and copies ran while one was open for 0% -> 1% of each run, Pallas kernels for 23% -> 22%
where the time goes in v4:
time: 117 us
  waiting for transfers between devices  48.6 us (42%)
  starting transfers between devices  36.6 us (31%)
  Pallas kernels  29.4 us (25%)
  between operations  1.3 us (1%)
    ppermute x25, waiting for transfers between devices, route(): return lax.ppermute(block, ('tm', 'tile'), table)  48.6 us
    ppermute x25, starting transfers between devices, route(): return lax.ppermute(block, ('tm', 'tile'), table)  36.6 us
    pallas_call x7, Pallas kernels, call(): pl.pallas_call(kernel, out_shape=out_shape, in_specs=[smem()] + [vmem()]...  22.8 us
    pallas_call x3, Pallas kernels, pack(): pl.pallas_call(kernel, out_shape=out_shape, in_specs=[smem()] + [pl.Block...  3.8 us
    pallas_call x1, Pallas kernels, ring_shards(): pl.pallas_call(innovation_kernel, out_shape=(shape(obs_value.shape, F32),...  2.76 us
  transfers between devices with their start and end apart: 25, of which 4 were waited for; matrix products, arithmetic and copies ran while one was open for 1% of the time, Pallas kernels for 22%

profile of v4, /device:TPU:0, one launch (start us, length us, event | category | flops | bytes accessed | tf_op | source)
XLA Modules:
  0.0 116.9 jit_solution(16438608836029332446)
XLA Ops:
  0.6 0.8 collective-permute-start
  1.5 0.7 collective-permute-start.1
  2.2 0.6 pad_add_fusion.where
  2.8 0.0 copy-start.11
  2.8 2.7 %pack.1.n0 = bf16[272,768]{1,0:T(8,128)(2,1)} custom-call(s32[3]{0:T(128)} %pad_add_fusion.where, bf16[2,256,1024]{2,1,0:T(8,128)(2,1)} %refs_0_.1, bf16[256,1024]{1,0:T(8,128)(2,1)} %bitcast.18, bf16[2,256]{1,0:T(2,128)(2,1)} %refs_1_.1, f32[1,256]{1,0:T(1,128)} %offset.9), custom_call_target="tpu_custom_call" | custom-call | bytes 1000000 | tf_op jit(solution)/shard_map/pack/pallas_call | solution.py:492
  5.5 12.2 %collective-permute-start.3 = (bf16[272,768]{1,0:T(8,128)(2,1)}, bf16[272,768]{1,0:T(8,128)(2,1)S(1)}, u32[]{:S(2)}, u32[]{:S(2)}) collective-permute-start(bf16[272,768]{1,0:T(8,128)(2,1)} %pack.1.n0), channel_id=1, source_target_pairs={{2,12},{3,13},{0,14},{1,15},{6,4},{7,5},{4,6},{5,7},{18,28},{19,29... | collective-permute-start | bytes 1253384 | tf_op jit(solution)/shard_map/ppermute | solution.py:465
  17.6 0.7 collective-permute-start.2
  18.3 0.7 collective-permute-start.4
  19.0 9.0 %collective-permute-done.3.refs_3_.event.n2 = bf16[272,768]{1,0:T(8,128)(2,1)S(1)} collective-permute-done((bf16[272,768]{1,0:T(8,128)(2,1)}, bf16[272,768]{1,0:T(8,128)(2,1)S(1)}, u32[]{:S(2)}, u32[]{:S(2)}) %collective-permute-start.3) | collective-permute-done | bytes 417824 | tf_op jit(solution)/shard_map/ppermute | solution.py:465
  28.1 0.6 hand_1.1
  28.6 0.7 collective-permute-start.9
  29.3 0.0 collective-permute-done.2.refs_2_.n1
  29.3 0.0 collective-permute-done.4.refs_4_.n3
  29.3 0.0 collective-permute-done.g1.a1
  29.4 0.0 collective-permute-done.1.g2.g3.a3
  29.4 0.6 pairs_3.1
  30.0 0.7 collective-permute-start.5
  30.7 0.7 collective-permute-start.6
  31.4 0.7 collective-permute-start.7
  32.1 0.7 collective-permute-start.8
  32.8 0.0 collective-permute-done.5.refs_0_
  32.8 0.0 collective-permute-done.6.refs_1_
  32.8 0.0 collective-permute-done.7.refs_2_
  32.8 0.0 collective-permute-done.8.refs_3_
  32.8 0.0 copy-start.4
  32.8 0.6 pairs_2.1
  33.4 0.0 collective-permute-done.9.g2.a2
  33.4 0.4 copy-done.4
  33.8 0.5 stack.17
  34.4 0.0 copy-start.3
  34.4 1.6 %collective-permute-start.10 = (bf16[2064,1024]{1,0:T(8,128)(2,1)S(1)}, bf16[2064,1024]{1,0:T(8,128)(2,1)S(1)}, u32[]{:S(2)}, u32[]{:S(2)}) collective-permute-start(bf16[2064,1024]{1,0:T(8,128)(2,1)S(1)} %stack.17), channel_id=1, source_target_pairs={{4,0},{5,1},{6,2},{7,3},{20,16},{21,17},{22,18},{23,19}} | collective-permute-start | bytes 12681224 | tf_op jit(solution)/shard_map/ppermute | solution.py:465
  35.9 0.7 collective-permute-start.15
  36.6 0.7 collective-permute-start.13
  37.3 0.7 collective-permute-start.14
  38.0 0.7 collective-permute-start.16
  38.7 0.0 collective-permute-done.15.t2
  38.7 0.7 collective-permute-start.17
  39.4 29.3 %collective-permute-done.10.event.lift = bf16[2064,1024]{1,0:T(8,128)(2,1)S(1)} collective-permute-done((bf16[2064,1024]{1,0:T(8,128)(2,1)S(1)}, bf16[2064,1024]{1,0:T(8,128)(2,1)S(1)}, u32[]{:S(2)}, u32[]{:S(2)}) %collective-permute-start.10) | collective-permute-done | bytes 4227104 | tf_op jit(solution)/shard_map/ppermute | solution.py:465
  68.8 0.6 hand_0.1.event
  69.4 11.0 %ahead.1 = (bf16[8,256,1024]{2,1,0:T(8,128)(2,1)S(1)}, f32[8,256]{1,0:T(8,128)S(1)}, bf16[256,1024]{1,0:T(8,128)(2,1)S(1)}, f32[256,1024]{1,0:T(8,128)S(1)}, bf1...) custom-call(s32[3]{0:T(128)S(1)} %copy-done.5, bf16[256,1024]{1,0:T(8,128)(2,1)S(1)} %hand_0.1.event, ...), custom_call_target="tpu_custom_call" | custom-call | flops 9663676416 | bytes 15769600 | tf_op jit(solution)/shard_map/ahead/pallas_call | solution.py:479
  80.4 0.7 collective-permute-start.11
  81.0 0.0 collective-permute-done.13.t0
  81.0 0.0 copy-start.8
  81.0 0.0 copy-start.9
  81.1 0.7 collective-permute-start.12
  81.7 0.0 collective-permute-done.14.t1
  81.7 0.0 collective-permute-done.16.t3
  81.8 0.0 collective-permute-done.17.t4
  81.8 0.0 collective-permute-done.12.far
  81.8 0.6 turn.1.ends_1
  82.4 1.3 %collective-permute-start.18 = (bf16[4,272,768]{2,1,0:T(8,128)(2,1)S(1)}, bf16[4,272,768]{2,1,0:T(8,128)(2,1)S(1)}, u32[]{:S(2)}, u32[]{:S(2)}) collective-permute-start(bf16[4,272,768]{2,1,0:T(8,128)(2,1)S(1)} %turn.1.ends_1), channel_id=1, source_target_pairs={{4,0},{5,1},{6,2},{7,3},{20,16},{21,17},{22,18},{23,19}} | collective-permute-start | bytes 5013512 | tf_op jit(solution)/shard_map/ppermute | solution.py:465
  83.7 4.0 %collective-permute-start.22 = (bf16[256,1024]{1,0:T(8,128)(2,1)S(1)}, bf16[256,1024]{1,0:T(8,128)(2,1)S(1)}, u32[]{:S(2)}, u32[]{:S(2)}) collective-permute-start(bf16[256,1024]{1,0:T(8,128)(2,1)S(1)} %hand_0.1.event), channel_id=1, source_target_pairs={{1,0},{2,1},{3,2},{0,3},{17,16},{18,17},{19,18},{16,19}} | collective-permute-start | bytes 1572872 | tf_op jit(solution)/shard_map/ppermute | solution.py:465
  87.7 1.9 %collective-permute-start.23 = (bf16[256,1024]{1,0:T(8,128)(2,1)S(1)}, bf16[256,1024]{1,0:T(8,128)(2,1)S(1)}, u32[]{:S(2)}, u32[]{:S(2)}) collective-permute-start(bf16[256,1024]{1,0:T(8,128)(2,1)S(1)} %hand_0.1.event), channel_id=1, source_target_pairs={{0,2},{1,3},{2,0},{3,1},{16,18},{17,19},{18,16},{19,17}} | collective-permute-start | bytes 1572872 | tf_op jit(solution)/shard_map/ppermute | solution.py:465
  89.6 2.5 %collective-permute-start.24 = (bf16[256,1024]{1,0:T(8,128)(2,1)S(1)}, bf16[256,1024]{1,0:T(8,128)(2,1)S(1)}, u32[]{:S(2)}, u32[]{:S(2)}) collective-permute-start(bf16[256,1024]{1,0:T(8,128)(2,1)S(1)} %hand_0.1.event), channel_id=1, source_target_pairs={{0,1},{1,2},{2,3},{3,0},{16,17},{17,18},{18,19},{19,16}} | collective-permute-start | bytes 1572872 | tf_op jit(solution)/shard_map/ppermute | solution.py:465
  92.1 9.2 %collective-permute-done.18.ends_0 = bf16[4,272,768]{2,1,0:T(8,128)(2,1)S(1)} collective-permute-done((bf16[4,272,768]{2,1,0:T(8,128)(2,1)S(1)}, bf16[4,272,768]{2,1,0:T(8,128)(2,1)S(1)}, u32[]{:S(2)}, u32[]{:S(2)}) %collective-permute-start.18) | collective-permute-done | bytes 1671200 | tf_op jit(solution)/shard_map/ppermute | solution.py:465
  101.3 6.1 %moments.1 = (bf16[4,768,256]{2,1,0:T(8,128)(2,1)S(1)}, bf16[16,1024]{1,0:T(8,128)(2,1)S(1)}, f32[8,256]{1,0:T(8,128)}, f32[8,256]{1,0:T(8,128)}, f32[2,8,256]{2,1,0:T(8,128)S(1)}) custom-call(s32[3]{0:T(128)S(1)} %copy-done.5, bf16[4,272,768]{2,1,0:T(8,128)(2,1)S(1)} %turn.1.ends_1, ...), custom_call_target="tpu_custom_call", output_to_operand_aliasing={{0}: (9, {}), {1}: (10, {})} | custom-call | flops 4294967296 | bytes 19226624 | tf_op jit(solution)/shard_map/moments/pallas_call | solution.py:479
  107.4 0.0 collective-permute-start.19
  107.4 1.0 collective-permute-start.20
  108.4 0.0 collective-permute-done.22.b1
  108.4 1.0 collective-permute-start.21
  109.4 3.5 %last.1 = (bf16[256,1024]{1,0:T(8,128)(2,1)}, bf16[16,256]{1,0:T(8,128)(2,1)S(1)}, bf16[256,1024]{1,0:T(8,128)(2,1)S(1)}) custom-call(s32[3]{0:T(128)S(1)} %copy-done.5, bf16[256,1024]{1,0:T(8,128)(2,1)S(1)} %bitcast.16, bf16[256,1024]{1,0:T(8,128)(2,1)S(1)} %collective-permute-done.g1.a1, bf16[256,1024]{1,0:T(8,128)(2,1)S(1)} %collective-permute-done.9.g2.a2, ...), custom_call_target="tpu_custom_call" | custom-call | flops 1073741824 | bytes 12854272 | tf_op jit(solution)/shard_map/last/pallas_call | solution.py:479
  112.9 0.0 collective-permute-done.20.s2
  112.9 1.0 collective-permute-done.21.s3
  113.9 2.8 %innovation.1 = (f32[8,4,128]{2,1,0:T(4,128)}, bf16[1,256]{1,0:T(2,128)(2,1)}, bf16[256,1024]{1,0:T(8,128)(2,1)}) custom-call(s32[3]{0:T(128)S(1)} %copy-done.5, s32[4,8]{1,0:T(4,128)S(1)} %bitcast.24, s32[8]{0:T(128)S(1)} %copy-done.13, f32[2,8,256]{2,1,0:T(8,128)S(1)} %get-tuple-element.43.s0, ...), custom_call_target="tpu_custom_call", output_to_operand_aliasing={{2}: (21, {})} | custom-call | bytes 200000 | tf_op jit(solution)/shard_map/innovation/pallas_call | solution.py:580
  (26 shorter events, 0.1 us)
Async XLA Ops:
  0.6 27.4 %copy-start = (bf16[1,256,1024]{2,1,0:T(8,128)(2,1)S(1)}, bf16[1,256,1024]{2,1,0:T(8,128)(2,1)}, u32[]{:S(2)}) copy-start(bf16[1,256,1024]{2,1,0:T(8,128)(2,1)} %param.12) | copy-start | bytes 1572868
  0.6 28.7 %collective-permute-start = (bf16[256,1024]{1,0:T(8,128)(2,1)}, bf16[256,1024]{1,0:T(8,128)(2,1)S(1)}, u32[]{:S(2)}, u32[]{:S(2)}) collective-permute-start(bf16[256,1024]{1,0:T(8,128)(2,1)} %bitcast.8), channel_id=1, source_target_pairs={{13,12},{14,13},{15,14},{12,15},{9,8},{10,9},{11,10},{8,11},{5,4},... | collective-permute-start | bytes 1572872 | tf_op jit(solution)/shard_map/ppermute | solution.py:465
  1.5 27.9 %collective-permute-start.1 = (bf16[256,1024]{1,0:T(8,128)(2,1)}, bf16[256,1024]{1,0:T(8,128)(2,1)S(1)}, u32[]{:S(2)}, u32[]{:S(2)}) collective-permute-start(bf16[256,1024]{1,0:T(8,128)(2,1)} %bitcast.9), channel_id=1, source_target_pairs={{14,12},{13,15},{10,8},{9,11},{4,5},{5,6},{6,7},{7,4},{30,28},{29,... | collective-permute-start | bytes 1572872 | tf_op jit(solution)/shard_map/ppermute | solution.py:465
  2.8 25.3 %copy-start.5 = (s32[3]{0:T(128)S(1)}, s32[3]{0:T(128)}, u32[]{:S(2)}) copy-start(s32[3]{0:T(128)} %pad_add_fusion.where) | copy-start | bytes 40
  2.8 26.6 %copy-start.1 = (bf16[1,256,1024]{2,1,0:T(8,128)(2,1)S(1)}, bf16[1,256,1024]{2,1,0:T(8,128)(2,1)}, u32[]{:S(2)}) copy-start(bf16[1,256,1024]{2,1,0:T(8,128)(2,1)} %param.14) | copy-start | bytes 1572868
  2.8 26.6 %copy-start.2 = (bf16[2,256,1024]{2,1,0:T(8,128)(2,1)S(1)}, bf16[2,256,1024]{2,1,0:T(8,128)(2,1)}, u32[]{:S(2)}) copy-start(bf16[2,256,1024]{2,1,0:T(8,128)(2,1)} %refs_0_.1) | copy-start | bytes 3145732
  2.8 26.6 %copy-start.7 = (f32[1,256]{1,0:T(1,128)S(1)}, f32[1,256]{1,0:T(1,128)}, u32[]{:S(2)}) copy-start(f32[1,256]{1,0:T(1,128)} %offset.9) | copy-start | bytes 3076
  2.8 26.6 %copy-start.11 = (bf16[2,256]{1,0:T(2,128)(2,1)S(1)}, bf16[2,256]{1,0:T(2,128)(2,1)}, u32[]{:S(2)}) copy-start(bf16[2,256]{1,0:T(2,128)(2,1)} %refs_1_.1) | copy-start | bytes 3076
  5.5 22.6 %collective-permute-start.3 = (bf16[272,768]{1,0:T(8,128)(2,1)}, bf16[272,768]{1,0:T(8,128)(2,1)S(1)}, u32[]{:S(2)}, u32[]{:S(2)}) collective-permute-start(bf16[272,768]{1,0:T(8,128)(2,1)} %pack.1.n0), channel_id=1, source_target_pairs={{2,12},{3,13},{0,14},{1,15},{6,4},{7,5},{4,6},{5,7},{18,28},{19,29... | collective-permute-start | bytes 1253384 | tf_op jit(solution)/shard_map/ppermute | solution.py:465
  17.6 11.7 %collective-permute-start.2 = (bf16[272,768]{1,0:T(8,128)(2,1)}, bf16[272,768]{1,0:T(8,128)(2,1)S(1)}, u32[]{:S(2)}, u32[]{:S(2)}) collective-permute-start(bf16[272,768]{1,0:T(8,128)(2,1)} %pack.1.n0), channel_id=1, source_target_pairs={{13,12},{14,13},{15,14},{12,15},{5,4},{6,5},{7,6},{4,7},{29,28},{3... | collective-permute-start | bytes 1253384 | tf_op jit(solution)/shard_map/ppermute | solution.py:465
  18.3 11.0 %collective-permute-start.4 = (bf16[272,768]{1,0:T(8,128)(2,1)}, bf16[272,768]{1,0:T(8,128)(2,1)S(1)}, u32[]{:S(2)}, u32[]{:S(2)}) collective-permute-start(bf16[272,768]{1,0:T(8,128)(2,1)} %pack.1.n0), channel_id=1, source_target_pairs={{15,12},{12,13},{13,14},{14,15},{7,4},{4,5},{5,6},{6,7},{31,28},{2... | collective-permute-start | bytes 1253384 | tf_op jit(solution)/shard_map/ppermute | solution.py:465
  28.6 4.8 %collective-permute-start.9 = (bf16[256,1024]{1,0:T(8,128)(2,1)S(1)}, bf16[256,1024]{1,0:T(8,128)(2,1)S(1)}, u32[]{:S(2)}, u32[]{:S(2)}) collective-permute-start(bf16[256,1024]{1,0:T(8,128)(2,1)S(1)} %hand_1.1), channel_id=1, source_target_pairs={{4,6},{5,7},{6,4},{7,5},{20,22},{21,23},{22,20},{23,21}} | collective-permute-start | bytes 1572872 | tf_op jit(solution)/shard_map/ppermute | solution.py:465
  30.0 2.8 %collective-permute-start.5 = (bf16[272,768]{1,0:T(8,128)(2,1)S(1)}, bf16[272,768]{1,0:T(8,128)(2,1)S(1)}, u32[]{:S(2)}, u32[]{:S(2)}) collective-permute-start(bf16[272,768]{1,0:T(8,128)(2,1)S(1)} %get-tuple-element.31.refs_4_), channel_id=1, source_target_pairs={{12,8},{13,9},{14,10},{15,11},{28,24},{29,25},{30,26},{31,27}} | collective-permute-start | bytes 1253384 | tf_op jit(solution)/shard_map/ppermute | solution.py:465
  30.7 2.1 %collective-permute-start.6 = (bf16[272,768]{1,0:T(8,128)(2,1)S(1)}, bf16[272,768]{1,0:T(8,128)(2,1)S(1)}, u32[]{:S(2)}, u32[]{:S(2)}) collective-permute-start(bf16[272,768]{1,0:T(8,128)(2,1)S(1)} %get-tuple-element.31.refs_4_), channel_id=1, source_target_pairs={{13,8},{14,9},{15,10},{12,11},{29,24},{30,25},{31,26},{28,27}} | collective-permute-start | bytes 1253384 | tf_op jit(solution)/shard_map/ppermute | solution.py:465
  31.4 1.4 %collective-permute-start.7 = (bf16[272,768]{1,0:T(8,128)(2,1)S(1)}, bf16[272,768]{1,0:T(8,128)(2,1)S(1)}, u32[]{:S(2)}, u32[]{:S(2)}) collective-permute-start(bf16[272,768]{1,0:T(8,128)(2,1)S(1)} %get-tuple-element.31.refs_4_), channel_id=1, source_target_pairs={{14,8},{15,9},{12,10},{13,11},{30,24},{31,25},{28,26},{29,27}} | collective-permute-start | bytes 1253384 | tf_op jit(solution)/shard_map/ppermute | solution.py:465
  32.1 0.7 collective-permute-start.8
  32.8 1.0 copy-start.4
  34.4 35.0 %copy-start.3 = (bf16[8,256,1024]{2,1,0:T(8,128)(2,1)S(1)}, bf16[8,256,1024]{2,1,0:T(8,128)(2,1)}, u32[]{:S(2)}) copy-start(bf16[8,256,1024]{2,1,0:T(8,128)(2,1)} %gain.1) | copy-start | bytes 12582916
  34.4 34.4 %collective-permute-start.10 = (bf16[2064,1024]{1,0:T(8,128)(2,1)S(1)}, bf16[2064,1024]{1,0:T(8,128)(2,1)S(1)}, u32[]{:S(2)}, u32[]{:S(2)}) collective-permute-start(bf16[2064,1024]{1,0:T(8,128)(2,1)S(1)} %stack.17), channel_id=1, source_target_pairs={{4,0},{5,1},{6,2},{7,3},{20,16},{21,17},{22,18},{23,19}} | collective-permute-start | bytes 12681224 | tf_op jit(solution)/shard_map/ppermute | solution.py:465
  35.9 2.8 %collective-permute-start.15 = (bf16[272,768]{1,0:T(8,128)(2,1)S(1)}, bf16[272,768]{1,0:T(8,128)(2,1)S(1)}, u32[]{:S(2)}, u32[]{:S(2)}) collective-permute-start(bf16[272,768]{1,0:T(8,128)(2,1)S(1)} %get-tuple-element.34.event.own), channel_id=1, source_target_pairs={{10,4},{11,5},{8,6},{9,7},{26,20},{27,21},{24,22},{25,23}} | collective-permute-start | bytes 1253384 | tf_op jit(solution)/shard_map/ppermute | solution.py:465
  36.6 44.4 %collective-permute-start.13 = (bf16[272,768]{1,0:T(8,128)(2,1)S(1)}, bf16[272,768]{1,0:T(8,128)(2,1)S(1)}, u32[]{:S(2)}, u32[]{:S(2)}) collective-permute-start(bf16[272,768]{1,0:T(8,128)(2,1)S(1)} %get-tuple-element.34.event.own), channel_id=1, source_target_pairs={{8,4},{9,5},{10,6},{11,7},{24,20},{25,21},{26,22},{27,23}} | collective-permute-start | bytes 1253384 | tf_op jit(solution)/shard_map/ppermute | solution.py:465
  37.3 44.4 %collective-permute-start.14 = (bf16[272,768]{1,0:T(8,128)(2,1)S(1)}, bf16[272,768]{1,0:T(8,128)(2,1)S(1)}, u32[]{:S(2)}, u32[]{:S(2)}) collective-permute-start(bf16[272,768]{1,0:T(8,128)(2,1)S(1)} %get-tuple-element.34.event.own), channel_id=1, source_target_pairs={{9,4},{10,5},{11,6},{8,7},{25,20},{26,21},{27,22},{24,23}} | collective-permute-start | bytes 1253384 | tf_op jit(solution)/shard_map/ppermute | solution.py:465
  38.0 43.7 %collective-permute-start.16 = (bf16[272,768]{1,0:T(8,128)(2,1)S(1)}, bf16[272,768]{1,0:T(8,128)(2,1)S(1)}, u32[]{:S(2)}, u32[]{:S(2)}) collective-permute-start(bf16[272,768]{1,0:T(8,128)(2,1)S(1)} %get-tuple-element.34.event.own), channel_id=1, source_target_pairs={{8,5},{9,6},{10,7},{24,21},{25,22},{26,23}} | collective-permute-start | bytes 1253384 | tf_op jit(solution)/shard_map/ppermute | solution.py:465
  38.7 43.0 %collective-permute-start.17 = (bf16[272,768]{1,0:T(8,128)(2,1)S(1)}, bf16[272,768]{1,0:T(8,128)(2,1)S(1)}, u32[]{:S(2)}, u32[]{:S(2)}) collective-permute-start(bf16[272,768]{1,0:T(8,128)(2,1)S(1)} %collective-permute-done.15.t2), channel_id=1, source_target_pairs={{5,4},{21,20}} | collective-permute-start | bytes 1253384 | tf_op jit(solution)/shard_map/ppermute | solution.py:465
  80.4 1.4 %collective-permute-start.11 = (bf16[256,256]{1,0:T(8,128)(2,1)S(1)}, bf16[256,256]{1,0:T(8,128)(2,1)S(1)}, u32[]{:S(2)}, u32[]{:S(2)}) collective-permute-start(bf16[256,256]{1,0:T(8,128)(2,1)S(1)} %get-tuple-element.37), channel_id=1, source_target_pairs={{12,13},{13,14},{14,15},{15,12},{8,9},{9,10},{10,11},{11,8},{28,29... | collective-permute-start | bytes 393224 | tf_op jit(solution)/shard_map/ppermute | solution.py:465
  81.0 20.2 %copy-start.8 = (f32[8,256]{1,0:T(8,128)S(1)}, f32[8,256]{1,0:T(8,128)}, u32[]{:S(2)}) copy-start(f32[8,256]{1,0:T(8,128)} %offset.8) | copy-start | bytes 24580
  81.0 20.2 %copy-start.9 = (f32[8,256]{1,0:T(8,128)S(1)}, f32[8,256]{1,0:T(8,128)}, u32[]{:S(2)}) copy-start(f32[8,256]{1,0:T(8,128)} %var.1) | copy-start | bytes 24580
  81.1 0.7 collective-permute-start.12
  82.4 18.9 %collective-permute-start.18 = (bf16[4,272,768]{2,1,0:T(8,128)(2,1)S(1)}, bf16[4,272,768]{2,1,0:T(8,128)(2,1)S(1)}, u32[]{:S(2)}, u32[]{:S(2)}) collective-permute-start(bf16[4,272,768]{2,1,0:T(8,128)(2,1)S(1)} %turn.1.ends_1), channel_id=1, source_target_pairs={{4,0},{5,1},{6,2},{7,3},{20,16},{21,17},{22,18},{23,19}} | collective-permute-start | bytes 5013512 | tf_op jit(solution)/shard_map/ppermute | solution.py:465
  83.7 24.7 %collective-permute-start.22 = (bf16[256,1024]{1,0:T(8,128)(2,1)S(1)}, bf16[256,1024]{1,0:T(8,128)(2,1)S(1)}, u32[]{:S(2)}, u32[]{:S(2)}) collective-permute-start(bf16[256,1024]{1,0:T(8,128)(2,1)S(1)} %hand_0.1.event), channel_id=1, source_target_pairs={{1,0},{2,1},{3,2},{0,3},{17,16},{18,17},{19,18},{16,19}} | collective-permute-start | bytes 1572872 | tf_op jit(solution)/shard_map/ppermute | solution.py:465
  87.7 25.2 %collective-permute-start.23 = (bf16[256,1024]{1,0:T(8,128)(2,1)S(1)}, bf16[256,1024]{1,0:T(8,128)(2,1)S(1)}, u32[]{:S(2)}, u32[]{:S(2)}) collective-permute-start(bf16[256,1024]{1,0:T(8,128)(2,1)S(1)} %hand_0.1.event), channel_id=1, source_target_pairs={{0,2},{1,3},{2,0},{3,1},{16,18},{17,19},{18,16},{19,17}} | collective-permute-start | bytes 1572872 | tf_op jit(solution)/shard_map/ppermute | solution.py:465
  89.6 23.3 %collective-permute-start.24 = (bf16[256,1024]{1,0:T(8,128)(2,1)S(1)}, bf16[256,1024]{1,0:T(8,128)(2,1)S(1)}, u32[]{:S(2)}, u32[]{:S(2)}) collective-permute-start(bf16[256,1024]{1,0:T(8,128)(2,1)S(1)} %hand_0.1.event), channel_id=1, source_target_pairs={{0,1},{1,2},{2,3},{3,0},{16,17},{17,18},{18,19},{19,16}} | collective-permute-start | bytes 1572872 | tf_op jit(solution)/shard_map/ppermute | solution.py:465
  107.4 5.6 %collective-permute-start.19 = (f32[2,8,256]{2,1,0:T(8,128)S(1)}, f32[2,8,256]{2,1,0:T(8,128)S(1)}, u32[]{:S(2)}, u32[]{:S(2)}) collective-permute-start(f32[2,8,256]{2,1,0:T(8,128)S(1)} %get-tuple-element.43.s0), channel_id=1, source_target_pairs={{1,0},{2,1},{3,2},{0,3},{5,4},{6,5},{7,6},{4,7},{9,8},{10,9},{11,1... | collective-permute-start | bytes 49160 | tf_op jit(solution)/shard_map/ppermute | solution.py:465
  107.4 5.6 %collective-permute-start.20 = (f32[2,8,256]{2,1,0:T(8,128)S(1)}, f32[2,8,256]{2,1,0:T(8,128)S(1)}, u32[]{:S(2)}, u32[]{:S(2)}) collective-permute-start(f32[2,8,256]{2,1,0:T(8,128)S(1)} %get-tuple-element.43.s0), channel_id=1, source_target_pairs={{2,0},{3,1},{0,2},{1,3},{6,4},{7,5},{4,6},{5,7},{10,8},{11,9},{8,1... | collective-permute-start | bytes 49160 | tf_op jit(solution)/shard_map/ppermute | solution.py:465
  108.4 5.5 %collective-permute-start.21 = (f32[2,8,256]{2,1,0:T(8,128)S(1)}, f32[2,8,256]{2,1,0:T(8,128)S(1)}, u32[]{:S(2)}, u32[]{:S(2)}) collective-permute-start(f32[2,8,256]{2,1,0:T(8,128)S(1)} %get-tuple-element.43.s0), channel_id=1, source_target_pairs={{3,0},{0,1},{1,2},{2,3},{7,4},{4,5},{5,6},{6,7},{11,8},{8,9},{9,10... | collective-permute-start | bytes 49160 | tf_op jit(solution)/shard_map/ppermute | solution.py:465
  109.4 4.5 %copy-start.6 = (f32[8,4,128]{2,1,0:T(4,128)S(1)}, f32[8,4,128]{2,1,0:T(4,128)}, u32[]{:S(2)}) copy-start(f32[8,4,128]{2,1,0:T(4,128)} %value.1) | copy-start | bytes 49156
  109.4 4.5 %copy-start.10 = (f32[1024]{0:T(1024)S(1)}, f32[1024]{0:T(1024)}, u32[]{:S(2)}) copy-start(f32[1024]{0:T(1024)} %param.23) | copy-start | bytes 12292
  109.4 4.5 %copy-start.12 = (s32[8,4]{0,1:T(4,128)S(1)}, s32[8,4]{0,1:T(4,128)}, u32[]{:S(2)}) copy-start(s32[8,4]{0,1:T(4,128)} %param.20) | copy-start | bytes 388
  109.4 4.5 %copy-start.13 = (s32[8]{0:T(128)S(1)}, s32[8]{0:T(128)}, u32[]{:S(2)}) copy-start(s32[8]{0:T(128)} %counts.1) | copy-start | bytes 100

commit v5 on v4

--- a/solution.py
+++ b/solution.py
@@ -279,7 +279,7 @@
         lay_out(z, (n0, n1, n2, n3), lift.at[pl.ds(states, states)], lift.at[pl.ds(2 * states, TAIL)])
 
 
-def turn_kernel(where, near, far, t0, t1, t2, t3, t4, out):
+def turn_kernel(where, near, far, b2, t0, t1, t2, t3, t4, out):
     def body(a, parcel):
         out[a] = parcel[...]
 
@@ -555,7 +555,7 @@
     )
     gains_0 = [route(gain_0, within((0,), moves)) for moves in (back, two_on, on)]
     near, far = route(beside_block, within((3, 2), on)), route(far_block, within((3, 2), ((0, 2), (3, 1))))
-    (ends_1,) = call(turn_kernel, "turn", (shape((RING, *parcel_shape.shape)),), (near, far, *third), [], 0)
+    (ends_1,) = call(turn_kernel, "turn", (shape((RING, *parcel_shape.shape)),), (near, far, gains_0[1], *third), [], 0)
     ends_0 = send(ends_1, ((1, 0),), 0)
     out_steps = shape((steps, BLOCK), F32)
     _, means, step_mean, step_spread, stats = call(

time: 117 us -> 116 us (level)
  waiting for transfers between devices: 48.6 us -> 43.4 us
  starting transfers between devices: 36.6 us -> 39.6 us
    ppermute x25, waiting for transfers between devices: 48.6 us -> 43.4 us  [route(): return lax.ppermute(block, ('tm', 'tile'), table)]
    ppermute x25, starting transfers between devices: 36.6 us -> 39.6 us  [route(): return lax.ppermute(block, ('tm', 'tile'), table)]
where the time goes in v5:
time: 116 us; the launch traced here: 115 us
  waiting for transfers between devices  43.4 us (37%)
  starting transfers between devices  39.6 us (34%)
  Pallas kernels  29.4 us (25%)
  between operations  1.32 us (1%)
    ppermute x25, waiting for transfers between devices, route(): return lax.ppermute(block, ('tm', 'tile'), table)  43.4 us
    ppermute x25, starting transfers between devices, route(): return lax.ppermute(block, ('tm', 'tile'), table)  39.6 us
    pallas_call x7, Pallas kernels, call(): pl.pallas_call(kernel, out_shape=out_shape, in_specs=[smem()] + [vmem()]...  22.8 us
    pallas_call x3, Pallas kernels, pack(): pl.pallas_call(kernel, out_shape=out_shape, in_specs=[smem()] + [pl.Block...  3.8 us
    pallas_call x1, Pallas kernels, ring_shards(): pl.pallas_call(innovation_kernel, out_shape=(shape(obs_value.shape, F32),...  2.76 us
  transfers between devices with their start and end apart: 25, of which 4 were waited for; matrix products, arithmetic and copies ran while one was open for 1% of the time, Pallas kernels for 22%

profile of v5, /device:TPU:0, one launch (start us, length us, event | category | flops | bytes accessed | tf_op | source)
XLA Modules:
  0.0 114.8 jit_solution(16527775924753392752)
XLA Ops:
  0.6 0.8 collective-permute-start
  1.5 0.7 collective-permute-start.1
  2.2 0.6 pad_add_fusion.where
  2.8 0.0 copy-start.11
  2.8 2.7 %pack.1.n0 = bf16[272,768]{1,0:T(8,128)(2,1)} custom-call(s32[3]{0:T(128)} %pad_add_fusion.where, bf16[2,256,1024]{2,1,0:T(8,128)(2,1)} %refs_0_.1, bf16[256,1024]{1,0:T(8,128)(2,1)} %bitcast.18, bf16[2,256]{1,0:T(2,128)(2,1)} %refs_1_.1, f32[1,256]{1,0:T(1,128)} %offset.9), custom_call_target="tpu_custom_call" | custom-call | bytes 1000000 | tf_op jit(solution)/shard_map/pack/pallas_call | solution.py:492
  5.5 12.2 %collective-permute-start.3 = (bf16[272,768]{1,0:T(8,128)(2,1)}, bf16[272,768]{1,0:T(8,128)(2,1)S(1)}, u32[]{:S(2)}, u32[]{:S(2)}) collective-permute-start(bf16[272,768]{1,0:T(8,128)(2,1)} %pack.1.n0), channel_id=1, source_target_pairs={{2,12},{3,13},{0,14},{1,15},{6,4},{7,5},{4,6},{5,7},{18,28},{19,29... | collective-permute-start | bytes 1253384 | tf_op jit(solution)/shard_map/ppermute | solution.py:465
  17.6 0.7 collective-permute-start.2
  18.3 0.7 collective-permute-start.4
  19.0 9.0 %collective-permute-done.3.refs_3_.event.n2 = bf16[272,768]{1,0:T(8,128)(2,1)S(1)} collective-permute-done((bf16[272,768]{1,0:T(8,128)(2,1)}, bf16[272,768]{1,0:T(8,128)(2,1)S(1)}, u32[]{:S(2)}, u32[]{:S(2)}) %collective-permute-start.3) | collective-permute-done | bytes 417824 | tf_op jit(solution)/shard_map/ppermute | solution.py:465
  28.1 0.6 hand_1.1
  28.6 0.7 collective-permute-start.9
  29.3 0.0 collective-permute-done.2.refs_2_.n1
  29.3 0.0 collective-permute-done.4.refs_4_.n3
  29.3 0.0 collective-permute-done.g1.a1
  29.4 0.0 collective-permute-done.1.g2.g3.a3
  29.4 0.6 pairs_3.1
  30.0 0.7 collective-permute-start.5
  30.7 0.7 collective-permute-start.6
  31.4 0.7 collective-permute-start.7
  32.1 0.7 collective-permute-start.8
  32.8 0.0 collective-permute-done.5.refs_0_
  32.8 0.0 collective-permute-done.6.refs_1_
  32.8 0.0 collective-permute-done.7.refs_2_
  32.8 0.0 collective-permute-done.8.refs_3_
  32.8 0.0 copy-start.4
  32.8 0.6 pairs_2.1
  33.4 0.0 collective-permute-done.9.g2.a2
  33.4 0.4 copy-done.4
  33.8 0.5 stack.17
  34.4 0.0 copy-start.3
  34.4 1.6 %collective-permute-start.10 = (bf16[2064,1024]{1,0:T(8,128)(2,1)S(1)}, bf16[2064,1024]{1,0:T(8,128)(2,1)S(1)}, u32[]{:S(2)}, u32[]{:S(2)}) collective-permute-start(bf16[2064,1024]{1,0:T(8,128)(2,1)S(1)} %stack.17), channel_id=1, source_target_pairs={{4,0},{5,1},{6,2},{7,3},{20,16},{21,17},{22,18},{23,19}} | collective-permute-start | bytes 12681224 | tf_op jit(solution)/shard_map/ppermute | solution.py:465
  35.9 0.7 collective-permute-start.16
  36.6 0.7 collective-permute-start.14
  37.3 0.7 collective-permute-start.15
  38.0 0.7 collective-permute-start.17
  38.7 0.0 collective-permute-done.16.t2
  38.7 0.7 collective-permute-start.18
  39.4 29.3 %collective-permute-done.10.event.lift = bf16[2064,1024]{1,0:T(8,128)(2,1)S(1)} collective-permute-done((bf16[2064,1024]{1,0:T(8,128)(2,1)S(1)}, bf16[2064,1024]{1,0:T(8,128)(2,1)S(1)}, u32[]{:S(2)}, u32[]{:S(2)}) %collective-permute-start.10) | collective-permute-done | bytes 4227104 | tf_op jit(solution)/shard_map/ppermute | solution.py:465
  68.8 0.6 hand_0.1.event
  69.3 1.9 %collective-permute-start.13 = (bf16[256,1024]{1,0:T(8,128)(2,1)S(1)}, bf16[256,1024]{1,0:T(8,128)(2,1)S(1)}, u32[]{:S(2)}, u32[]{:S(2)}) collective-permute-start(bf16[256,1024]{1,0:T(8,128)(2,1)S(1)} %hand_0.1.event), channel_id=1, source_target_pairs={{0,2},{1,3},{2,0},{3,1},{16,18},{17,19},{18,16},{19,17}} | collective-permute-start | bytes 1572872 | tf_op jit(solution)/shard_map/ppermute | solution.py:465
  71.3 11.0 %ahead.1 = (bf16[8,256,1024]{2,1,0:T(8,128)(2,1)S(1)}, f32[8,256]{1,0:T(8,128)S(1)}, bf16[256,1024]{1,0:T(8,128)(2,1)S(1)}, f32[256,1024]{1,0:T(8,128)S(1)}, bf1...) custom-call(s32[3]{0:T(128)S(1)} %copy-done.5, bf16[256,1024]{1,0:T(8,128)(2,1)S(1)} %hand_0.1.event, ...), custom_call_target="tpu_custom_call" | custom-call | flops 9663676416 | bytes 15769600 | tf_op jit(solution)/shard_map/ahead/pallas_call | solution.py:479
  82.3 0.0 collective-permute-done.14.t0
  82.3 0.7 collective-permute-start.11
  83.0 0.0 copy-start.8
  83.0 0.0 copy-start.9
  83.0 0.7 collective-permute-start.12
  83.7 0.0 collective-permute-done.18.t4
  83.7 0.0 collective-permute-done.11.near
  83.8 2.4 %collective-permute-done.13.b2 = bf16[256,1024]{1,0:T(8,128)(2,1)S(1)} collective-permute-done((bf16[256,1024]{1,0:T(8,128)(2,1)S(1)}, bf16[256,1024]{1,0:T(8,128)(2,1)S(1)}, u32[]{:S(2)}, u32[]{:S(2)}) %collective-permute-start.13) | collective-permute-done | bytes 524320 | tf_op jit(solution)/shard_map/ppermute | solution.py:465
  86.2 0.5 turn.1.ends_1
  86.7 1.3 %collective-permute-start.19 = (bf16[4,272,768]{2,1,0:T(8,128)(2,1)S(1)}, bf16[4,272,768]{2,1,0:T(8,128)(2,1)S(1)}, u32[]{:S(2)}, u32[]{:S(2)}) collective-permute-start(bf16[4,272,768]{2,1,0:T(8,128)(2,1)S(1)} %turn.1.ends_1), channel_id=1, source_target_pairs={{4,0},{5,1},{6,2},{7,3},{20,16},{21,17},{22,18},{23,19}} | collective-permute-start | bytes 5013512 | tf_op jit(solution)/shard_map/ppermute | solution.py:465
  88.0 3.6 %collective-permute-start.23 = (bf16[256,1024]{1,0:T(8,128)(2,1)S(1)}, bf16[256,1024]{1,0:T(8,128)(2,1)S(1)}, u32[]{:S(2)}, u32[]{:S(2)}) collective-permute-start(bf16[256,1024]{1,0:T(8,128)(2,1)S(1)} %hand_0.1.event), channel_id=1, source_target_pairs={{1,0},{2,1},{3,2},{0,3},{17,16},{18,17},{19,18},{16,19}} | collective-permute-start | bytes 1572872 | tf_op jit(solution)/shard_map/ppermute | solution.py:465
  91.6 2.2 %collective-permute-start.24 = (bf16[256,1024]{1,0:T(8,128)(2,1)S(1)}, bf16[256,1024]{1,0:T(8,128)(2,1)S(1)}, u32[]{:S(2)}, u32[]{:S(2)}) collective-permute-start(bf16[256,1024]{1,0:T(8,128)(2,1)S(1)} %hand_0.1.event), channel_id=1, source_target_pairs={{0,1},{1,2},{2,3},{3,0},{16,17},{17,18},{18,19},{19,16}} | collective-permute-start | bytes 1572872 | tf_op jit(solution)/shard_map/ppermute | solution.py:465
  93.9 2.6 %collective-permute-done.19.ends_0 = bf16[4,272,768]{2,1,0:T(8,128)(2,1)S(1)} collective-permute-done((bf16[4,272,768]{2,1,0:T(8,128)(2,1)S(1)}, bf16[4,272,768]{2,1,0:T(8,128)(2,1)S(1)}, u32[]{:S(2)}, u32[]{:S(2)}) %collective-permute-start.19) | collective-permute-done | bytes 1671200 | tf_op jit(solution)/shard_map/ppermute | solution.py:465
  96.5 6.1 %moments.1 = (bf16[4,768,256]{2,1,0:T(8,128)(2,1)S(1)}, bf16[16,1024]{1,0:T(8,128)(2,1)S(1)}, f32[8,256]{1,0:T(8,128)}, f32[8,256]{1,0:T(8,128)}, f32[2,8,256]{2,1,0:T(8,128)S(1)}) custom-call(s32[3]{0:T(128)S(1)} %copy-done.5, bf16[4,272,768]{2,1,0:T(8,128)(2,1)S(1)} %turn.1.ends_1, ...), custom_call_target="tpu_custom_call", output_to_operand_aliasing={{0}: (9, {}), {1}: (10, {})} | custom-call | flops 4294967296 | bytes 19226624 | tf_op jit(solution)/shard_map/moments/pallas_call | solution.py:479
  102.5 1.7 %collective-permute-start.20 = (f32[2,8,256]{2,1,0:T(8,128)S(1)}, f32[2,8,256]{2,1,0:T(8,128)S(1)}, u32[]{:S(2)}, u32[]{:S(2)}) collective-permute-start(f32[2,8,256]{2,1,0:T(8,128)S(1)} %get-tuple-element.43.s0), channel_id=1, source_target_pairs={{1,0},{2,1},{3,2},{0,3},{5,4},{6,5},{7,6},{4,7},{9,8},{10,9},{11,1... | collective-permute-start | bytes 49160 | tf_op jit(solution)/shard_map/ppermute | solution.py:465
  104.3 2.0 %collective-permute-start.21 = (f32[2,8,256]{2,1,0:T(8,128)S(1)}, f32[2,8,256]{2,1,0:T(8,128)S(1)}, u32[]{:S(2)}, u32[]{:S(2)}) collective-permute-start(f32[2,8,256]{2,1,0:T(8,128)S(1)} %get-tuple-element.43.s0), channel_id=1, source_target_pairs={{2,0},{3,1},{0,2},{1,3},{6,4},{7,5},{4,6},{5,7},{10,8},{11,9},{8,1... | collective-permute-start | bytes 49160 | tf_op jit(solution)/shard_map/ppermute | solution.py:465
  106.3 2.0 %collective-permute-start.22 = (f32[2,8,256]{2,1,0:T(8,128)S(1)}, f32[2,8,256]{2,1,0:T(8,128)S(1)}, u32[]{:S(2)}, u32[]{:S(2)}) collective-permute-start(f32[2,8,256]{2,1,0:T(8,128)S(1)} %get-tuple-element.43.s0), channel_id=1, source_target_pairs={{3,0},{0,1},{1,2},{2,3},{7,4},{4,5},{5,6},{6,7},{11,8},{8,9},{9,10... | collective-permute-start | bytes 49160 | tf_op jit(solution)/shard_map/ppermute | solution.py:465
  108.3 3.5 %last.1 = (bf16[256,1024]{1,0:T(8,128)(2,1)}, bf16[16,256]{1,0:T(8,128)(2,1)S(1)}, bf16[256,1024]{1,0:T(8,128)(2,1)S(1)}) custom-call(s32[3]{0:T(128)S(1)} %copy-done.5, bf16[256,1024]{1,0:T(8,128)(2,1)S(1)} %bitcast.16, bf16[256,1024]{1,0:T(8,128)(2,1)S(1)} %collective-permute-done.g1.a1, bf16[256,1024]{1,0:T(8,128)(2,1)S(1)} %collective-permute-done.9.g2.a2, ...), custom_call_target="tpu_custom_call" | custom-call | flops 1073741824 | bytes 12854272 | tf_op jit(solution)/shard_map/last/pallas_call | solution.py:479
  111.8 0.0 collective-permute-done.23.b1
  111.8 0.0 collective-permute-done.24.b3
  111.8 0.0 collective-permute-done.21.s2
  111.8 0.0 collective-permute-done.22.s3
  111.8 2.8 %innovation.1 = (f32[8,4,128]{2,1,0:T(4,128)}, bf16[1,256]{1,0:T(2,128)(2,1)}, bf16[256,1024]{1,0:T(8,128)(2,1)}) custom-call(s32[3]{0:T(128)S(1)} %copy-done.5, s32[4,8]{1,0:T(4,128)S(1)} %bitcast.24, s32[8]{0:T(128)S(1)} %copy-done.13, f32[2,8,256]{2,1,0:T(8,128)S(1)} %get-tuple-element.43.s0, ...), custom_call_target="tpu_custom_call", output_to_operand_aliasing={{2}: (21, {})} | custom-call | bytes 200000 | tf_op jit(solution)/shard_map/innovation/pallas_call | solution.py:580
  (26 shorter events, 0.1 us)
Async XLA Ops:
  0.6 27.4 %copy-start = (bf16[1,256,1024]{2,1,0:T(8,128)(2,1)S(1)}, bf16[1,256,1024]{2,1,0:T(8,128)(2,1)}, u32[]{:S(2)}) copy-start(bf16[1,256,1024]{2,1,0:T(8,128)(2,1)} %param.12) | copy-start | bytes 1572868
  0.6 28.7 %collective-permute-start = (bf16[256,1024]{1,0:T(8,128)(2,1)}, bf16[256,1024]{1,0:T(8,128)(2,1)S(1)}, u32[]{:S(2)}, u32[]{:S(2)}) collective-permute-start(bf16[256,1024]{1,0:T(8,128)(2,1)} %bitcast.8), channel_id=1, source_target_pairs={{13,12},{14,13},{15,14},{12,15},{9,8},{10,9},{11,10},{8,11},{5,4},... | collective-permute-start | bytes 1572872 | tf_op jit(solution)/shard_map/ppermute | solution.py:465
  1.5 27.9 %collective-permute-start.1 = (bf16[256,1024]{1,0:T(8,128)(2,1)}, bf16[256,1024]{1,0:T(8,128)(2,1)S(1)}, u32[]{:S(2)}, u32[]{:S(2)}) collective-permute-start(bf16[256,1024]{1,0:T(8,128)(2,1)} %bitcast.9), channel_id=1, source_target_pairs={{14,12},{13,15},{10,8},{9,11},{4,5},{5,6},{6,7},{7,4},{30,28},{29,... | collective-permute-start | bytes 1572872 | tf_op jit(solution)/shard_map/ppermute | solution.py:465
  2.8 25.3 %copy-start.5 = (s32[3]{0:T(128)S(1)}, s32[3]{0:T(128)}, u32[]{:S(2)}) copy-start(s32[3]{0:T(128)} %pad_add_fusion.where) | copy-start | bytes 40
  2.8 26.6 %copy-start.1 = (bf16[1,256,1024]{2,1,0:T(8,128)(2,1)S(1)}, bf16[1,256,1024]{2,1,0:T(8,128)(2,1)}, u32[]{:S(2)}) copy-start(bf16[1,256,1024]{2,1,0:T(8,128)(2,1)} %param.14) | copy-start | bytes 1572868
  2.8 26.6 %copy-start.2 = (bf16[2,256,1024]{2,1,0:T(8,128)(2,1)S(1)}, bf16[2,256,1024]{2,1,0:T(8,128)(2,1)}, u32[]{:S(2)}) copy-start(bf16[2,256,1024]{2,1,0:T(8,128)(2,1)} %refs_0_.1) | copy-start | bytes 3145732
  2.8 26.6 %copy-start.7 = (f32[1,256]{1,0:T(1,128)S(1)}, f32[1,256]{1,0:T(1,128)}, u32[]{:S(2)}) copy-start(f32[1,256]{1,0:T(1,128)} %offset.9) | copy-start | bytes 3076
  2.8 26.6 %copy-start.11 = (bf16[2,256]{1,0:T(2,128)(2,1)S(1)}, bf16[2,256]{1,0:T(2,128)(2,1)}, u32[]{:S(2)}) copy-start(bf16[2,256]{1,0:T(2,128)(2,1)} %refs_1_.1) | copy-start | bytes 3076
  5.5 22.6 %collective-permute-start.3 = (bf16[272,768]{1,0:T(8,128)(2,1)}, bf16[272,768]{1,0:T(8,128)(2,1)S(1)}, u32[]{:S(2)}, u32[]{:S(2)}) collective-permute-start(bf16[272,768]{1,0:T(8,128)(2,1)} %pack.1.n0), channel_id=1, source_target_pairs={{2,12},{3,13},{0,14},{1,15},{6,4},{7,5},{4,6},{5,7},{18,28},{19,29... | collective-permute-start | bytes 1253384 | tf_op jit(solution)/shard_map/ppermute | solution.py:465
  17.6 11.7 %collective-permute-start.2 = (bf16[272,768]{1,0:T(8,128)(2,1)}, bf16[272,768]{1,0:T(8,128)(2,1)S(1)}, u32[]{:S(2)}, u32[]{:S(2)}) collective-permute-start(bf16[272,768]{1,0:T(8,128)(2,1)} %pack.1.n0), channel_id=1, source_target_pairs={{13,12},{14,13},{15,14},{12,15},{5,4},{6,5},{7,6},{4,7},{29,28},{3... | collective-permute-start | bytes 1253384 | tf_op jit(solution)/shard_map/ppermute | solution.py:465
  18.3 11.0 %collective-permute-start.4 = (bf16[272,768]{1,0:T(8,128)(2,1)}, bf16[272,768]{1,0:T(8,128)(2,1)S(1)}, u32[]{:S(2)}, u32[]{:S(2)}) collective-permute-start(bf16[272,768]{1,0:T(8,128)(2,1)} %pack.1.n0), channel_id=1, source_target_pairs={{15,12},{12,13},{13,14},{14,15},{7,4},{4,5},{5,6},{6,7},{31,28},{2... | collective-permute-start | bytes 1253384 | tf_op jit(solution)/shard_map/ppermute | solution.py:465
  28.6 4.8 %collective-permute-start.9 = (bf16[256,1024]{1,0:T(8,128)(2,1)S(1)}, bf16[256,1024]{1,0:T(8,128)(2,1)S(1)}, u32[]{:S(2)}, u32[]{:S(2)}) collective-permute-start(bf16[256,1024]{1,0:T(8,128)(2,1)S(1)} %hand_1.1), channel_id=1, source_target_pairs={{4,6},{5,7},{6,4},{7,5},{20,22},{21,23},{22,20},{23,21}} | collective-permute-start | bytes 1572872 | tf_op jit(solution)/shard_map/ppermute | solution.py:465
  30.0 2.8 %collective-permute-start.5 = (bf16[272,768]{1,0:T(8,128)(2,1)S(1)}, bf16[272,768]{1,0:T(8,128)(2,1)S(1)}, u32[]{:S(2)}, u32[]{:S(2)}) collective-permute-start(bf16[272,768]{1,0:T(8,128)(2,1)S(1)} %get-tuple-element.31.refs_4_), channel_id=1, source_target_pairs={{12,8},{13,9},{14,10},{15,11},{28,24},{29,25},{30,26},{31,27}} | collective-permute-start | bytes 1253384 | tf_op jit(solution)/shard_map/ppermute | solution.py:465
  30.7 2.1 %collective-permute-start.6 = (bf16[272,768]{1,0:T(8,128)(2,1)S(1)}, bf16[272,768]{1,0:T(8,128)(2,1)S(1)}, u32[]{:S(2)}, u32[]{:S(2)}) collective-permute-start(bf16[272,768]{1,0:T(8,128)(2,1)S(1)} %get-tuple-element.31.refs_4_), channel_id=1, source_target_pairs={{13,8},{14,9},{15,10},{12,11},{29,24},{30,25},{31,26},{28,27}} | collective-permute-start | bytes 1253384 | tf_op jit(solution)/shard_map/ppermute | solution.py:465
  31.4 1.4 %collective-permute-start.7 = (bf16[272,768]{1,0:T(8,128)(2,1)S(1)}, bf16[272,768]{1,0:T(8,128)(2,1)S(1)}, u32[]{:S(2)}, u32[]{:S(2)}) collective-permute-start(bf16[272,768]{1,0:T(8,128)(2,1)S(1)} %get-tuple-element.31.refs_4_), channel_id=1, source_target_pairs={{14,8},{15,9},{12,10},{13,11},{30,24},{31,25},{28,26},{29,27}} | collective-permute-start | bytes 1253384 | tf_op jit(solution)/shard_map/ppermute | solution.py:465
  32.1 0.7 collective-permute-start.8
  32.8 1.0 copy-start.4
  34.4 36.9 %copy-start.3 = (bf16[8,256,1024]{2,1,0:T(8,128)(2,1)S(1)}, bf16[8,256,1024]{2,1,0:T(8,128)(2,1)}, u32[]{:S(2)}) copy-start(bf16[8,256,1024]{2,1,0:T(8,128)(2,1)} %gain.1) | copy-start | bytes 12582916
  34.4 34.4 %collective-permute-start.10 = (bf16[2064,1024]{1,0:T(8,128)(2,1)S(1)}, bf16[2064,1024]{1,0:T(8,128)(2,1)S(1)}, u32[]{:S(2)}, u32[]{:S(2)}) collective-permute-start(bf16[2064,1024]{1,0:T(8,128)(2,1)S(1)} %stack.17), channel_id=1, source_target_pairs={{4,0},{5,1},{6,2},{7,3},{20,16},{21,17},{22,18},{23,19}} | collective-permute-start | bytes 12681224 | tf_op jit(solution)/shard_map/ppermute | solution.py:465
  35.9 2.8 %collective-permute-start.16 = (bf16[272,768]{1,0:T(8,128)(2,1)S(1)}, bf16[272,768]{1,0:T(8,128)(2,1)S(1)}, u32[]{:S(2)}, u32[]{:S(2)}) collective-permute-start(bf16[272,768]{1,0:T(8,128)(2,1)S(1)} %get-tuple-element.34.event.own), channel_id=1, source_target_pairs={{10,4},{11,5},{8,6},{9,7},{26,20},{27,21},{24,22},{25,23}} | collective-permute-start | bytes 1253384 | tf_op jit(solution)/shard_map/ppermute | solution.py:465
  36.6 45.7 %collective-permute-start.14 = (bf16[272,768]{1,0:T(8,128)(2,1)S(1)}, bf16[272,768]{1,0:T(8,128)(2,1)S(1)}, u32[]{:S(2)}, u32[]{:S(2)}) collective-permute-start(bf16[272,768]{1,0:T(8,128)(2,1)S(1)} %get-tuple-element.34.event.own), channel_id=1, source_target_pairs={{8,4},{9,5},{10,6},{11,7},{24,20},{25,21},{26,22},{27,23}} | collective-permute-start | bytes 1253384 | tf_op jit(solution)/shard_map/ppermute | solution.py:465
  37.3 45.7 %collective-permute-start.15 = (bf16[272,768]{1,0:T(8,128)(2,1)S(1)}, bf16[272,768]{1,0:T(8,128)(2,1)S(1)}, u32[]{:S(2)}, u32[]{:S(2)}) collective-permute-start(bf16[272,768]{1,0:T(8,128)(2,1)S(1)} %get-tuple-element.34.event.own), channel_id=1, source_target_pairs={{9,4},{10,5},{11,6},{8,7},{25,20},{26,21},{27,22},{24,23}} | collective-permute-start | bytes 1253384 | tf_op jit(solution)/shard_map/ppermute | solution.py:465
  38.0 45.7 %collective-permute-start.17 = (bf16[272,768]{1,0:T(8,128)(2,1)S(1)}, bf16[272,768]{1,0:T(8,128)(2,1)S(1)}, u32[]{:S(2)}, u32[]{:S(2)}) collective-permute-start(bf16[272,768]{1,0:T(8,128)(2,1)S(1)} %get-tuple-element.34.event.own), channel_id=1, source_target_pairs={{8,5},{9,6},{10,7},{24,21},{25,22},{26,23}} | collective-permute-start | bytes 1253384 | tf_op jit(solution)/shard_map/ppermute | solution.py:465
  38.7 45.0 %collective-permute-start.18 = (bf16[272,768]{1,0:T(8,128)(2,1)S(1)}, bf16[272,768]{1,0:T(8,128)(2,1)S(1)}, u32[]{:S(2)}, u32[]{:S(2)}) collective-permute-start(bf16[272,768]{1,0:T(8,128)(2,1)S(1)} %collective-permute-done.16.t2), channel_id=1, source_target_pairs={{5,4},{21,20}} | collective-permute-start | bytes 1253384 | tf_op jit(solution)/shard_map/ppermute | solution.py:465
  69.3 16.8 %collective-permute-start.13 = (bf16[256,1024]{1,0:T(8,128)(2,1)S(1)}, bf16[256,1024]{1,0:T(8,128)(2,1)S(1)}, u32[]{:S(2)}, u32[]{:S(2)}) collective-permute-start(bf16[256,1024]{1,0:T(8,128)(2,1)S(1)} %hand_0.1.event), channel_id=1, source_target_pairs={{0,2},{1,3},{2,0},{3,1},{16,18},{17,19},{18,16},{19,17}} | collective-permute-start | bytes 1572872 | tf_op jit(solution)/shard_map/ppermute | solution.py:465
  82.3 1.4 %collective-permute-start.11 = (bf16[256,256]{1,0:T(8,128)(2,1)S(1)}, bf16[256,256]{1,0:T(8,128)(2,1)S(1)}, u32[]{:S(2)}, u32[]{:S(2)}) collective-permute-start(bf16[256,256]{1,0:T(8,128)(2,1)S(1)} %get-tuple-element.37), channel_id=1, source_target_pairs={{12,13},{13,14},{14,15},{15,12},{8,9},{9,10},{10,11},{11,8},{28,29... | collective-permute-start | bytes 393224 | tf_op jit(solution)/shard_map/ppermute | solution.py:465
  83.0 13.5 %copy-start.8 = (f32[8,256]{1,0:T(8,128)S(1)}, f32[8,256]{1,0:T(8,128)}, u32[]{:S(2)}) copy-start(f32[8,256]{1,0:T(8,128)} %offset.8) | copy-start | bytes 24580
  83.0 13.4 %copy-start.9 = (f32[8,256]{1,0:T(8,128)S(1)}, f32[8,256]{1,0:T(8,128)}, u32[]{:S(2)}) copy-start(f32[8,256]{1,0:T(8,128)} %var.1) | copy-start | bytes 24580
  83.0 0.7 collective-permute-start.12
  86.7 9.8 %collective-permute-start.19 = (bf16[4,272,768]{2,1,0:T(8,128)(2,1)S(1)}, bf16[4,272,768]{2,1,0:T(8,128)(2,1)S(1)}, u32[]{:S(2)}, u32[]{:S(2)}) collective-permute-start(bf16[4,272,768]{2,1,0:T(8,128)(2,1)S(1)} %turn.1.ends_1), channel_id=1, source_target_pairs={{4,0},{5,1},{6,2},{7,3},{20,16},{21,17},{22,18},{23,19}} | collective-permute-start | bytes 5013512 | tf_op jit(solution)/shard_map/ppermute | solution.py:465
  88.0 23.8 %collective-permute-start.23 = (bf16[256,1024]{1,0:T(8,128)(2,1)S(1)}, bf16[256,1024]{1,0:T(8,128)(2,1)S(1)}, u32[]{:S(2)}, u32[]{:S(2)}) collective-permute-start(bf16[256,1024]{1,0:T(8,128)(2,1)S(1)} %hand_0.1.event), channel_id=1, source_target_pairs={{1,0},{2,1},{3,2},{0,3},{17,16},{18,17},{19,18},{16,19}} | collective-permute-start | bytes 1572872 | tf_op jit(solution)/shard_map/ppermute | solution.py:465
  91.6 20.1 %collective-permute-start.24 = (bf16[256,1024]{1,0:T(8,128)(2,1)S(1)}, bf16[256,1024]{1,0:T(8,128)(2,1)S(1)}, u32[]{:S(2)}, u32[]{:S(2)}) collective-permute-start(bf16[256,1024]{1,0:T(8,128)(2,1)S(1)} %hand_0.1.event), channel_id=1, source_target_pairs={{0,1},{1,2},{2,3},{3,0},{16,17},{17,18},{18,19},{19,16}} | collective-permute-start | bytes 1572872 | tf_op jit(solution)/shard_map/ppermute | solution.py:465
  102.5 9.2 %collective-permute-start.20 = (f32[2,8,256]{2,1,0:T(8,128)S(1)}, f32[2,8,256]{2,1,0:T(8,128)S(1)}, u32[]{:S(2)}, u32[]{:S(2)}) collective-permute-start(f32[2,8,256]{2,1,0:T(8,128)S(1)} %get-tuple-element.43.s0), channel_id=1, source_target_pairs={{1,0},{2,1},{3,2},{0,3},{5,4},{6,5},{7,6},{4,7},{9,8},{10,9},{11,1... | collective-permute-start | bytes 49160 | tf_op jit(solution)/shard_map/ppermute | solution.py:465
  104.3 7.5 %collective-permute-start.21 = (f32[2,8,256]{2,1,0:T(8,128)S(1)}, f32[2,8,256]{2,1,0:T(8,128)S(1)}, u32[]{:S(2)}, u32[]{:S(2)}) collective-permute-start(f32[2,8,256]{2,1,0:T(8,128)S(1)} %get-tuple-element.43.s0), channel_id=1, source_target_pairs={{2,0},{3,1},{0,2},{1,3},{6,4},{7,5},{4,6},{5,7},{10,8},{11,9},{8,1... | collective-permute-start | bytes 49160 | tf_op jit(solution)/shard_map/ppermute | solution.py:465
  106.3 5.5 %collective-permute-start.22 = (f32[2,8,256]{2,1,0:T(8,128)S(1)}, f32[2,8,256]{2,1,0:T(8,128)S(1)}, u32[]{:S(2)}, u32[]{:S(2)}) collective-permute-start(f32[2,8,256]{2,1,0:T(8,128)S(1)} %get-tuple-element.43.s0), channel_id=1, source_target_pairs={{3,0},{0,1},{1,2},{2,3},{7,4},{4,5},{5,6},{6,7},{11,8},{8,9},{9,10... | collective-permute-start | bytes 49160 | tf_op jit(solution)/shard_map/ppermute | solution.py:465
  108.3 3.6 %copy-start.6 = (f32[8,4,128]{2,1,0:T(4,128)S(1)}, f32[8,4,128]{2,1,0:T(4,128)}, u32[]{:S(2)}) copy-start(f32[8,4,128]{2,1,0:T(4,128)} %value.1) | copy-start | bytes 49156
  108.3 3.6 %copy-start.10 = (f32[1024]{0:T(1024)S(1)}, f32[1024]{0:T(1024)}, u32[]{:S(2)}) copy-start(f32[1024]{0:T(1024)} %param.23) | copy-start | bytes 12292
  108.3 3.6 %copy-start.12 = (s32[8,4]{0,1:T(4,128)S(1)}, s32[8,4]{0,1:T(4,128)}, u32[]{:S(2)}) copy-start(s32[8,4]{0,1:T(4,128)} %param.20) | copy-start | bytes 388
  108.3 3.6 %copy-start.13 = (s32[8]{0:T(128)S(1)}, s32[8]{0:T(128)}, u32[]{:S(2)}) copy-start(s32[8]{0:T(128)} %counts.1) | copy-start | bytes 100

commit v6 on v5

--- a/solution.py
+++ b/solution.py
@@ -229,8 +229,8 @@
 def pairs_kernel(at_seg, where, g0, g1, g2, noise, offset, *refs):
     z, seg, group = where[0], where[1], where[2]
     if at_seg == GROUP_SEGS - 1:
-        end_cov, end_mean, *others, half, half_mean, parcel, mean_row, full, mean, own = refs
-        parcels = (own, *others)
+        end_cov, end_mean, p1, p2, p3, from_1, across, half, half_mean, parcel, mean_row, full, mean, own = refs
+        parcels = (own, (z < RING - 1, p1, across), (z > 0, p2, from_1), (z > 0, p3, across))
     else:
         *parcels, early, _, _, half, half_mean, parcel, mean_row, beside, far, full, mean = refs
 
@@ -362,7 +362,7 @@
         steps(gain, None)
 
 
-def last_kernel(where, g0, a1, a2, a3, ends_1, ends_0, lift, through, beside, noise, offset, means, rows, mean_row, product, full, mean):
+def last_kernel(where, g0, a1, a2, a3, ends_1, ends_0, lift, through, beside, noise, offset, means, own, far, near, rows, mean_row, product, full, mean):
     z, seg = where[0], where[1]
     states = g0.shape[1]
     mean_row[...] = (dot_nt(means[...], g0[...]) + offset[...]).astype(BF16)
@@ -377,6 +377,20 @@
     def _():
         lay_out(z, [ends_1.at[a] for a in range(RING)], full, mean)
         finish(z, dot(g0[...], full[...]).astype(BF16), (g0, a1, a2, a3), noise, rows)
+
+    @pl.when(seg > 1)
+    def _():
+        rows[:, cols(z)] = own[:BLOCK, :BLOCK]
+        rows[:, cols(spot(z, 1))] = own[:BLOCK, BLOCK : 2 * BLOCK]
+        rows[:, cols(spot(z, 3))] = near[...].T
+
+        @pl.when(owns_far(z))
+        def _():
+            rows[:, cols(spot(z, 2))] = own[:BLOCK, 2 * BLOCK :]
+
+        @pl.when(jnp.logical_not(owns_far(z)))
+        def _():
+            rows[:, cols(spot(z, 2))] = far[...].T
 
 
 def finish(z, product, gains, noise, rows):
@@ -385,29 +399,13 @@
         rows[:, column] = (dot_nt(product, gain[...]) + noise[:, column].astype(F32)).astype(BF16)
 
 
-def innovation_kernel(where, tiles, counts, s0, s1, s2, s3, value, noise, own, far, near, mean_1, mean_2, mean_3, product, g0, b1, b2, b3, cov_noise, _, out, mean_row, rows_out, full, rows, sem):
+def innovation_kernel(where, tiles, counts, s0, s1, s2, s3, value, noise, mean_1, mean_2, mean_3, product, g0, b1, b2, b3, cov_noise, _, out, mean_row, rows_out, full, rows, sem):
     z, seg = where[0], where[1]
     copy = pltpu.make_async_copy(rows, rows_out, sem)
 
     @pl.when(seg == 0)
     def _():
         finish(z, product[...], (g0, b1, b2, b3), cov_noise, rows)
-        copy.start()
-
-    @pl.when(seg > 1)
-    def _():
-        rows[:, cols(z)] = own[:BLOCK, :BLOCK]
-        rows[:, cols(spot(z, 1))] = own[:BLOCK, BLOCK : 2 * BLOCK]
-        rows[:, cols(spot(z, 3))] = near[...].T
-
-        @pl.when(owns_far(z))
-        def _():
-            rows[:, cols(spot(z, 2))] = own[:BLOCK, 2 * BLOCK :]
-
-        @pl.when(jnp.logical_not(owns_far(z)))
-        def _():
-            rows[:, cols(spot(z, 2))] = far[...].T
-
         copy.start()
 
     mean = mean_1[0:1].astype(F32)
@@ -423,7 +421,7 @@
             result = (value[k, j : j + 1, :] - full[0, k : k + 1, at]) / full[1, k : k + 1, at]
             out[k, j : j + 1, :] = jnp.where(j < counts[k], result, 0.0)
 
-    @pl.when(seg != 1)
+    @pl.when(seg == 0)
     def _():
         copy.wait()
 
@@ -507,7 +505,13 @@
     back, two_on, on = ((1, 0), (2, 1), (3, 2), (0, 3)), ((0, 2), (1, 3), (2, 0), (3, 1)), ((0, 1), (1, 2), (2, 3), (3, 0))
     pair_gains = [route(gain, within((3, 2, 1), back)), route(gain, within((3, 2), ((2, 0), (1, 3))) + within((1,), on))]
     parcel = pack(pack_kernel, "pack", parcel_shape, (end_cov, noise), (end_mean, seg_offset), pltpu.SemaphoreType.DMA((3,)), ALL_VMEM)
-    first = [send(parcel, ((0 if a == 2 else 3, 3), (1, 1)), a) for a in range(1, RING)]
+    ups, downs = ((0, 1), (1, 2), (2, 3)), ((1, 0), (2, 1), (3, 2))
+    first = [
+        route(parcel, within((3,), downs) + within((1,), back)),
+        route(parcel, [((0, start), (3, to)) for start, to in two_on if to != 0] + within((1,), two_on)),
+        route(parcel, within((3,), ups) + within((1,), on)),
+    ]
+    handed = [route(first[0], within((3,), ((1, 0),))), route(first[1], within((3,), ((1, 0), (2, 3))))]
 
     def hand(segment, event):
         kernel = functools.partial(hand_kernel, segment)
@@ -520,7 +524,7 @@
         functools.partial(pairs_kernel, 3),
         "pairs_3",
         (*half_shapes, parcel_shape, mean_shape),
-        (gain, *pair_gains, noise, seg_offset, end_cov, end_mean, *first),
+        (gain, *pair_gains, noise, seg_offset, end_cov, end_mean, *first, *handed),
         full_and_mean + [pltpu.VMEM(parcel_shape.shape, BF16)],
         flops,
     )
@@ -573,21 +577,21 @@
         last_kernel,
         "last",
         (row_shape, mean_shape, row_shape),
-        (gain, *gains_1, ends_1, ends_0, lift, through, beside, noise, seg_offset, means),
+        (gain, *gains_1, ends_1, ends_0, lift, through, beside, noise, seg_offset, means, parcel_2, far, near),
         full_and_mean,
         flops,
     )
     innovation, out_mean, out_cov = pl.pallas_call(
         innovation_kernel,
         out_shape=(shape(obs_value.shape, F32), shape((1, BLOCK)), row_shape),
-        in_specs=[smem()] * 3 + [vmem()] * 18 + [pl.BlockSpec(memory_space=pl.ANY)],
+        in_specs=[smem()] * 3 + [vmem()] * 15 + [pl.BlockSpec(memory_space=pl.ANY)],
         out_specs=(vmem(), vmem(), pl.BlockSpec(memory_space=pl.ANY)),
         scratch_shapes=[pltpu.VMEM((2, steps, states), F32), pltpu.VMEM(row_shape.shape, BF16), pltpu.SemaphoreType.DMA],
-        input_output_aliases={21: 2},
+        input_output_aliases={18: 2},
         compiler_params=params(),
         cost_estimate=cost(0, 2e5),
         name="innovation",
-    )(where, obs_tiles.T, obs_count, *all_stats, obs_value, obs_noise.reshape(1, states), parcel_2, far, near, mean_1, mean_2, mean_3, product, gain, *gains_0, noise, rows)
+    )(where, obs_tiles.T, obs_count, *all_stats, obs_value, obs_noise.reshape(1, states), mean_1, mean_2, mean_3, product, gain, *gains_0, noise, rows)
     return out_cov[None], out_mean, step_mean, step_spread, innovation
 
 

time: 116 us -> 123 us (1.060)
  waiting for transfers between devices: 43.4 us -> 50.3 us
  starting transfers between devices: 39.6 us -> 41 us
    ppermute x25 -> x27, waiting for transfers between devices: 43.4 us -> 50.3 us  [route(): return lax.ppermute(block, ('tm', 'tile'), table)]
    ppermute x25 -> x27, starting transfers between devices: 39.6 us -> 41 us  [route(): return lax.ppermute(block, ('tm', 'tile'), table)]
  transfers between devices with their start and end apart: 25 -> 27, of which waited for: 4 -> 4; matrix products, arithmetic and copies ran while one was open for 1% -> 0% of each run, Pallas kernels for 22% -> 18%
where the time goes in v6:
time: 123 us
  waiting for transfers between devices  50.3 us (41%)
  starting transfers between devices  41 us (33%)
  Pallas kernels  29.2 us (24%)
  between operations  1.37 us (1%)
    ppermute x27, waiting for transfers between devices, route(): return lax.ppermute(block, ('tm', 'tile'), table)  50.3 us
    ppermute x27, starting transfers between devices, route(): return lax.ppermute(block, ('tm', 'tile'), table)  41 us
    pallas_call x7, Pallas kernels, call(): pl.pallas_call(kernel, out_shape=out_shape, in_specs=[smem()] + [vmem()]...  22.6 us
    pallas_call x3, Pallas kernels, pack(): pl.pallas_call(kernel, out_shape=out_shape, in_specs=[smem()] + [pl.Block...  3.8 us
    pallas_call x1, Pallas kernels, ring_shards(): pl.pallas_call(innovation_kernel, out_shape=(shape(obs_value.shape, F32),...  2.76 us
  transfers between devices with their start and end apart: 27, of which 4 were waited for; matrix products, arithmetic and copies ran while one was open for 0% of the time, Pallas kernels for 18%

profile of v6, /device:TPU:0, one launch (start us, length us, event | category | flops | bytes accessed | tf_op | source)
XLA Modules:
  0.0 123.0 jit_solution(4689653097289568148)
XLA Ops:
  0.7 0.6 pad_add_fusion.where
  1.3 0.0 copy-start.11
  1.3 2.7 %pack.1.n0 = bf16[272,768]{1,0:T(8,128)(2,1)} custom-call(s32[3]{0:T(128)} %pad_add_fusion.where, bf16[2,256,1024]{2,1,0:T(8,128)(2,1)} %refs_0_.1, bf16[256,1024]{1,0:T(8,128)(2,1)} %bitcast.18, bf16[2,256]{1,0:T(2,128)(2,1)} %refs_1_.1, f32[1,256]{1,0:T(1,128)} %offset.9), custom_call_target="tpu_custom_call" | custom-call | bytes 1000000 | tf_op jit(solution)/shard_map/pack/pallas_call | solution.py:490
  3.9 0.7 collective-permute-start.2
  4.6 7.7 %collective-permute-start.3 = (bf16[272,768]{1,0:T(8,128)(2,1)}, bf16[272,768]{1,0:T(8,128)(2,1)S(1)}, u32[]{:S(2)}, u32[]{:S(2)}) collective-permute-start(bf16[272,768]{1,0:T(8,128)(2,1)} %pack.1.n0), channel_id=1, source_target_pairs={{0,14},{1,15},{3,13},{4,6},{5,7},{6,4},{7,5},{16,30},{17,31},{19,2... | collective-permute-start | bytes 1253384 | tf_op jit(solution)/shard_map/ppermute | solution.py:463
  12.4 0.7 collective-permute-start
  13.1 0.7 collective-permute-start.1
  13.8 0.7 collective-permute-start.4
  14.5 0.0 collective-permute-done.2.refs_2_.n1
  14.5 0.7 collective-permute-start.5
  15.2 7.6 %collective-permute-done.3.refs_3_.event.n2 = bf16[272,768]{1,0:T(8,128)(2,1)S(1)} collective-permute-done((bf16[272,768]{1,0:T(8,128)(2,1)}, bf16[272,768]{1,0:T(8,128)(2,1)S(1)}, u32[]{:S(2)}, u32[]{:S(2)}) %collective-permute-start.3) | collective-permute-done | bytes 417824 | tf_op jit(solution)/shard_map/ppermute | solution.py:463
  22.8 0.7 collective-permute-start.6
  23.5 0.6 hand_1.1
  24.0 0.0 collective-permute-done.4.refs_4_.n3
  24.0 0.7 collective-permute-start.11
  24.7 0.0 collective-permute-done.g1.a1
  24.8 0.0 collective-permute-done.1.g2.g3.a3
  24.8 0.0 collective-permute-done.5.refs_5_
  24.8 0.6 pairs_3.1
  25.4 0.7 collective-permute-start.10
  26.1 0.7 collective-permute-start.7
  26.8 0.7 collective-permute-start.8
  27.5 0.7 collective-permute-start.9
  28.2 0.0 collective-permute-done.7.refs_0_
  28.2 0.0 collective-permute-done.8.refs_1_
  28.2 0.0 copy-start.4
  28.2 0.6 pairs_2.1
  28.8 0.0 collective-permute-done.11.g2.a2
  28.8 0.4 copy-done.4
  29.2 0.5 stack.17
  29.8 0.0 copy-start.3
  29.8 1.6 %collective-permute-start.12 = (bf16[2064,1024]{1,0:T(8,128)(2,1)S(1)}, bf16[2064,1024]{1,0:T(8,128)(2,1)S(1)}, u32[]{:S(2)}, u32[]{:S(2)}) collective-permute-start(bf16[2064,1024]{1,0:T(8,128)(2,1)S(1)} %stack.17), channel_id=1, source_target_pairs={{4,0},{5,1},{6,2},{7,3},{20,16},{21,17},{22,18},{23,19}} | collective-permute-start | bytes 12681224 | tf_op jit(solution)/shard_map/ppermute | solution.py:463
  31.4 0.7 collective-permute-start.18
  32.1 0.7 collective-permute-start.16
  32.7 0.7 collective-permute-start.17
  33.4 0.7 collective-permute-start.19
  34.1 0.7 collective-permute-start.20
  34.8 40.9 %collective-permute-done.12.event.lift = bf16[2064,1024]{1,0:T(8,128)(2,1)S(1)} collective-permute-done((bf16[2064,1024]{1,0:T(8,128)(2,1)S(1)}, bf16[2064,1024]{1,0:T(8,128)(2,1)S(1)}, u32[]{:S(2)}, u32[]{:S(2)}) %collective-permute-start.12) | collective-permute-done | bytes 4227104 | tf_op jit(solution)/shard_map/ppermute | solution.py:463
  75.7 0.6 hand_0.1.event
  76.3 1.9 %collective-permute-start.15 = (bf16[256,1024]{1,0:T(8,128)(2,1)S(1)}, bf16[256,1024]{1,0:T(8,128)(2,1)S(1)}, u32[]{:S(2)}, u32[]{:S(2)}) collective-permute-start(bf16[256,1024]{1,0:T(8,128)(2,1)S(1)} %hand_0.1.event), channel_id=1, source_target_pairs={{0,2},{1,3},{2,0},{3,1},{16,18},{17,19},{18,16},{19,17}} | collective-permute-start | bytes 1572872 | tf_op jit(solution)/shard_map/ppermute | solution.py:463
  78.3 11.0 %ahead.1 = (bf16[8,256,1024]{2,1,0:T(8,128)(2,1)S(1)}, f32[8,256]{1,0:T(8,128)S(1)}, bf16[256,1024]{1,0:T(8,128)(2,1)S(1)}, f32[256,1024]{1,0:T(8,128)S(1)}, bf1...) custom-call(s32[3]{0:T(128)S(1)} %copy-done.5, bf16[256,1024]{1,0:T(8,128)(2,1)S(1)} %hand_0.1.event, ...), custom_call_target="tpu_custom_call" | custom-call | flops 9663676416 | bytes 15769600 | tf_op jit(solution)/shard_map/ahead/pallas_call | solution.py:477
  89.3 0.7 collective-permute-start.13
  90.0 0.0 collective-permute-done.17.t1
  90.0 0.0 copy-start.8
  90.0 0.0 copy-start.9
  90.0 0.7 collective-permute-start.14
  90.7 0.0 collective-permute-done.19.t3
  90.7 0.0 collective-permute-done.20.t4
  90.7 0.0 collective-permute-done.14.far
  90.7 1.2 %collective-permute-done.15.b2 = bf16[256,1024]{1,0:T(8,128)(2,1)S(1)} collective-permute-done((bf16[256,1024]{1,0:T(8,128)(2,1)S(1)}, bf16[256,1024]{1,0:T(8,128)(2,1)S(1)}, u32[]{:S(2)}, u32[]{:S(2)}) %collective-permute-start.15) | collective-permute-done | bytes 524320 | tf_op jit(solution)/shard_map/ppermute | solution.py:463
  91.9 0.5 turn.1.ends_1
  92.5 1.3 %collective-permute-start.21 = (bf16[4,272,768]{2,1,0:T(8,128)(2,1)S(1)}, bf16[4,272,768]{2,1,0:T(8,128)(2,1)S(1)}, u32[]{:S(2)}, u32[]{:S(2)}) collective-permute-start(bf16[4,272,768]{2,1,0:T(8,128)(2,1)S(1)} %turn.1.ends_1), channel_id=1, source_target_pairs={{4,0},{5,1},{6,2},{7,3},{20,16},{21,17},{22,18},{23,19}} | collective-permute-start | bytes 5013512 | tf_op jit(solution)/shard_map/ppermute | solution.py:463
  93.8 4.9 %collective-permute-start.25 = (bf16[256,1024]{1,0:T(8,128)(2,1)S(1)}, bf16[256,1024]{1,0:T(8,128)(2,1)S(1)}, u32[]{:S(2)}, u32[]{:S(2)}) collective-permute-start(bf16[256,1024]{1,0:T(8,128)(2,1)S(1)} %hand_0.1.event), channel_id=1, source_target_pairs={{1,0},{2,1},{3,2},{0,3},{17,16},{18,17},{19,18},{16,19}} | collective-permute-start | bytes 1572872 | tf_op jit(solution)/shard_map/ppermute | solution.py:463
  98.7 1.9 %collective-permute-start.26 = (bf16[256,1024]{1,0:T(8,128)(2,1)S(1)}, bf16[256,1024]{1,0:T(8,128)(2,1)S(1)}, u32[]{:S(2)}, u32[]{:S(2)}) collective-permute-start(bf16[256,1024]{1,0:T(8,128)(2,1)S(1)} %hand_0.1.event), channel_id=1, source_target_pairs={{0,1},{1,2},{2,3},{3,0},{16,17},{17,18},{18,19},{19,16}} | collective-permute-start | bytes 1572872 | tf_op jit(solution)/shard_map/ppermute | solution.py:463
  100.7 0.5 collective-permute-done.21.ends_0
  101.2 5.9 %moments.1 = (bf16[4,768,256]{2,1,0:T(8,128)(2,1)S(1)}, bf16[16,1024]{1,0:T(8,128)(2,1)S(1)}, f32[8,256]{1,0:T(8,128)}, f32[8,256]{1,0:T(8,128)}, f32[2,8,256]{2,1,0:T(8,128)S(1)}) custom-call(s32[3]{0:T(128)S(1)} %copy-done.5, bf16[4,272,768]{2,1,0:T(8,128)(2,1)S(1)} %turn.1.ends_1, ...), custom_call_target="tpu_custom_call", output_to_operand_aliasing={{0}: (9, {}), {1}: (10, {})} | custom-call | flops 4294967296 | bytes 19226624 | tf_op jit(solution)/shard_map/moments/pallas_call | solution.py:477
  107.1 4.1 %collective-permute-start.22 = (f32[2,8,256]{2,1,0:T(8,128)S(1)}, f32[2,8,256]{2,1,0:T(8,128)S(1)}, u32[]{:S(2)}, u32[]{:S(2)}) collective-permute-start(f32[2,8,256]{2,1,0:T(8,128)S(1)} %get-tuple-element.43.s0), channel_id=1, source_target_pairs={{1,0},{2,1},{3,2},{0,3},{5,4},{6,5},{7,6},{4,7},{9,8},{10,9},{11,1... | collective-permute-start | bytes 49160 | tf_op jit(solution)/shard_map/ppermute | solution.py:463
  111.1 3.3 %collective-permute-start.23 = (f32[2,8,256]{2,1,0:T(8,128)S(1)}, f32[2,8,256]{2,1,0:T(8,128)S(1)}, u32[]{:S(2)}, u32[]{:S(2)}) collective-permute-start(f32[2,8,256]{2,1,0:T(8,128)S(1)} %get-tuple-element.43.s0), channel_id=1, source_target_pairs={{2,0},{3,1},{0,2},{1,3},{6,4},{7,5},{4,6},{5,7},{10,8},{11,9},{8,1... | collective-permute-start | bytes 49160 | tf_op jit(solution)/shard_map/ppermute | solution.py:463
  114.4 2.0 %collective-permute-start.24 = (f32[2,8,256]{2,1,0:T(8,128)S(1)}, f32[2,8,256]{2,1,0:T(8,128)S(1)}, u32[]{:S(2)}, u32[]{:S(2)}) collective-permute-start(f32[2,8,256]{2,1,0:T(8,128)S(1)} %get-tuple-element.43.s0), channel_id=1, source_target_pairs={{3,0},{0,1},{1,2},{2,3},{7,4},{4,5},{5,6},{6,7},{11,8},{8,9},{9,10... | collective-permute-start | bytes 49160 | tf_op jit(solution)/shard_map/ppermute | solution.py:463
  116.4 3.5 %last.1 = (bf16[256,1024]{1,0:T(8,128)(2,1)}, bf16[16,256]{1,0:T(8,128)(2,1)S(1)}, bf16[256,1024]{1,0:T(8,128)(2,1)S(1)}) custom-call(s32[3]{0:T(128)S(1)} %copy-done.5, bf16[256,1024]{1,0:T(8,128)(2,1)S(1)} %bitcast.16, bf16[256,1024]{1,0:T(8,128)(2,1)S(1)} %collective-permute-done.g1.a1, bf16[256,1024]{1,0:T(8,128)(2,1)S(1)} %collective-permute-done.11.g2.a2, ...), custom_call_target="tpu_custom_call" | custom-call | flops 1073741824 | bytes 13534208 | tf_op jit(solution)/shard_map/last/pallas_call | solution.py:477
  120.0 0.0 collective-permute-done.25.b1
  120.0 0.0 collective-permute-done.26.b3
  120.0 0.0 collective-permute-done.23.s2
  120.0 2.8 %innovation.1 = (f32[8,4,128]{2,1,0:T(4,128)}, bf16[1,256]{1,0:T(2,128)(2,1)}, bf16[256,1024]{1,0:T(8,128)(2,1)}) custom-call(s32[3]{0:T(128)S(1)} %copy-done.5, s32[4,8]{1,0:T(4,128)S(1)} %bitcast.24, s32[8]{0:T(128)S(1)} %copy-done.13, f32[2,8,256]{2,1,0:T(8,128)S(1)} %get-tuple-element.43.s0, ...), custom_call_target="tpu_custom_call", output_to_operand_aliasing={{2}: (18, {})} | custom-call | bytes 200000 | tf_op jit(solution)/shard_map/innovation/pallas_call | solution.py:584
  (30 shorter events, 0.1 us)
Async XLA Ops:
  0.6 11.7 %copy-start = (bf16[1,256,1024]{2,1,0:T(8,128)(2,1)S(1)}, bf16[1,256,1024]{2,1,0:T(8,128)(2,1)}, u32[]{:S(2)}) copy-start(bf16[1,256,1024]{2,1,0:T(8,128)(2,1)} %param.12) | copy-start | bytes 1572868
  1.2 22.2 %copy-start.5 = (s32[3]{0:T(128)S(1)}, s32[3]{0:T(128)}, u32[]{:S(2)}) copy-start(s32[3]{0:T(128)} %pad_add_fusion.where) | copy-start | bytes 40
  1.3 23.5 %copy-start.1 = (bf16[1,256,1024]{2,1,0:T(8,128)(2,1)S(1)}, bf16[1,256,1024]{2,1,0:T(8,128)(2,1)}, u32[]{:S(2)}) copy-start(bf16[1,256,1024]{2,1,0:T(8,128)(2,1)} %param.14) | copy-start | bytes 1572868
  1.3 23.5 %copy-start.2 = (bf16[2,256,1024]{2,1,0:T(8,128)(2,1)S(1)}, bf16[2,256,1024]{2,1,0:T(8,128)(2,1)}, u32[]{:S(2)}) copy-start(bf16[2,256,1024]{2,1,0:T(8,128)(2,1)} %refs_0_.1) | copy-start | bytes 3145732
  1.3 23.6 %copy-start.7 = (f32[1,256]{1,0:T(1,128)S(1)}, f32[1,256]{1,0:T(1,128)}, u32[]{:S(2)}) copy-start(f32[1,256]{1,0:T(1,128)} %offset.9) | copy-start | bytes 3076
  1.3 23.6 %copy-start.11 = (bf16[2,256]{1,0:T(2,128)(2,1)S(1)}, bf16[2,256]{1,0:T(2,128)(2,1)}, u32[]{:S(2)}) copy-start(bf16[2,256]{1,0:T(2,128)(2,1)} %refs_1_.1) | copy-start | bytes 3076
  3.9 10.5 %collective-permute-start.2 = (bf16[272,768]{1,0:T(8,128)(2,1)}, bf16[272,768]{1,0:T(8,128)(2,1)S(1)}, u32[]{:S(2)}, u32[]{:S(2)}) collective-permute-start(bf16[272,768]{1,0:T(8,128)(2,1)} %pack.1.n0), channel_id=1, source_target_pairs={{13,12},{14,13},{15,14},{5,4},{6,5},{7,6},{4,7},{29,28},{30,29},{3... | collective-permute-start | bytes 1253384 | tf_op jit(solution)/shard_map/ppermute | solution.py:463
  4.6 18.1 %collective-permute-start.3 = (bf16[272,768]{1,0:T(8,128)(2,1)}, bf16[272,768]{1,0:T(8,128)(2,1)S(1)}, u32[]{:S(2)}, u32[]{:S(2)}) collective-permute-start(bf16[272,768]{1,0:T(8,128)(2,1)} %pack.1.n0), channel_id=1, source_target_pairs={{0,14},{1,15},{3,13},{4,6},{5,7},{6,4},{7,5},{16,30},{17,31},{19,2... | collective-permute-start | bytes 1253384 | tf_op jit(solution)/shard_map/ppermute | solution.py:463
  12.4 12.4 %collective-permute-start = (bf16[256,1024]{1,0:T(8,128)(2,1)S(1)}, bf16[256,1024]{1,0:T(8,128)(2,1)S(1)}, u32[]{:S(2)}, u32[]{:S(2)}) collective-permute-start(bf16[256,1024]{1,0:T(8,128)(2,1)S(1)} %bitcast.8), channel_id=1, source_target_pairs={{13,12},{14,13},{15,14},{12,15},{9,8},{10,9},{11,10},{8,11},{5,4},... | collective-permute-start | bytes 1572872 | tf_op jit(solution)/shard_map/ppermute | solution.py:463
  13.1 11.7 %collective-permute-start.1 = (bf16[256,1024]{1,0:T(8,128)(2,1)S(1)}, bf16[256,1024]{1,0:T(8,128)(2,1)S(1)}, u32[]{:S(2)}, u32[]{:S(2)}) collective-permute-start(bf16[256,1024]{1,0:T(8,128)(2,1)S(1)} %bitcast.9), channel_id=1, source_target_pairs={{14,12},{13,15},{10,8},{9,11},{4,5},{5,6},{6,7},{7,4},{30,28},{29,... | collective-permute-start | bytes 1572872 | tf_op jit(solution)/shard_map/ppermute | solution.py:463
  13.8 10.3 %collective-permute-start.4 = (bf16[272,768]{1,0:T(8,128)(2,1)}, bf16[272,768]{1,0:T(8,128)(2,1)S(1)}, u32[]{:S(2)}, u32[]{:S(2)}) collective-permute-start(bf16[272,768]{1,0:T(8,128)(2,1)} %pack.1.n0), channel_id=1, source_target_pairs={{12,13},{13,14},{14,15},{4,5},{5,6},{6,7},{7,4},{28,29},{29,30},{3... | collective-permute-start | bytes 1253384 | tf_op jit(solution)/shard_map/ppermute | solution.py:463
  14.5 10.3 %collective-permute-start.5 = (bf16[272,768]{1,0:T(8,128)(2,1)S(1)}, bf16[272,768]{1,0:T(8,128)(2,1)S(1)}, u32[]{:S(2)}, u32[]{:S(2)}) collective-permute-start(bf16[272,768]{1,0:T(8,128)(2,1)S(1)} %collective-permute-done.2.refs_2_.n1), channel_id=1, source_target_pairs={{13,12},{29,28}} | collective-permute-start | bytes 1253384 | tf_op jit(solution)/shard_map/ppermute | solution.py:463
  22.8 2.0 %collective-permute-start.6 = (bf16[272,768]{1,0:T(8,128)(2,1)S(1)}, bf16[272,768]{1,0:T(8,128)(2,1)S(1)}, u32[]{:S(2)}, u32[]{:S(2)}) collective-permute-start(bf16[272,768]{1,0:T(8,128)(2,1)S(1)} %collective-permute-done.3.refs_3_.event.n2), channel_id=1, source_target_pairs={{13,12},{14,15},{29,28},{30,31}} | collective-permute-start | bytes 1253384 | tf_op jit(solution)/shard_map/ppermute | solution.py:463
  24.0 4.8 %collective-permute-start.11 = (bf16[256,1024]{1,0:T(8,128)(2,1)S(1)}, bf16[256,1024]{1,0:T(8,128)(2,1)S(1)}, u32[]{:S(2)}, u32[]{:S(2)}) collective-permute-start(bf16[256,1024]{1,0:T(8,128)(2,1)S(1)} %hand_1.1), channel_id=1, source_target_pairs={{4,6},{5,7},{6,4},{7,5},{20,22},{21,23},{22,20},{23,21}} | collective-permute-start | bytes 1572872 | tf_op jit(solution)/shard_map/ppermute | solution.py:463
  25.4 2.8 %collective-permute-start.10 = (bf16[272,768]{1,0:T(8,128)(2,1)S(1)}, bf16[272,768]{1,0:T(8,128)(2,1)S(1)}, u32[]{:S(2)}, u32[]{:S(2)}) collective-permute-start(bf16[272,768]{1,0:T(8,128)(2,1)S(1)} %get-tuple-element.31.refs_4_), channel_id=1, source_target_pairs={{15,8},{12,9},{13,10},{14,11},{31,24},{28,25},{29,26},{30,27}} | collective-permute-start | bytes 1253384 | tf_op jit(solution)/shard_map/ppermute | solution.py:463
  26.1 2.1 %collective-permute-start.7 = (bf16[272,768]{1,0:T(8,128)(2,1)S(1)}, bf16[272,768]{1,0:T(8,128)(2,1)S(1)}, u32[]{:S(2)}, u32[]{:S(2)}) collective-permute-start(bf16[272,768]{1,0:T(8,128)(2,1)S(1)} %get-tuple-element.31.refs_4_), channel_id=1, source_target_pairs={{12,8},{13,9},{14,10},{15,11},{28,24},{29,25},{30,26},{31,27}} | collective-permute-start | bytes 1253384 | tf_op jit(solution)/shard_map/ppermute | solution.py:463
  26.8 1.4 %collective-permute-start.8 = (bf16[272,768]{1,0:T(8,128)(2,1)S(1)}, bf16[272,768]{1,0:T(8,128)(2,1)S(1)}, u32[]{:S(2)}, u32[]{:S(2)}) collective-permute-start(bf16[272,768]{1,0:T(8,128)(2,1)S(1)} %get-tuple-element.31.refs_4_), channel_id=1, source_target_pairs={{13,8},{14,9},{15,10},{12,11},{29,24},{30,25},{31,26},{28,27}} | collective-permute-start | bytes 1253384 | tf_op jit(solution)/shard_map/ppermute | solution.py:463
  27.5 0.7 collective-permute-start.9
  28.2 1.0 copy-start.4
  29.8 48.5 %copy-start.3 = (bf16[8,256,1024]{2,1,0:T(8,128)(2,1)S(1)}, bf16[8,256,1024]{2,1,0:T(8,128)(2,1)}, u32[]{:S(2)}) copy-start(bf16[8,256,1024]{2,1,0:T(8,128)(2,1)} %gain.1) | copy-start | bytes 12582916
  29.8 45.9 %collective-permute-start.12 = (bf16[2064,1024]{1,0:T(8,128)(2,1)S(1)}, bf16[2064,1024]{1,0:T(8,128)(2,1)S(1)}, u32[]{:S(2)}, u32[]{:S(2)}) collective-permute-start(bf16[2064,1024]{1,0:T(8,128)(2,1)S(1)} %stack.17), channel_id=1, source_target_pairs={{4,0},{5,1},{6,2},{7,3},{20,16},{21,17},{22,18},{23,19}} | collective-permute-start | bytes 12681224 | tf_op jit(solution)/shard_map/ppermute | solution.py:463
  31.4 2.8 %collective-permute-start.18 = (bf16[272,768]{1,0:T(8,128)(2,1)S(1)}, bf16[272,768]{1,0:T(8,128)(2,1)S(1)}, u32[]{:S(2)}, u32[]{:S(2)}) collective-permute-start(bf16[272,768]{1,0:T(8,128)(2,1)S(1)} %get-tuple-element.34.event.own), channel_id=1, source_target_pairs={{10,4},{11,5},{8,6},{9,7},{26,20},{27,21},{24,22},{25,23}} | collective-permute-start | bytes 1253384 | tf_op jit(solution)/shard_map/ppermute | solution.py:463
  32.1 57.2 %collective-permute-start.16 = (bf16[272,768]{1,0:T(8,128)(2,1)S(1)}, bf16[272,768]{1,0:T(8,128)(2,1)S(1)}, u32[]{:S(2)}, u32[]{:S(2)}) collective-permute-start(bf16[272,768]{1,0:T(8,128)(2,1)S(1)} %get-tuple-element.34.event.own), channel_id=1, source_target_pairs={{8,4},{9,5},{10,6},{11,7},{24,20},{25,21},{26,22},{27,23}} | collective-permute-start | bytes 1253384 | tf_op jit(solution)/shard_map/ppermute | solution.py:463
  32.7 57.2 %collective-permute-start.17 = (bf16[272,768]{1,0:T(8,128)(2,1)S(1)}, bf16[272,768]{1,0:T(8,128)(2,1)S(1)}, u32[]{:S(2)}, u32[]{:S(2)}) collective-permute-start(bf16[272,768]{1,0:T(8,128)(2,1)S(1)} %get-tuple-element.34.event.own), channel_id=1, source_target_pairs={{9,4},{10,5},{11,6},{8,7},{25,20},{26,21},{27,22},{24,23}} | collective-permute-start | bytes 1253384 | tf_op jit(solution)/shard_map/ppermute | solution.py:463
  33.4 57.2 %collective-permute-start.19 = (bf16[272,768]{1,0:T(8,128)(2,1)S(1)}, bf16[272,768]{1,0:T(8,128)(2,1)S(1)}, u32[]{:S(2)}, u32[]{:S(2)}) collective-permute-start(bf16[272,768]{1,0:T(8,128)(2,1)S(1)} %get-tuple-element.34.event.own), channel_id=1, source_target_pairs={{8,5},{9,6},{10,7},{24,21},{25,22},{26,23}} | collective-permute-start | bytes 1253384 | tf_op jit(solution)/shard_map/ppermute | solution.py:463
  34.1 56.5 %collective-permute-start.20 = (bf16[272,768]{1,0:T(8,128)(2,1)S(1)}, bf16[272,768]{1,0:T(8,128)(2,1)S(1)}, u32[]{:S(2)}, u32[]{:S(2)}) collective-permute-start(bf16[272,768]{1,0:T(8,128)(2,1)S(1)} %collective-permute-done.18.t2), channel_id=1, source_target_pairs={{5,4},{21,20}} | collective-permute-start | bytes 1253384 | tf_op jit(solution)/shard_map/ppermute | solution.py:463
  76.3 15.6 %collective-permute-start.15 = (bf16[256,1024]{1,0:T(8,128)(2,1)S(1)}, bf16[256,1024]{1,0:T(8,128)(2,1)S(1)}, u32[]{:S(2)}, u32[]{:S(2)}) collective-permute-start(bf16[256,1024]{1,0:T(8,128)(2,1)S(1)} %hand_0.1.event), channel_id=1, source_target_pairs={{0,2},{1,3},{2,0},{3,1},{16,18},{17,19},{18,16},{19,17}} | collective-permute-start | bytes 1572872 | tf_op jit(solution)/shard_map/ppermute | solution.py:463
  89.3 1.4 %collective-permute-start.13 = (bf16[256,256]{1,0:T(8,128)(2,1)S(1)}, bf16[256,256]{1,0:T(8,128)(2,1)S(1)}, u32[]{:S(2)}, u32[]{:S(2)}) collective-permute-start(bf16[256,256]{1,0:T(8,128)(2,1)S(1)} %get-tuple-element.37), channel_id=1, source_target_pairs={{12,13},{13,14},{14,15},{15,12},{8,9},{9,10},{10,11},{11,8},{28,29... | collective-permute-start | bytes 393224 | tf_op jit(solution)/shard_map/ppermute | solution.py:463
  90.0 11.2 %copy-start.8 = (f32[8,256]{1,0:T(8,128)S(1)}, f32[8,256]{1,0:T(8,128)}, u32[]{:S(2)}) copy-start(f32[8,256]{1,0:T(8,128)} %offset.8) | copy-start | bytes 24580
  90.0 11.2 %copy-start.9 = (f32[8,256]{1,0:T(8,128)S(1)}, f32[8,256]{1,0:T(8,128)}, u32[]{:S(2)}) copy-start(f32[8,256]{1,0:T(8,128)} %var.1) | copy-start | bytes 24580
  90.0 0.7 collective-permute-start.14
  92.5 8.7 %collective-permute-start.21 = (bf16[4,272,768]{2,1,0:T(8,128)(2,1)S(1)}, bf16[4,272,768]{2,1,0:T(8,128)(2,1)S(1)}, u32[]{:S(2)}, u32[]{:S(2)}) collective-permute-start(bf16[4,272,768]{2,1,0:T(8,128)(2,1)S(1)} %turn.1.ends_1), channel_id=1, source_target_pairs={{4,0},{5,1},{6,2},{7,3},{20,16},{21,17},{22,18},{23,19}} | collective-permute-start | bytes 5013512 | tf_op jit(solution)/shard_map/ppermute | solution.py:463
  93.8 26.2 %collective-permute-start.25 = (bf16[256,1024]{1,0:T(8,128)(2,1)S(1)}, bf16[256,1024]{1,0:T(8,128)(2,1)S(1)}, u32[]{:S(2)}, u32[]{:S(2)}) collective-permute-start(bf16[256,1024]{1,0:T(8,128)(2,1)S(1)} %hand_0.1.event), channel_id=1, source_target_pairs={{1,0},{2,1},{3,2},{0,3},{17,16},{18,17},{19,18},{16,19}} | collective-permute-start | bytes 1572872 | tf_op jit(solution)/shard_map/ppermute | solution.py:463
  98.7 21.2 %collective-permute-start.26 = (bf16[256,1024]{1,0:T(8,128)(2,1)S(1)}, bf16[256,1024]{1,0:T(8,128)(2,1)S(1)}, u32[]{:S(2)}, u32[]{:S(2)}) collective-permute-start(bf16[256,1024]{1,0:T(8,128)(2,1)S(1)} %hand_0.1.event), channel_id=1, source_target_pairs={{0,1},{1,2},{2,3},{3,0},{16,17},{17,18},{18,19},{19,16}} | collective-permute-start | bytes 1572872 | tf_op jit(solution)/shard_map/ppermute | solution.py:463
  107.1 12.9 %collective-permute-start.22 = (f32[2,8,256]{2,1,0:T(8,128)S(1)}, f32[2,8,256]{2,1,0:T(8,128)S(1)}, u32[]{:S(2)}, u32[]{:S(2)}) collective-permute-start(f32[2,8,256]{2,1,0:T(8,128)S(1)} %get-tuple-element.43.s0), channel_id=1, source_target_pairs={{1,0},{2,1},{3,2},{0,3},{5,4},{6,5},{7,6},{4,7},{9,8},{10,9},{11,1... | collective-permute-start | bytes 49160 | tf_op jit(solution)/shard_map/ppermute | solution.py:463
  111.1 8.9 %collective-permute-start.23 = (f32[2,8,256]{2,1,0:T(8,128)S(1)}, f32[2,8,256]{2,1,0:T(8,128)S(1)}, u32[]{:S(2)}, u32[]{:S(2)}) collective-permute-start(f32[2,8,256]{2,1,0:T(8,128)S(1)} %get-tuple-element.43.s0), channel_id=1, source_target_pairs={{2,0},{3,1},{0,2},{1,3},{6,4},{7,5},{4,6},{5,7},{10,8},{11,9},{8,1... | collective-permute-start | bytes 49160 | tf_op jit(solution)/shard_map/ppermute | solution.py:463
  114.4 5.6 %collective-permute-start.24 = (f32[2,8,256]{2,1,0:T(8,128)S(1)}, f32[2,8,256]{2,1,0:T(8,128)S(1)}, u32[]{:S(2)}, u32[]{:S(2)}) collective-permute-start(f32[2,8,256]{2,1,0:T(8,128)S(1)} %get-tuple-element.43.s0), channel_id=1, source_target_pairs={{3,0},{0,1},{1,2},{2,3},{7,4},{4,5},{5,6},{6,7},{11,8},{8,9},{9,10... | collective-permute-start | bytes 49160 | tf_op jit(solution)/shard_map/ppermute | solution.py:463
  116.4 3.6 %copy-start.6 = (f32[8,4,128]{2,1,0:T(4,128)S(1)}, f32[8,4,128]{2,1,0:T(4,128)}, u32[]{:S(2)}) copy-start(f32[8,4,128]{2,1,0:T(4,128)} %value.1) | copy-start | bytes 49156
  116.4 3.6 %copy-start.10 = (f32[1024]{0:T(1024)S(1)}, f32[1024]{0:T(1024)}, u32[]{:S(2)}) copy-start(f32[1024]{0:T(1024)} %param.23) | copy-start | bytes 12292
  116.4 3.6 %copy-start.12 = (s32[8,4]{0,1:T(4,128)S(1)}, s32[8,4]{0,1:T(4,128)}, u32[]{:S(2)}) copy-start(s32[8,4]{0,1:T(4,128)} %param.20) | copy-start | bytes 388
  116.4 3.6 %copy-start.13 = (s32[8]{0:T(128)S(1)}, s32[8]{0:T(128)}, u32[]{:S(2)}) copy-start(s32[8]{0:T(128)} %counts.1) | copy-start | bytes 100

commit v7 on v6

--- a/solution.py
+++ b/solution.py
@@ -229,10 +229,11 @@
 def pairs_kernel(at_seg, where, g0, g1, g2, noise, offset, *refs):
     z, seg, group = where[0], where[1], where[2]
     if at_seg == GROUP_SEGS - 1:
-        end_cov, end_mean, p1, p2, p3, from_1, across, half, half_mean, parcel, mean_row, full, mean, own = refs
-        parcels = (own, (z < RING - 1, p1, across), (z > 0, p2, from_1), (z > 0, p3, across))
+        end_cov, end_mean, *others, half, half_mean, parcel, mean_row, full, mean, own = refs
+        parcels = (own, *others)
     else:
-        *parcels, early, _, _, half, half_mean, parcel, mean_row, beside, far, full, mean = refs
+        p2, p1, p3, p0, early, _, _, half, half_mean, parcel, mean_row, beside, far, full, mean = refs
+        parcels = (p0, p1, p2, p3)
 
     @pl.when(seg == at_seg)
     def _():
@@ -279,7 +280,7 @@
         lay_out(z, (n0, n1, n2, n3), lift.at[pl.ds(states, states)], lift.at[pl.ds(2 * states, TAIL)])
 
 
-def turn_kernel(where, near, far, b2, t0, t1, t2, t3, t4, out):
+def turn_kernel(where, near, far, b2, t2, t1, t3, t4, t0, out):
     def body(a, parcel):
         out[a] = parcel[...]
 
@@ -505,13 +506,7 @@
     back, two_on, on = ((1, 0), (2, 1), (3, 2), (0, 3)), ((0, 2), (1, 3), (2, 0), (3, 1)), ((0, 1), (1, 2), (2, 3), (3, 0))
     pair_gains = [route(gain, within((3, 2, 1), back)), route(gain, within((3, 2), ((2, 0), (1, 3))) + within((1,), on))]
     parcel = pack(pack_kernel, "pack", parcel_shape, (end_cov, noise), (end_mean, seg_offset), pltpu.SemaphoreType.DMA((3,)), ALL_VMEM)
-    ups, downs = ((0, 1), (1, 2), (2, 3)), ((1, 0), (2, 1), (3, 2))
-    first = [
-        route(parcel, within((3,), downs) + within((1,), back)),
-        route(parcel, [((0, start), (3, to)) for start, to in two_on if to != 0] + within((1,), two_on)),
-        route(parcel, within((3,), ups) + within((1,), on)),
-    ]
-    handed = [route(first[0], within((3,), ((1, 0),))), route(first[1], within((3,), ((1, 0), (2, 3))))]
+    first = [send(parcel, ((0 if a == 2 else 3, 3), (1, 1)), a) for a in range(1, RING)]
 
     def hand(segment, event):
         kernel = functools.partial(hand_kernel, segment)
@@ -524,7 +519,7 @@
         functools.partial(pairs_kernel, 3),
         "pairs_3",
         (*half_shapes, parcel_shape, mean_shape),
-        (gain, *pair_gains, noise, seg_offset, end_cov, end_mean, *first, *handed),
+        (gain, *pair_gains, noise, seg_offset, end_cov, end_mean, *first),
         full_and_mean + [pltpu.VMEM(parcel_shape.shape, BF16)],
         flops,
     )
@@ -534,7 +529,7 @@
         functools.partial(pairs_kernel, 2),
         "pairs_2",
         (*half_shapes, parcel_shape, mean_shape, block_shape, block_shape),
-        (gain, *pair_gains, noise, seg_offset, *second, parcel_3, *kept),
+        (gain, *pair_gains, noise, seg_offset, second[2], second[1], second[3], second[0], parcel_3, *kept),
         full_and_mean,
         flops,
         {11: 0, 12: 1},
@@ -559,7 +554,7 @@
     )
     gains_0 = [route(gain_0, within((0,), moves)) for moves in (back, two_on, on)]
     near, far = route(beside_block, within((3, 2), on)), route(far_block, within((3, 2), ((0, 2), (3, 1))))
-    (ends_1,) = call(turn_kernel, "turn", (shape((RING, *parcel_shape.shape)),), (near, far, gains_0[1], *third), [], 0)
+    (ends_1,) = call(turn_kernel, "turn", (shape((RING, *parcel_shape.shape)),), (near, far, gains_0[1], third[2], third[1], third[3], third[4], third[0]), [], 0)
     ends_0 = send(ends_1, ((1, 0),), 0)
     out_steps = shape((steps, BLOCK), F32)
     _, means, step_mean, step_spread, stats = call(

time: 123 us -> 114 us (0.927)
  waiting for transfers between devices: 50.3 us -> 42.4 us
  starting transfers between devices: 41 us -> 39.4 us
    ppermute x27 -> x25, waiting for transfers between devices: 50.3 us -> 42.4 us  [route(): return lax.ppermute(block, ('tm', 'tile'), table)]
    ppermute x27 -> x25, starting transfers between devices: 41 us -> 39.4 us  [route(): return lax.ppermute(block, ('tm', 'tile'), table)]
  transfers between devices with their start and end apart: 27 -> 25, of which waited for: 4 -> 4; matrix products, arithmetic and copies ran while one was open for 0% -> 1% of each run, Pallas kernels for 18% -> 22%
where the time goes in v7:
time: 114 us
  waiting for transfers between devices  42.4 us (37%)
  starting transfers between devices  39.4 us (35%)
  Pallas kernels  29.4 us (26%)
  between operations  1.33 us (1%)
    ppermute x25, waiting for transfers between devices, route(): return lax.ppermute(block, ('tm', 'tile'), table)  42.4 us
    ppermute x25, starting transfers between devices, route(): return lax.ppermute(block, ('tm', 'tile'), table)  39.4 us
    pallas_call x7, Pallas kernels, call(): pl.pallas_call(kernel, out_shape=out_shape, in_specs=[smem()] + [vmem()]...  22.8 us
    pallas_call x3, Pallas kernels, pack(): pl.pallas_call(kernel, out_shape=out_shape, in_specs=[smem()] + [pl.Block...  3.8 us
    pallas_call x1, Pallas kernels, ring_shards(): pl.pallas_call(innovation_kernel, out_shape=(shape(obs_value.shape, F32),...  2.76 us
  transfers between devices with their start and end apart: 25, of which 4 were waited for; matrix products, arithmetic and copies ran while one was open for 1% of the time, Pallas kernels for 22%

profile of v7, /device:TPU:0, one launch (start us, length us, event | category | flops | bytes accessed | tf_op | source)
XLA Modules:
  0.0 113.6 jit_solution(14715889024100686915)
XLA Ops:
  0.6 0.8 collective-permute-start
  1.5 0.7 collective-permute-start.1
  2.2 0.6 pad_add_fusion.where
  2.8 0.0 copy-start.11
  2.8 2.7 %pack.1.n0 = bf16[272,768]{1,0:T(8,128)(2,1)} custom-call(s32[3]{0:T(128)} %pad_add_fusion.where, bf16[2,256,1024]{2,1,0:T(8,128)(2,1)} %refs_0_.1, bf16[256,1024]{1,0:T(8,128)(2,1)} %bitcast.18, bf16[2,256]{1,0:T(2,128)(2,1)} %refs_1_.1, f32[1,256]{1,0:T(1,128)} %offset.9), custom_call_target="tpu_custom_call" | custom-call | bytes 1000000 | tf_op jit(solution)/shard_map/pack/pallas_call | solution.py:491
  5.5 12.2 %collective-permute-start.3 = (bf16[272,768]{1,0:T(8,128)(2,1)}, bf16[272,768]{1,0:T(8,128)(2,1)S(1)}, u32[]{:S(2)}, u32[]{:S(2)}) collective-permute-start(bf16[272,768]{1,0:T(8,128)(2,1)} %pack.1.n0), channel_id=1, source_target_pairs={{2,12},{3,13},{0,14},{1,15},{6,4},{7,5},{4,6},{5,7},{18,28},{19,29... | collective-permute-start | bytes 1253384 | tf_op jit(solution)/shard_map/ppermute | solution.py:464
  17.6 0.7 collective-permute-start.2
  18.3 0.7 collective-permute-start.4
  19.0 9.0 %collective-permute-done.3.refs_3_.event.n2 = bf16[272,768]{1,0:T(8,128)(2,1)S(1)} collective-permute-done((bf16[272,768]{1,0:T(8,128)(2,1)}, bf16[272,768]{1,0:T(8,128)(2,1)S(1)}, u32[]{:S(2)}, u32[]{:S(2)}) %collective-permute-start.3) | collective-permute-done | bytes 417824 | tf_op jit(solution)/shard_map/ppermute | solution.py:464
  28.1 0.6 hand_1.1
  28.6 0.7 collective-permute-start.9
  29.3 0.0 collective-permute-done.2.refs_2_.n1
  29.3 0.0 collective-permute-done.4.refs_4_.n3
  29.3 0.0 collective-permute-done.g1.a1
  29.4 0.0 collective-permute-done.1.g2.g3.a3
  29.4 0.6 pairs_3.1
  30.0 0.7 collective-permute-start.5
  30.7 0.7 collective-permute-start.6
  31.4 0.7 collective-permute-start.7
  32.1 0.7 collective-permute-start.8
  32.8 0.0 collective-permute-done.5.refs_0_
  32.8 0.0 collective-permute-done.6.refs_1_
  32.8 0.0 collective-permute-done.7.refs_2_
  32.8 0.0 collective-permute-done.8.refs_3_
  32.8 0.0 copy-start.4
  32.8 0.6 pairs_2.1
  33.4 0.0 collective-permute-done.9.g2.a2
  33.4 0.4 copy-done.4
  33.8 0.5 stack.17
  34.4 0.0 copy-start.3
  34.4 1.6 %collective-permute-start.10 = (bf16[2064,1024]{1,0:T(8,128)(2,1)S(1)}, bf16[2064,1024]{1,0:T(8,128)(2,1)S(1)}, u32[]{:S(2)}, u32[]{:S(2)}) collective-permute-start(bf16[2064,1024]{1,0:T(8,128)(2,1)S(1)} %stack.17), channel_id=1, source_target_pairs={{4,0},{5,1},{6,2},{7,3},{20,16},{21,17},{22,18},{23,19}} | collective-permute-start | bytes 12681224 | tf_op jit(solution)/shard_map/ppermute | solution.py:464
  35.9 0.7 collective-permute-start.14
  36.6 0.7 collective-permute-start.15
  37.3 0.7 collective-permute-start.16
  38.0 0.7 collective-permute-start.18
  38.7 0.0 collective-permute-done.14.t2
  38.7 0.7 collective-permute-start.17
  39.4 29.3 %collective-permute-done.10.event.lift = bf16[2064,1024]{1,0:T(8,128)(2,1)S(1)} collective-permute-done((bf16[2064,1024]{1,0:T(8,128)(2,1)S(1)}, bf16[2064,1024]{1,0:T(8,128)(2,1)S(1)}, u32[]{:S(2)}, u32[]{:S(2)}) %collective-permute-start.10) | collective-permute-done | bytes 4227104 | tf_op jit(solution)/shard_map/ppermute | solution.py:464
  68.8 0.6 hand_0.1.event
  69.3 1.9 %collective-permute-start.13 = (bf16[256,1024]{1,0:T(8,128)(2,1)S(1)}, bf16[256,1024]{1,0:T(8,128)(2,1)S(1)}, u32[]{:S(2)}, u32[]{:S(2)}) collective-permute-start(bf16[256,1024]{1,0:T(8,128)(2,1)S(1)} %hand_0.1.event), channel_id=1, source_target_pairs={{0,2},{1,3},{2,0},{3,1},{16,18},{17,19},{18,16},{19,17}} | collective-permute-start | bytes 1572872 | tf_op jit(solution)/shard_map/ppermute | solution.py:464
  71.3 11.0 %ahead.1 = (bf16[8,256,1024]{2,1,0:T(8,128)(2,1)S(1)}, f32[8,256]{1,0:T(8,128)S(1)}, bf16[256,1024]{1,0:T(8,128)(2,1)S(1)}, f32[256,1024]{1,0:T(8,128)S(1)}, bf1...) custom-call(s32[3]{0:T(128)S(1)} %copy-done.5, bf16[256,1024]{1,0:T(8,128)(2,1)S(1)} %hand_0.1.event, ...), custom_call_target="tpu_custom_call" | custom-call | flops 9663676416 | bytes 15769600 | tf_op jit(solution)/shard_map/ahead/pallas_call | solution.py:478
  82.3 0.0 collective-permute-done.15.t1
  82.3 0.7 collective-permute-start.11
  83.0 0.0 collective-permute-done.16.t3
  83.0 0.0 copy-start.8
  83.0 0.0 copy-start.9
  83.0 0.7 collective-permute-start.12
  83.7 0.0 collective-permute-done.18.t0
  83.7 0.0 collective-permute-done.11.near
  83.7 0.0 collective-permute-done.12.far
  83.8 2.5 %collective-permute-done.13.b2 = bf16[256,1024]{1,0:T(8,128)(2,1)S(1)} collective-permute-done((bf16[256,1024]{1,0:T(8,128)(2,1)S(1)}, bf16[256,1024]{1,0:T(8,128)(2,1)S(1)}, u32[]{:S(2)}, u32[]{:S(2)}) %collective-permute-start.13) | collective-permute-done | bytes 524320 | tf_op jit(solution)/shard_map/ppermute | solution.py:464
  86.3 0.5 turn.1.ends_1
  86.8 1.3 %collective-permute-start.19 = (bf16[4,272,768]{2,1,0:T(8,128)(2,1)S(1)}, bf16[4,272,768]{2,1,0:T(8,128)(2,1)S(1)}, u32[]{:S(2)}, u32[]{:S(2)}) collective-permute-start(bf16[4,272,768]{2,1,0:T(8,128)(2,1)S(1)} %turn.1.ends_1), channel_id=1, source_target_pairs={{4,0},{5,1},{6,2},{7,3},{20,16},{21,17},{22,18},{23,19}} | collective-permute-start | bytes 5013512 | tf_op jit(solution)/shard_map/ppermute | solution.py:464
  88.1 3.5 %collective-permute-start.23 = (bf16[256,1024]{1,0:T(8,128)(2,1)S(1)}, bf16[256,1024]{1,0:T(8,128)(2,1)S(1)}, u32[]{:S(2)}, u32[]{:S(2)}) collective-permute-start(bf16[256,1024]{1,0:T(8,128)(2,1)S(1)} %hand_0.1.event), channel_id=1, source_target_pairs={{1,0},{2,1},{3,2},{0,3},{17,16},{18,17},{19,18},{16,19}} | collective-permute-start | bytes 1572872 | tf_op jit(solution)/shard_map/ppermute | solution.py:464
  91.6 2.3 %collective-permute-start.24 = (bf16[256,1024]{1,0:T(8,128)(2,1)S(1)}, bf16[256,1024]{1,0:T(8,128)(2,1)S(1)}, u32[]{:S(2)}, u32[]{:S(2)}) collective-permute-start(bf16[256,1024]{1,0:T(8,128)(2,1)S(1)} %hand_0.1.event), channel_id=1, source_target_pairs={{0,1},{1,2},{2,3},{3,0},{16,17},{17,18},{18,19},{19,16}} | collective-permute-start | bytes 1572872 | tf_op jit(solution)/shard_map/ppermute | solution.py:464
  94.0 1.5 %collective-permute-done.19.ends_0 = bf16[4,272,768]{2,1,0:T(8,128)(2,1)S(1)} collective-permute-done((bf16[4,272,768]{2,1,0:T(8,128)(2,1)S(1)}, bf16[4,272,768]{2,1,0:T(8,128)(2,1)S(1)}, u32[]{:S(2)}, u32[]{:S(2)}) %collective-permute-start.19) | collective-permute-done | bytes 1671200 | tf_op jit(solution)/shard_map/ppermute | solution.py:464
  95.5 6.1 %moments.1 = (bf16[4,768,256]{2,1,0:T(8,128)(2,1)S(1)}, bf16[16,1024]{1,0:T(8,128)(2,1)S(1)}, f32[8,256]{1,0:T(8,128)}, f32[8,256]{1,0:T(8,128)}, f32[2,8,256]{2,1,0:T(8,128)S(1)}) custom-call(s32[3]{0:T(128)S(1)} %copy-done.5, bf16[4,272,768]{2,1,0:T(8,128)(2,1)S(1)} %turn.1.ends_1, ...), custom_call_target="tpu_custom_call", output_to_operand_aliasing={{0}: (9, {}), {1}: (10, {})} | custom-call | flops 4294967296 | bytes 19226624 | tf_op jit(solution)/shard_map/moments/pallas_call | solution.py:478
  101.5 3.1 %collective-permute-start.20 = (f32[2,8,256]{2,1,0:T(8,128)S(1)}, f32[2,8,256]{2,1,0:T(8,128)S(1)}, u32[]{:S(2)}, u32[]{:S(2)}) collective-permute-start(f32[2,8,256]{2,1,0:T(8,128)S(1)} %get-tuple-element.43.s0), channel_id=1, source_target_pairs={{1,0},{2,1},{3,2},{0,3},{5,4},{6,5},{7,6},{4,7},{9,8},{10,9},{11,1... | collective-permute-start | bytes 49160 | tf_op jit(solution)/shard_map/ppermute | solution.py:464
  104.6 0.4 collective-permute-start.21
  105.0 2.0 %collective-permute-start.22 = (f32[2,8,256]{2,1,0:T(8,128)S(1)}, f32[2,8,256]{2,1,0:T(8,128)S(1)}, u32[]{:S(2)}, u32[]{:S(2)}) collective-permute-start(f32[2,8,256]{2,1,0:T(8,128)S(1)} %get-tuple-element.43.s0), channel_id=1, source_target_pairs={{3,0},{0,1},{1,2},{2,3},{7,4},{4,5},{5,6},{6,7},{11,8},{8,9},{9,10... | collective-permute-start | bytes 49160 | tf_op jit(solution)/shard_map/ppermute | solution.py:464
  107.1 3.5 %last.1 = (bf16[256,1024]{1,0:T(8,128)(2,1)}, bf16[16,256]{1,0:T(8,128)(2,1)S(1)}, bf16[256,1024]{1,0:T(8,128)(2,1)S(1)}) custom-call(s32[3]{0:T(128)S(1)} %copy-done.5, bf16[256,1024]{1,0:T(8,128)(2,1)S(1)} %bitcast.16, bf16[256,1024]{1,0:T(8,128)(2,1)S(1)} %collective-permute-done.g1.a1, bf16[256,1024]{1,0:T(8,128)(2,1)S(1)} %collective-permute-done.9.g2.a2, ...), custom_call_target="tpu_custom_call" | custom-call | flops 1073741824 | bytes 13534208 | tf_op jit(solution)/shard_map/last/pallas_call | solution.py:478
  110.6 0.0 collective-permute-done.23.b1
  110.6 0.0 collective-permute-done.21.s2
  110.7 2.8 %innovation.1 = (f32[8,4,128]{2,1,0:T(4,128)}, bf16[1,256]{1,0:T(2,128)(2,1)}, bf16[256,1024]{1,0:T(8,128)(2,1)}) custom-call(s32[3]{0:T(128)S(1)} %copy-done.5, s32[4,8]{1,0:T(4,128)S(1)} %bitcast.24, s32[8]{0:T(128)S(1)} %copy-done.13, f32[2,8,256]{2,1,0:T(8,128)S(1)} %get-tuple-element.43.s0, ...), custom_call_target="tpu_custom_call", output_to_operand_aliasing={{2}: (18, {})} | custom-call | bytes 200000 | tf_op jit(solution)/shard_map/innovation/pallas_call | solution.py:579
  (26 shorter events, 0.1 us)
Async XLA Ops:
  0.6 27.4 %copy-start = (bf16[1,256,1024]{2,1,0:T(8,128)(2,1)S(1)}, bf16[1,256,1024]{2,1,0:T(8,128)(2,1)}, u32[]{:S(2)}) copy-start(bf16[1,256,1024]{2,1,0:T(8,128)(2,1)} %param.12) | copy-start | bytes 1572868
  0.6 28.7 %collective-permute-start = (bf16[256,1024]{1,0:T(8,128)(2,1)}, bf16[256,1024]{1,0:T(8,128)(2,1)S(1)}, u32[]{:S(2)}, u32[]{:S(2)}) collective-permute-start(bf16[256,1024]{1,0:T(8,128)(2,1)} %bitcast.8), channel_id=1, source_target_pairs={{13,12},{14,13},{15,14},{12,15},{9,8},{10,9},{11,10},{8,11},{5,4},... | collective-permute-start | bytes 1572872 | tf_op jit(solution)/shard_map/ppermute | solution.py:464
  1.5 27.9 %collective-permute-start.1 = (bf16[256,1024]{1,0:T(8,128)(2,1)}, bf16[256,1024]{1,0:T(8,128)(2,1)S(1)}, u32[]{:S(2)}, u32[]{:S(2)}) collective-permute-start(bf16[256,1024]{1,0:T(8,128)(2,1)} %bitcast.9), channel_id=1, source_target_pairs={{14,12},{13,15},{10,8},{9,11},{4,5},{5,6},{6,7},{7,4},{30,28},{29,... | collective-permute-start | bytes 1572872 | tf_op jit(solution)/shard_map/ppermute | solution.py:464
  2.8 25.3 %copy-start.5 = (s32[3]{0:T(128)S(1)}, s32[3]{0:T(128)}, u32[]{:S(2)}) copy-start(s32[3]{0:T(128)} %pad_add_fusion.where) | copy-start | bytes 40
  2.8 26.6 %copy-start.1 = (bf16[1,256,1024]{2,1,0:T(8,128)(2,1)S(1)}, bf16[1,256,1024]{2,1,0:T(8,128)(2,1)}, u32[]{:S(2)}) copy-start(bf16[1,256,1024]{2,1,0:T(8,128)(2,1)} %param.14) | copy-start | bytes 1572868
  2.8 26.6 %copy-start.2 = (bf16[2,256,1024]{2,1,0:T(8,128)(2,1)S(1)}, bf16[2,256,1024]{2,1,0:T(8,128)(2,1)}, u32[]{:S(2)}) copy-start(bf16[2,256,1024]{2,1,0:T(8,128)(2,1)} %refs_0_.1) | copy-start | bytes 3145732
  2.8 26.6 %copy-start.7 = (f32[1,256]{1,0:T(1,128)S(1)}, f32[1,256]{1,0:T(1,128)}, u32[]{:S(2)}) copy-start(f32[1,256]{1,0:T(1,128)} %offset.9) | copy-start | bytes 3076
  2.8 26.6 %copy-start.11 = (bf16[2,256]{1,0:T(2,128)(2,1)S(1)}, bf16[2,256]{1,0:T(2,128)(2,1)}, u32[]{:S(2)}) copy-start(bf16[2,256]{1,0:T(2,128)(2,1)} %refs_1_.1) | copy-start | bytes 3076
  5.5 22.6 %collective-permute-start.3 = (bf16[272,768]{1,0:T(8,128)(2,1)}, bf16[272,768]{1,0:T(8,128)(2,1)S(1)}, u32[]{:S(2)}, u32[]{:S(2)}) collective-permute-start(bf16[272,768]{1,0:T(8,128)(2,1)} %pack.1.n0), channel_id=1, source_target_pairs={{2,12},{3,13},{0,14},{1,15},{6,4},{7,5},{4,6},{5,7},{18,28},{19,29... | collective-permute-start | bytes 1253384 | tf_op jit(solution)/shard_map/ppermute | solution.py:464
  17.6 11.7 %collective-permute-start.2 = (bf16[272,768]{1,0:T(8,128)(2,1)}, bf16[272,768]{1,0:T(8,128)(2,1)S(1)}, u32[]{:S(2)}, u32[]{:S(2)}) collective-permute-start(bf16[272,768]{1,0:T(8,128)(2,1)} %pack.1.n0), channel_id=1, source_target_pairs={{13,12},{14,13},{15,14},{12,15},{5,4},{6,5},{7,6},{4,7},{29,28},{3... | collective-permute-start | bytes 1253384 | tf_op jit(solution)/shard_map/ppermute | solution.py:464
  18.3 11.0 %collective-permute-start.4 = (bf16[272,768]{1,0:T(8,128)(2,1)}, bf16[272,768]{1,0:T(8,128)(2,1)S(1)}, u32[]{:S(2)}, u32[]{:S(2)}) collective-permute-start(bf16[272,768]{1,0:T(8,128)(2,1)} %pack.1.n0), channel_id=1, source_target_pairs={{15,12},{12,13},{13,14},{14,15},{7,4},{4,5},{5,6},{6,7},{31,28},{2... | collective-permute-start | bytes 1253384 | tf_op jit(solution)/shard_map/ppermute | solution.py:464
  28.6 4.8 %collective-permute-start.9 = (bf16[256,1024]{1,0:T(8,128)(2,1)S(1)}, bf16[256,1024]{1,0:T(8,128)(2,1)S(1)}, u32[]{:S(2)}, u32[]{:S(2)}) collective-permute-start(bf16[256,1024]{1,0:T(8,128)(2,1)S(1)} %hand_1.1), channel_id=1, source_target_pairs={{4,6},{5,7},{6,4},{7,5},{20,22},{21,23},{22,20},{23,21}} | collective-permute-start | bytes 1572872 | tf_op jit(solution)/shard_map/ppermute | solution.py:464
  30.0 2.8 %collective-permute-start.5 = (bf16[272,768]{1,0:T(8,128)(2,1)S(1)}, bf16[272,768]{1,0:T(8,128)(2,1)S(1)}, u32[]{:S(2)}, u32[]{:S(2)}) collective-permute-start(bf16[272,768]{1,0:T(8,128)(2,1)S(1)} %get-tuple-element.31.refs_4_), channel_id=1, source_target_pairs={{14,8},{15,9},{12,10},{13,11},{30,24},{31,25},{28,26},{29,27}} | collective-permute-start | bytes 1253384 | tf_op jit(solution)/shard_map/ppermute | solution.py:464
  30.7 2.1 %collective-permute-start.6 = (bf16[272,768]{1,0:T(8,128)(2,1)S(1)}, bf16[272,768]{1,0:T(8,128)(2,1)S(1)}, u32[]{:S(2)}, u32[]{:S(2)}) collective-permute-start(bf16[272,768]{1,0:T(8,128)(2,1)S(1)} %get-tuple-element.31.refs_4_), channel_id=1, source_target_pairs={{13,8},{14,9},{15,10},{12,11},{29,24},{30,25},{31,26},{28,27}} | collective-permute-start | bytes 1253384 | tf_op jit(solution)/shard_map/ppermute | solution.py:464
  31.4 1.4 %collective-permute-start.7 = (bf16[272,768]{1,0:T(8,128)(2,1)S(1)}, bf16[272,768]{1,0:T(8,128)(2,1)S(1)}, u32[]{:S(2)}, u32[]{:S(2)}) collective-permute-start(bf16[272,768]{1,0:T(8,128)(2,1)S(1)} %get-tuple-element.31.refs_4_), channel_id=1, source_target_pairs={{15,8},{12,9},{13,10},{14,11},{31,24},{28,25},{29,26},{30,27}} | collective-permute-start | bytes 1253384 | tf_op jit(solution)/shard_map/ppermute | solution.py:464
  32.1 0.7 collective-permute-start.8
  32.8 1.0 copy-start.4
  34.4 36.9 %copy-start.3 = (bf16[8,256,1024]{2,1,0:T(8,128)(2,1)S(1)}, bf16[8,256,1024]{2,1,0:T(8,128)(2,1)}, u32[]{:S(2)}) copy-start(bf16[8,256,1024]{2,1,0:T(8,128)(2,1)} %gain.1) | copy-start | bytes 12582916
  34.4 34.4 %collective-permute-start.10 = (bf16[2064,1024]{1,0:T(8,128)(2,1)S(1)}, bf16[2064,1024]{1,0:T(8,128)(2,1)S(1)}, u32[]{:S(2)}, u32[]{:S(2)}) collective-permute-start(bf16[2064,1024]{1,0:T(8,128)(2,1)S(1)} %stack.17), channel_id=1, source_target_pairs={{4,0},{5,1},{6,2},{7,3},{20,16},{21,17},{22,18},{23,19}} | collective-permute-start | bytes 12681224 | tf_op jit(solution)/shard_map/ppermute | solution.py:464
  35.9 2.8 %collective-permute-start.14 = (bf16[272,768]{1,0:T(8,128)(2,1)S(1)}, bf16[272,768]{1,0:T(8,128)(2,1)S(1)}, u32[]{:S(2)}, u32[]{:S(2)}) collective-permute-start(bf16[272,768]{1,0:T(8,128)(2,1)S(1)} %get-tuple-element.34.event.own), channel_id=1, source_target_pairs={{10,4},{11,5},{8,6},{9,7},{26,20},{27,21},{24,22},{25,23}} | collective-permute-start | bytes 1253384 | tf_op jit(solution)/shard_map/ppermute | solution.py:464
  36.6 45.7 %collective-permute-start.15 = (bf16[272,768]{1,0:T(8,128)(2,1)S(1)}, bf16[272,768]{1,0:T(8,128)(2,1)S(1)}, u32[]{:S(2)}, u32[]{:S(2)}) collective-permute-start(bf16[272,768]{1,0:T(8,128)(2,1)S(1)} %get-tuple-element.34.event.own), channel_id=1, source_target_pairs={{9,4},{10,5},{11,6},{8,7},{25,20},{26,21},{27,22},{24,23}} | collective-permute-start | bytes 1253384 | tf_op jit(solution)/shard_map/ppermute | solution.py:464
  37.3 45.7 %collective-permute-start.16 = (bf16[272,768]{1,0:T(8,128)(2,1)S(1)}, bf16[272,768]{1,0:T(8,128)(2,1)S(1)}, u32[]{:S(2)}, u32[]{:S(2)}) collective-permute-start(bf16[272,768]{1,0:T(8,128)(2,1)S(1)} %get-tuple-element.34.event.own), channel_id=1, source_target_pairs={{8,5},{9,6},{10,7},{24,21},{25,22},{26,23}} | collective-permute-start | bytes 1253384 | tf_op jit(solution)/shard_map/ppermute | solution.py:464
  38.0 45.7 %collective-permute-start.18 = (bf16[272,768]{1,0:T(8,128)(2,1)S(1)}, bf16[272,768]{1,0:T(8,128)(2,1)S(1)}, u32[]{:S(2)}, u32[]{:S(2)}) collective-permute-start(bf16[272,768]{1,0:T(8,128)(2,1)S(1)} %get-tuple-element.34.event.own), channel_id=1, source_target_pairs={{8,4},{9,5},{10,6},{11,7},{24,20},{25,21},{26,22},{27,23}} | collective-permute-start | bytes 1253384 | tf_op jit(solution)/shard_map/ppermute | solution.py:464
  38.7 45.0 %collective-permute-start.17 = (bf16[272,768]{1,0:T(8,128)(2,1)S(1)}, bf16[272,768]{1,0:T(8,128)(2,1)S(1)}, u32[]{:S(2)}, u32[]{:S(2)}) collective-permute-start(bf16[272,768]{1,0:T(8,128)(2,1)S(1)} %collective-permute-done.14.t2), channel_id=1, source_target_pairs={{5,4},{21,20}} | collective-permute-start | bytes 1253384 | tf_op jit(solution)/shard_map/ppermute | solution.py:464
  69.3 16.9 %collective-permute-start.13 = (bf16[256,1024]{1,0:T(8,128)(2,1)S(1)}, bf16[256,1024]{1,0:T(8,128)(2,1)S(1)}, u32[]{:S(2)}, u32[]{:S(2)}) collective-permute-start(bf16[256,1024]{1,0:T(8,128)(2,1)S(1)} %hand_0.1.event), channel_id=1, source_target_pairs={{0,2},{1,3},{2,0},{3,1},{16,18},{17,19},{18,16},{19,17}} | collective-permute-start | bytes 1572872 | tf_op jit(solution)/shard_map/ppermute | solution.py:464
  82.3 1.4 %collective-permute-start.11 = (bf16[256,256]{1,0:T(8,128)(2,1)S(1)}, bf16[256,256]{1,0:T(8,128)(2,1)S(1)}, u32[]{:S(2)}, u32[]{:S(2)}) collective-permute-start(bf16[256,256]{1,0:T(8,128)(2,1)S(1)} %get-tuple-element.37), channel_id=1, source_target_pairs={{12,13},{13,14},{14,15},{15,12},{8,9},{9,10},{10,11},{11,8},{28,29... | collective-permute-start | bytes 393224 | tf_op jit(solution)/shard_map/ppermute | solution.py:464
  83.0 12.4 %copy-start.8 = (f32[8,256]{1,0:T(8,128)S(1)}, f32[8,256]{1,0:T(8,128)}, u32[]{:S(2)}) copy-start(f32[8,256]{1,0:T(8,128)} %offset.8) | copy-start | bytes 24580
  83.0 12.4 %copy-start.9 = (f32[8,256]{1,0:T(8,128)S(1)}, f32[8,256]{1,0:T(8,128)}, u32[]{:S(2)}) copy-start(f32[8,256]{1,0:T(8,128)} %var.1) | copy-start | bytes 24580
  83.0 0.7 collective-permute-start.12
  86.8 8.6 %collective-permute-start.19 = (bf16[4,272,768]{2,1,0:T(8,128)(2,1)S(1)}, bf16[4,272,768]{2,1,0:T(8,128)(2,1)S(1)}, u32[]{:S(2)}, u32[]{:S(2)}) collective-permute-start(bf16[4,272,768]{2,1,0:T(8,128)(2,1)S(1)} %turn.1.ends_1), channel_id=1, source_target_pairs={{4,0},{5,1},{6,2},{7,3},{20,16},{21,17},{22,18},{23,19}} | collective-permute-start | bytes 5013512 | tf_op jit(solution)/shard_map/ppermute | solution.py:464
  88.1 22.5 %collective-permute-start.23 = (bf16[256,1024]{1,0:T(8,128)(2,1)S(1)}, bf16[256,1024]{1,0:T(8,128)(2,1)S(1)}, u32[]{:S(2)}, u32[]{:S(2)}) collective-permute-start(bf16[256,1024]{1,0:T(8,128)(2,1)S(1)} %hand_0.1.event), channel_id=1, source_target_pairs={{1,0},{2,1},{3,2},{0,3},{17,16},{18,17},{19,18},{16,19}} | collective-permute-start | bytes 1572872 | tf_op jit(solution)/shard_map/ppermute | solution.py:464
  91.6 18.9 %collective-permute-start.24 = (bf16[256,1024]{1,0:T(8,128)(2,1)S(1)}, bf16[256,1024]{1,0:T(8,128)(2,1)S(1)}, u32[]{:S(2)}, u32[]{:S(2)}) collective-permute-start(bf16[256,1024]{1,0:T(8,128)(2,1)S(1)} %hand_0.1.event), channel_id=1, source_target_pairs={{0,1},{1,2},{2,3},{3,0},{16,17},{17,18},{18,19},{19,16}} | collective-permute-start | bytes 1572872 | tf_op jit(solution)/shard_map/ppermute | solution.py:464
  101.5 9.1 %collective-permute-start.20 = (f32[2,8,256]{2,1,0:T(8,128)S(1)}, f32[2,8,256]{2,1,0:T(8,128)S(1)}, u32[]{:S(2)}, u32[]{:S(2)}) collective-permute-start(f32[2,8,256]{2,1,0:T(8,128)S(1)} %get-tuple-element.43.s0), channel_id=1, source_target_pairs={{1,0},{2,1},{3,2},{0,3},{5,4},{6,5},{7,6},{4,7},{9,8},{10,9},{11,1... | collective-permute-start | bytes 49160 | tf_op jit(solution)/shard_map/ppermute | solution.py:464
  104.6 6.0 %collective-permute-start.21 = (f32[2,8,256]{2,1,0:T(8,128)S(1)}, f32[2,8,256]{2,1,0:T(8,128)S(1)}, u32[]{:S(2)}, u32[]{:S(2)}) collective-permute-start(f32[2,8,256]{2,1,0:T(8,128)S(1)} %get-tuple-element.43.s0), channel_id=1, source_target_pairs={{2,0},{3,1},{0,2},{1,3},{6,4},{7,5},{4,6},{5,7},{10,8},{11,9},{8,1... | collective-permute-start | bytes 49160 | tf_op jit(solution)/shard_map/ppermute | solution.py:464
  105.0 5.6 %collective-permute-start.22 = (f32[2,8,256]{2,1,0:T(8,128)S(1)}, f32[2,8,256]{2,1,0:T(8,128)S(1)}, u32[]{:S(2)}, u32[]{:S(2)}) collective-permute-start(f32[2,8,256]{2,1,0:T(8,128)S(1)} %get-tuple-element.43.s0), channel_id=1, source_target_pairs={{3,0},{0,1},{1,2},{2,3},{7,4},{4,5},{5,6},{6,7},{11,8},{8,9},{9,10... | collective-permute-start | bytes 49160 | tf_op jit(solution)/shard_map/ppermute | solution.py:464
  107.1 3.6 %copy-start.6 = (f32[8,4,128]{2,1,0:T(4,128)S(1)}, f32[8,4,128]{2,1,0:T(4,128)}, u32[]{:S(2)}) copy-start(f32[8,4,128]{2,1,0:T(4,128)} %value.1) | copy-start | bytes 49156
  107.1 3.6 %copy-start.10 = (f32[1024]{0:T(1024)S(1)}, f32[1024]{0:T(1024)}, u32[]{:S(2)}) copy-start(f32[1024]{0:T(1024)} %param.23) | copy-start | bytes 12292
  107.1 3.6 %copy-start.12 = (s32[8,4]{0,1:T(4,128)S(1)}, s32[8,4]{0,1:T(4,128)}, u32[]{:S(2)}) copy-start(s32[8,4]{0,1:T(4,128)} %param.20) | copy-start | bytes 388
  107.1 3.6 %copy-start.13 = (s32[8]{0:T(128)S(1)}, s32[8]{0:T(128)}, u32[]{:S(2)}) copy-start(s32[8]{0:T(128)} %counts.1) | copy-start | bytes 100

commit v8 on v7

--- a/solution.py
+++ b/solution.py
@@ -506,7 +506,8 @@
     back, two_on, on = ((1, 0), (2, 1), (3, 2), (0, 3)), ((0, 2), (1, 3), (2, 0), (3, 1)), ((0, 1), (1, 2), (2, 3), (3, 0))
     pair_gains = [route(gain, within((3, 2, 1), back)), route(gain, within((3, 2), ((2, 0), (1, 3))) + within((1,), on))]
     parcel = pack(pack_kernel, "pack", parcel_shape, (end_cov, noise), (end_mean, seg_offset), pltpu.SemaphoreType.DMA((3,)), ALL_VMEM)
-    first = [send(parcel, ((0 if a == 2 else 3, 3), (1, 1)), a) for a in range(1, RING)]
+    far_moves = [((0 if to else 3, start), (3, to)) for start, to in two_on] + within((1,), two_on)
+    first = [send(parcel, ((3, 3), (1, 1)), 1), route(parcel, far_moves), send(parcel, ((3, 3), (1, 1)), 3)]
 
     def hand(segment, event):
         kernel = functools.partial(hand_kernel, segment)

time: 114 us -> 117 us (1.026)
  starting transfers between devices: 39.4 us -> 49.2 us
  waiting for transfers between devices: 42.4 us -> 35.6 us
    ppermute x25, starting transfers between devices: 39.4 us -> 49.2 us  [route(): return lax.ppermute(block, ('tm', 'tile'), table)]
    ppermute x25, waiting for transfers between devices: 42.4 us -> 35.6 us  [route(): return lax.ppermute(block, ('tm', 'tile'), table)]
  transfers between devices with their start and end apart: 25 -> 25, of which waited for: 4 -> 5; matrix products, arithmetic and copies ran while one was open for 1% -> 1% of each run, Pallas kernels for 22% -> 22%
where the time goes in v8:
time: 117 us
  starting transfers between devices  49.2 us (42%)
  waiting for transfers between devices  35.6 us (30%)
  Pallas kernels  29.4 us (25%)
  between operations  1.3 us (1%)
    ppermute x25, starting transfers between devices, route(): return lax.ppermute(block, ('tm', 'tile'), table)  49.2 us
    ppermute x25, waiting for transfers between devices, route(): return lax.ppermute(block, ('tm', 'tile'), table)  35.6 us
    pallas_call x7, Pallas kernels, call(): pl.pallas_call(kernel, out_shape=out_shape, in_specs=[smem()] + [vmem()]...  22.8 us
    pallas_call x3, Pallas kernels, pack(): pl.pallas_call(kernel, out_shape=out_shape, in_specs=[smem()] + [pl.Block...  3.8 us
    pallas_call x1, Pallas kernels, ring_shards(): pl.pallas_call(innovation_kernel, out_shape=(shape(obs_value.shape, F32),...  2.75 us
  transfers between devices with their start and end apart: 25, of which 5 were waited for; matrix products, arithmetic and copies ran while one was open for 1% of the time, Pallas kernels for 22%

profile of v8, /device:TPU:0, one launch (start us, length us, event | category | flops | bytes accessed | tf_op | source)
XLA Modules:
  0.0 116.6 jit_solution(13944270700100648229)
XLA Ops:
  0.6 0.8 collective-permute-start
  1.5 0.7 collective-permute-start.1
  2.2 0.6 pad_add_fusion.where
  2.8 0.0 copy-start.11
  2.8 2.7 %pack.1.n0 = bf16[272,768]{1,0:T(8,128)(2,1)} custom-call(s32[3]{0:T(128)} %pad_add_fusion.where, bf16[2,256,1024]{2,1,0:T(8,128)(2,1)} %refs_0_.1, bf16[256,1024]{1,0:T(8,128)(2,1)} %bitcast.18, bf16[2,256]{1,0:T(2,128)(2,1)} %refs_1_.1, f32[1,256]{1,0:T(1,128)} %offset.9), custom_call_target="tpu_custom_call" | custom-call | bytes 1000000 | tf_op jit(solution)/shard_map/pack/pallas_call | solution.py:491
  5.5 12.2 %collective-permute-start.3 = (bf16[272,768]{1,0:T(8,128)(2,1)}, bf16[272,768]{1,0:T(8,128)(2,1)S(1)}, u32[]{:S(2)}, u32[]{:S(2)}) collective-permute-start(bf16[272,768]{1,0:T(8,128)(2,1)} %pack.1.n0), channel_id=1, source_target_pairs={{0,14},{1,15},{14,12},{3,13},{4,6},{5,7},{6,4},{7,5},{16,30},{17,3... | collective-permute-start | bytes 1253384 | tf_op jit(solution)/shard_map/ppermute | solution.py:464
  17.6 0.7 collective-permute-start.2
  18.3 0.7 collective-permute-start.4
  19.0 9.0 %collective-permute-done.3.refs_3_.event.n2 = bf16[272,768]{1,0:T(8,128)(2,1)S(1)} collective-permute-done((bf16[272,768]{1,0:T(8,128)(2,1)}, bf16[272,768]{1,0:T(8,128)(2,1)S(1)}, u32[]{:S(2)}, u32[]{:S(2)}) %collective-permute-start.3) | collective-permute-done | bytes 417824 | tf_op jit(solution)/shard_map/ppermute | solution.py:464
  28.1 0.6 hand_1.1
  28.6 0.7 collective-permute-start.9
  29.3 0.0 collective-permute-done.2.refs_2_.n1
  29.3 0.0 collective-permute-done.4.refs_4_.n3
  29.3 0.0 collective-permute-done.g1.a1
  29.4 0.0 collective-permute-done.1.g2.g3.a3
  29.4 0.6 pairs_3.1
  30.0 0.7 collective-permute-start.5
  30.7 0.7 collective-permute-start.6
  31.4 0.7 collective-permute-start.7
  32.1 0.7 collective-permute-start.8
  32.8 0.0 collective-permute-done.5.refs_0_
  32.8 0.0 collective-permute-done.6.refs_1_
  32.8 0.0 collective-permute-done.7.refs_2_
  32.8 0.0 collective-permute-done.8.refs_3_
  32.8 0.0 copy-start.4
  32.8 0.6 pairs_2.1
  33.4 0.0 collective-permute-done.9.g2.a2
  33.4 0.4 copy-done.4
  33.8 0.5 stack.17
  34.4 0.0 copy-start.3
  34.4 1.6 %collective-permute-start.10 = (bf16[2064,1024]{1,0:T(8,128)(2,1)S(1)}, bf16[2064,1024]{1,0:T(8,128)(2,1)S(1)}, u32[]{:S(2)}, u32[]{:S(2)}) collective-permute-start(bf16[2064,1024]{1,0:T(8,128)(2,1)S(1)} %stack.17), channel_id=1, source_target_pairs={{4,0},{5,1},{6,2},{7,3},{20,16},{21,17},{22,18},{23,19}} | collective-permute-start | bytes 12681224 | tf_op jit(solution)/shard_map/ppermute | solution.py:464
  35.9 0.7 collective-permute-start.14
  36.6 0.7 collective-permute-start.15
  37.3 0.7 collective-permute-start.16
  38.0 0.7 collective-permute-start.18
  38.7 0.0 collective-permute-done.14.t2
  38.7 0.7 collective-permute-start.17
  39.4 18.0 %collective-permute-done.10.event.lift = bf16[2064,1024]{1,0:T(8,128)(2,1)S(1)} collective-permute-done((bf16[2064,1024]{1,0:T(8,128)(2,1)S(1)}, bf16[2064,1024]{1,0:T(8,128)(2,1)S(1)}, u32[]{:S(2)}, u32[]{:S(2)}) %collective-permute-start.10) | collective-permute-done | bytes 4227104 | tf_op jit(solution)/shard_map/ppermute | solution.py:464
  57.4 0.6 hand_0.1.event
  58.0 13.3 %collective-permute-start.13 = (bf16[256,1024]{1,0:T(8,128)(2,1)S(1)}, bf16[256,1024]{1,0:T(8,128)(2,1)S(1)}, u32[]{:S(2)}, u32[]{:S(2)}) collective-permute-start(bf16[256,1024]{1,0:T(8,128)(2,1)S(1)} %hand_0.1.event), channel_id=1, source_target_pairs={{0,2},{1,3},{2,0},{3,1},{16,18},{17,19},{18,16},{19,17}} | collective-permute-start | bytes 1572872 | tf_op jit(solution)/shard_map/ppermute | solution.py:464
  71.3 11.0 %ahead.1 = (bf16[8,256,1024]{2,1,0:T(8,128)(2,1)S(1)}, f32[8,256]{1,0:T(8,128)S(1)}, bf16[256,1024]{1,0:T(8,128)(2,1)S(1)}, f32[256,1024]{1,0:T(8,128)S(1)}, bf1...) custom-call(s32[3]{0:T(128)S(1)} %copy-done.5, bf16[256,1024]{1,0:T(8,128)(2,1)S(1)} %hand_0.1.event, ...), custom_call_target="tpu_custom_call" | custom-call | flops 9663676416 | bytes 15769600 | tf_op jit(solution)/shard_map/ahead/pallas_call | solution.py:478
  82.3 0.0 collective-permute-done.15.t1
  82.3 0.7 collective-permute-start.11
  83.0 0.0 collective-permute-done.16.t3
  83.0 0.0 copy-start.8
  83.0 0.0 copy-start.9
  83.0 0.7 collective-permute-start.12
  83.7 0.0 collective-permute-done.18.t0
  83.7 0.0 collective-permute-done.17.t4
  83.7 0.0 collective-permute-done.11.near
  83.8 0.3 collective-permute-done.13.b2
  84.1 0.5 turn.1.ends_1
  84.6 1.3 %collective-permute-start.19 = (bf16[4,272,768]{2,1,0:T(8,128)(2,1)S(1)}, bf16[4,272,768]{2,1,0:T(8,128)(2,1)S(1)}, u32[]{:S(2)}, u32[]{:S(2)}) collective-permute-start(bf16[4,272,768]{2,1,0:T(8,128)(2,1)S(1)} %turn.1.ends_1), channel_id=1, source_target_pairs={{4,0},{5,1},{6,2},{7,3},{20,16},{21,17},{22,18},{23,19}} | collective-permute-start | bytes 5013512 | tf_op jit(solution)/shard_map/ppermute | solution.py:464
  85.9 5.7 %collective-permute-start.23 = (bf16[256,1024]{1,0:T(8,128)(2,1)S(1)}, bf16[256,1024]{1,0:T(8,128)(2,1)S(1)}, u32[]{:S(2)}, u32[]{:S(2)}) collective-permute-start(bf16[256,1024]{1,0:T(8,128)(2,1)S(1)} %hand_0.1.event), channel_id=1, source_target_pairs={{1,0},{2,1},{3,2},{0,3},{17,16},{18,17},{19,18},{16,19}} | collective-permute-start | bytes 1572872 | tf_op jit(solution)/shard_map/ppermute | solution.py:464
  91.6 1.9 %collective-permute-start.24 = (bf16[256,1024]{1,0:T(8,128)(2,1)S(1)}, bf16[256,1024]{1,0:T(8,128)(2,1)S(1)}, u32[]{:S(2)}, u32[]{:S(2)}) collective-permute-start(bf16[256,1024]{1,0:T(8,128)(2,1)S(1)} %hand_0.1.event), channel_id=1, source_target_pairs={{0,1},{1,2},{2,3},{3,0},{16,17},{17,18},{18,19},{19,16}} | collective-permute-start | bytes 1572872 | tf_op jit(solution)/shard_map/ppermute | solution.py:464
  93.6 6.7 %collective-permute-done.19.ends_0 = bf16[4,272,768]{2,1,0:T(8,128)(2,1)S(1)} collective-permute-done((bf16[4,272,768]{2,1,0:T(8,128)(2,1)S(1)}, bf16[4,272,768]{2,1,0:T(8,128)(2,1)S(1)}, u32[]{:S(2)}, u32[]{:S(2)}) %collective-permute-start.19) | collective-permute-done | bytes 1671200 | tf_op jit(solution)/shard_map/ppermute | solution.py:464
  100.3 6.1 %moments.1 = (bf16[4,768,256]{2,1,0:T(8,128)(2,1)S(1)}, bf16[16,1024]{1,0:T(8,128)(2,1)S(1)}, f32[8,256]{1,0:T(8,128)}, f32[8,256]{1,0:T(8,128)}, f32[2,8,256]{2,1,0:T(8,128)S(1)}) custom-call(s32[3]{0:T(128)S(1)} %copy-done.5, bf16[4,272,768]{2,1,0:T(8,128)(2,1)S(1)} %turn.1.ends_1, ...), custom_call_target="tpu_custom_call", output_to_operand_aliasing={{0}: (9, {}), {1}: (10, {})} | custom-call | flops 4294967296 | bytes 19226624 | tf_op jit(solution)/shard_map/moments/pallas_call | solution.py:478
  106.4 1.7 %collective-permute-start.21 = (f32[2,8,256]{2,1,0:T(8,128)S(1)}, f32[2,8,256]{2,1,0:T(8,128)S(1)}, u32[]{:S(2)}, u32[]{:S(2)}) collective-permute-start(f32[2,8,256]{2,1,0:T(8,128)S(1)} %get-tuple-element.43.s0), channel_id=1, source_target_pairs={{2,0},{3,1},{0,2},{1,3},{6,4},{7,5},{4,6},{5,7},{10,8},{11,9},{8,1... | collective-permute-start | bytes 49160 | tf_op jit(solution)/shard_map/ppermute | solution.py:464
  108.1 0.4 collective-permute-start.22
  108.5 3.5 %last.1 = (bf16[256,1024]{1,0:T(8,128)(2,1)}, bf16[16,256]{1,0:T(8,128)(2,1)S(1)}, bf16[256,1024]{1,0:T(8,128)(2,1)S(1)}) custom-call(s32[3]{0:T(128)S(1)} %copy-done.5, bf16[256,1024]{1,0:T(8,128)(2,1)S(1)} %bitcast.16, bf16[256,1024]{1,0:T(8,128)(2,1)S(1)} %collective-permute-done.g1.a1, bf16[256,1024]{1,0:T(8,128)(2,1)S(1)} %collective-permute-done.9.g2.a2, ...), custom_call_target="tpu_custom_call" | custom-call | flops 1073741824 | bytes 13534208 | tf_op jit(solution)/shard_map/last/pallas_call | solution.py:478
  112.0 0.0 collective-permute-done.23.b1
  112.1 0.0 collective-permute-done.21.s2
  112.1 1.6 %collective-permute-done.22.s3 = f32[2,8,256]{2,1,0:T(8,128)S(1)} collective-permute-done((f32[2,8,256]{2,1,0:T(8,128)S(1)}, f32[2,8,256]{2,1,0:T(8,128)S(1)}, u32[]{:S(2)}, u32[]{:S(2)}) %collective-permute-start.22) | collective-permute-done | bytes 16416 | tf_op jit(solution)/shard_map/ppermute | solution.py:464
  113.6 2.8 %innovation.1 = (f32[8,4,128]{2,1,0:T(4,128)}, bf16[1,256]{1,0:T(2,128)(2,1)}, bf16[256,1024]{1,0:T(8,128)(2,1)}) custom-call(s32[3]{0:T(128)S(1)} %copy-done.5, s32[4,8]{1,0:T(4,128)S(1)} %bitcast.24, s32[8]{0:T(128)S(1)} %copy-done.13, f32[2,8,256]{2,1,0:T(8,128)S(1)} %get-tuple-element.43.s0, ...), custom_call_target="tpu_custom_call", output_to_operand_aliasing={{2}: (18, {})} | custom-call | bytes 200000 | tf_op jit(solution)/shard_map/innovation/pallas_call | solution.py:580
  (26 shorter events, 0.1 us)
Async XLA Ops:
  0.6 27.4 %copy-start = (bf16[1,256,1024]{2,1,0:T(8,128)(2,1)S(1)}, bf16[1,256,1024]{2,1,0:T(8,128)(2,1)}, u32[]{:S(2)}) copy-start(bf16[1,256,1024]{2,1,0:T(8,128)(2,1)} %param.12) | copy-start | bytes 1572868
  0.6 28.7 %collective-permute-start = (bf16[256,1024]{1,0:T(8,128)(2,1)}, bf16[256,1024]{1,0:T(8,128)(2,1)S(1)}, u32[]{:S(2)}, u32[]{:S(2)}) collective-permute-start(bf16[256,1024]{1,0:T(8,128)(2,1)} %bitcast.8), channel_id=1, source_target_pairs={{13,12},{14,13},{15,14},{12,15},{9,8},{10,9},{11,10},{8,11},{5,4},... | collective-permute-start | bytes 1572872 | tf_op jit(solution)/shard_map/ppermute | solution.py:464
  1.5 27.9 %collective-permute-start.1 = (bf16[256,1024]{1,0:T(8,128)(2,1)}, bf16[256,1024]{1,0:T(8,128)(2,1)S(1)}, u32[]{:S(2)}, u32[]{:S(2)}) collective-permute-start(bf16[256,1024]{1,0:T(8,128)(2,1)} %bitcast.9), channel_id=1, source_target_pairs={{14,12},{13,15},{10,8},{9,11},{4,5},{5,6},{6,7},{7,4},{30,28},{29,... | collective-permute-start | bytes 1572872 | tf_op jit(solution)/shard_map/ppermute | solution.py:464
  2.8 25.3 %copy-start.5 = (s32[3]{0:T(128)S(1)}, s32[3]{0:T(128)}, u32[]{:S(2)}) copy-start(s32[3]{0:T(128)} %pad_add_fusion.where) | copy-start | bytes 40
  2.8 26.6 %copy-start.1 = (bf16[1,256,1024]{2,1,0:T(8,128)(2,1)S(1)}, bf16[1,256,1024]{2,1,0:T(8,128)(2,1)}, u32[]{:S(2)}) copy-start(bf16[1,256,1024]{2,1,0:T(8,128)(2,1)} %param.14) | copy-start | bytes 1572868
  2.8 26.6 %copy-start.2 = (bf16[2,256,1024]{2,1,0:T(8,128)(2,1)S(1)}, bf16[2,256,1024]{2,1,0:T(8,128)(2,1)}, u32[]{:S(2)}) copy-start(bf16[2,256,1024]{2,1,0:T(8,128)(2,1)} %refs_0_.1) | copy-start | bytes 3145732
  2.8 26.6 %copy-start.7 = (f32[1,256]{1,0:T(1,128)S(1)}, f32[1,256]{1,0:T(1,128)}, u32[]{:S(2)}) copy-start(f32[1,256]{1,0:T(1,128)} %offset.9) | copy-start | bytes 3076
  2.8 26.6 %copy-start.11 = (bf16[2,256]{1,0:T(2,128)(2,1)S(1)}, bf16[2,256]{1,0:T(2,128)(2,1)}, u32[]{:S(2)}) copy-start(bf16[2,256]{1,0:T(2,128)(2,1)} %refs_1_.1) | copy-start | bytes 3076
  5.5 22.6 %collective-permute-start.3 = (bf16[272,768]{1,0:T(8,128)(2,1)}, bf16[272,768]{1,0:T(8,128)(2,1)S(1)}, u32[]{:S(2)}, u32[]{:S(2)}) collective-permute-start(bf16[272,768]{1,0:T(8,128)(2,1)} %pack.1.n0), channel_id=1, source_target_pairs={{0,14},{1,15},{14,12},{3,13},{4,6},{5,7},{6,4},{7,5},{16,30},{17,3... | collective-permute-start | bytes 1253384 | tf_op jit(solution)/shard_map/ppermute | solution.py:464
  17.6 11.7 %collective-permute-start.2 = (bf16[272,768]{1,0:T(8,128)(2,1)}, bf16[272,768]{1,0:T(8,128)(2,1)S(1)}, u32[]{:S(2)}, u32[]{:S(2)}) collective-permute-start(bf16[272,768]{1,0:T(8,128)(2,1)} %pack.1.n0), channel_id=1, source_target_pairs={{13,12},{14,13},{15,14},{12,15},{5,4},{6,5},{7,6},{4,7},{29,28},{3... | collective-permute-start | bytes 1253384 | tf_op jit(solution)/shard_map/ppermute | solution.py:464
  18.3 11.0 %collective-permute-start.4 = (bf16[272,768]{1,0:T(8,128)(2,1)}, bf16[272,768]{1,0:T(8,128)(2,1)S(1)}, u32[]{:S(2)}, u32[]{:S(2)}) collective-permute-start(bf16[272,768]{1,0:T(8,128)(2,1)} %pack.1.n0), channel_id=1, source_target_pairs={{15,12},{12,13},{13,14},{14,15},{7,4},{4,5},{5,6},{6,7},{31,28},{2... | collective-permute-start | bytes 1253384 | tf_op jit(solution)/shard_map/ppermute | solution.py:464
  28.6 4.8 %collective-permute-start.9 = (bf16[256,1024]{1,0:T(8,128)(2,1)S(1)}, bf16[256,1024]{1,0:T(8,128)(2,1)S(1)}, u32[]{:S(2)}, u32[]{:S(2)}) collective-permute-start(bf16[256,1024]{1,0:T(8,128)(2,1)S(1)} %hand_1.1), channel_id=1, source_target_pairs={{4,6},{5,7},{6,4},{7,5},{20,22},{21,23},{22,20},{23,21}} | collective-permute-start | bytes 1572872 | tf_op jit(solution)/shard_map/ppermute | solution.py:464
  30.0 2.8 %collective-permute-start.5 = (bf16[272,768]{1,0:T(8,128)(2,1)S(1)}, bf16[272,768]{1,0:T(8,128)(2,1)S(1)}, u32[]{:S(2)}, u32[]{:S(2)}) collective-permute-start(bf16[272,768]{1,0:T(8,128)(2,1)S(1)} %get-tuple-element.31.refs_4_), channel_id=1, source_target_pairs={{14,8},{15,9},{12,10},{13,11},{30,24},{31,25},{28,26},{29,27}} | collective-permute-start | bytes 1253384 | tf_op jit(solution)/shard_map/ppermute | solution.py:464
  30.7 2.1 %collective-permute-start.6 = (bf16[272,768]{1,0:T(8,128)(2,1)S(1)}, bf16[272,768]{1,0:T(8,128)(2,1)S(1)}, u32[]{:S(2)}, u32[]{:S(2)}) collective-permute-start(bf16[272,768]{1,0:T(8,128)(2,1)S(1)} %get-tuple-element.31.refs_4_), channel_id=1, source_target_pairs={{13,8},{14,9},{15,10},{12,11},{29,24},{30,25},{31,26},{28,27}} | collective-permute-start | bytes 1253384 | tf_op jit(solution)/shard_map/ppermute | solution.py:464
  31.4 1.4 %collective-permute-start.7 = (bf16[272,768]{1,0:T(8,128)(2,1)S(1)}, bf16[272,768]{1,0:T(8,128)(2,1)S(1)}, u32[]{:S(2)}, u32[]{:S(2)}) collective-permute-start(bf16[272,768]{1,0:T(8,128)(2,1)S(1)} %get-tuple-element.31.refs_4_), channel_id=1, source_target_pairs={{15,8},{12,9},{13,10},{14,11},{31,24},{28,25},{29,26},{30,27}} | collective-permute-start | bytes 1253384 | tf_op jit(solution)/shard_map/ppermute | solution.py:464
  32.1 0.7 collective-permute-start.8
  32.8 1.0 copy-start.4
  34.4 36.9 %copy-start.3 = (bf16[8,256,1024]{2,1,0:T(8,128)(2,1)S(1)}, bf16[8,256,1024]{2,1,0:T(8,128)(2,1)}, u32[]{:S(2)}) copy-start(bf16[8,256,1024]{2,1,0:T(8,128)(2,1)} %gain.1) | copy-start | bytes 12582916
  34.4 23.0 %collective-permute-start.10 = (bf16[2064,1024]{1,0:T(8,128)(2,1)S(1)}, bf16[2064,1024]{1,0:T(8,128)(2,1)S(1)}, u32[]{:S(2)}, u32[]{:S(2)}) collective-permute-start(bf16[2064,1024]{1,0:T(8,128)(2,1)S(1)} %stack.17), channel_id=1, source_target_pairs={{4,0},{5,1},{6,2},{7,3},{20,16},{21,17},{22,18},{23,19}} | collective-permute-start | bytes 12681224 | tf_op jit(solution)/shard_map/ppermute | solution.py:464
  35.9 2.8 %collective-permute-start.14 = (bf16[272,768]{1,0:T(8,128)(2,1)S(1)}, bf16[272,768]{1,0:T(8,128)(2,1)S(1)}, u32[]{:S(2)}, u32[]{:S(2)}) collective-permute-start(bf16[272,768]{1,0:T(8,128)(2,1)S(1)} %get-tuple-element.34.event.own), channel_id=1, source_target_pairs={{10,4},{11,5},{8,6},{9,7},{26,20},{27,21},{24,22},{25,23}} | collective-permute-start | bytes 1253384 | tf_op jit(solution)/shard_map/ppermute | solution.py:464
  36.6 45.7 %collective-permute-start.15 = (bf16[272,768]{1,0:T(8,128)(2,1)S(1)}, bf16[272,768]{1,0:T(8,128)(2,1)S(1)}, u32[]{:S(2)}, u32[]{:S(2)}) collective-permute-start(bf16[272,768]{1,0:T(8,128)(2,1)S(1)} %get-tuple-element.34.event.own), channel_id=1, source_target_pairs={{9,4},{10,5},{11,6},{8,7},{25,20},{26,21},{27,22},{24,23}} | collective-permute-start | bytes 1253384 | tf_op jit(solution)/shard_map/ppermute | solution.py:464
  37.3 45.7 %collective-permute-start.16 = (bf16[272,768]{1,0:T(8,128)(2,1)S(1)}, bf16[272,768]{1,0:T(8,128)(2,1)S(1)}, u32[]{:S(2)}, u32[]{:S(2)}) collective-permute-start(bf16[272,768]{1,0:T(8,128)(2,1)S(1)} %get-tuple-element.34.event.own), channel_id=1, source_target_pairs={{8,5},{9,6},{10,7},{24,21},{25,22},{26,23}} | collective-permute-start | bytes 1253384 | tf_op jit(solution)/shard_map/ppermute | solution.py:464
  38.0 45.7 %collective-permute-start.18 = (bf16[272,768]{1,0:T(8,128)(2,1)S(1)}, bf16[272,768]{1,0:T(8,128)(2,1)S(1)}, u32[]{:S(2)}, u32[]{:S(2)}) collective-permute-start(bf16[272,768]{1,0:T(8,128)(2,1)S(1)} %get-tuple-element.34.event.own), channel_id=1, source_target_pairs={{8,4},{9,5},{10,6},{11,7},{24,20},{25,21},{26,22},{27,23}} | collective-permute-start | bytes 1253384 | tf_op jit(solution)/shard_map/ppermute | solution.py:464
  38.7 45.0 %collective-permute-start.17 = (bf16[272,768]{1,0:T(8,128)(2,1)S(1)}, bf16[272,768]{1,0:T(8,128)(2,1)S(1)}, u32[]{:S(2)}, u32[]{:S(2)}) collective-permute-start(bf16[272,768]{1,0:T(8,128)(2,1)S(1)} %collective-permute-done.14.t2), channel_id=1, source_target_pairs={{5,4},{21,20}} | collective-permute-start | bytes 1253384 | tf_op jit(solution)/shard_map/ppermute | solution.py:464
  58.0 26.1 %collective-permute-start.13 = (bf16[256,1024]{1,0:T(8,128)(2,1)S(1)}, bf16[256,1024]{1,0:T(8,128)(2,1)S(1)}, u32[]{:S(2)}, u32[]{:S(2)}) collective-permute-start(bf16[256,1024]{1,0:T(8,128)(2,1)S(1)} %hand_0.1.event), channel_id=1, source_target_pairs={{0,2},{1,3},{2,0},{3,1},{16,18},{17,19},{18,16},{19,17}} | collective-permute-start | bytes 1572872 | tf_op jit(solution)/shard_map/ppermute | solution.py:464
  82.3 1.4 %collective-permute-start.11 = (bf16[256,256]{1,0:T(8,128)(2,1)S(1)}, bf16[256,256]{1,0:T(8,128)(2,1)S(1)}, u32[]{:S(2)}, u32[]{:S(2)}) collective-permute-start(bf16[256,256]{1,0:T(8,128)(2,1)S(1)} %get-tuple-element.37), channel_id=1, source_target_pairs={{12,13},{13,14},{14,15},{15,12},{8,9},{9,10},{10,11},{11,8},{28,29... | collective-permute-start | bytes 393224 | tf_op jit(solution)/shard_map/ppermute | solution.py:464
  83.0 17.3 %copy-start.8 = (f32[8,256]{1,0:T(8,128)S(1)}, f32[8,256]{1,0:T(8,128)}, u32[]{:S(2)}) copy-start(f32[8,256]{1,0:T(8,128)} %offset.8) | copy-start | bytes 24580
  83.0 17.3 %copy-start.9 = (f32[8,256]{1,0:T(8,128)S(1)}, f32[8,256]{1,0:T(8,128)}, u32[]{:S(2)}) copy-start(f32[8,256]{1,0:T(8,128)} %var.1) | copy-start | bytes 24580
  83.0 0.7 collective-permute-start.12
  84.6 15.7 %collective-permute-start.19 = (bf16[4,272,768]{2,1,0:T(8,128)(2,1)S(1)}, bf16[4,272,768]{2,1,0:T(8,128)(2,1)S(1)}, u32[]{:S(2)}, u32[]{:S(2)}) collective-permute-start(bf16[4,272,768]{2,1,0:T(8,128)(2,1)S(1)} %turn.1.ends_1), channel_id=1, source_target_pairs={{4,0},{5,1},{6,2},{7,3},{20,16},{21,17},{22,18},{23,19}} | collective-permute-start | bytes 5013512 | tf_op jit(solution)/shard_map/ppermute | solution.py:464
  85.9 26.1 %collective-permute-start.23 = (bf16[256,1024]{1,0:T(8,128)(2,1)S(1)}, bf16[256,1024]{1,0:T(8,128)(2,1)S(1)}, u32[]{:S(2)}, u32[]{:S(2)}) collective-permute-start(bf16[256,1024]{1,0:T(8,128)(2,1)S(1)} %hand_0.1.event), channel_id=1, source_target_pairs={{1,0},{2,1},{3,2},{0,3},{17,16},{18,17},{19,18},{16,19}} | collective-permute-start | bytes 1572872 | tf_op jit(solution)/shard_map/ppermute | solution.py:464
  91.6 20.4 %collective-permute-start.24 = (bf16[256,1024]{1,0:T(8,128)(2,1)S(1)}, bf16[256,1024]{1,0:T(8,128)(2,1)S(1)}, u32[]{:S(2)}, u32[]{:S(2)}) collective-permute-start(bf16[256,1024]{1,0:T(8,128)(2,1)S(1)} %hand_0.1.event), channel_id=1, source_target_pairs={{0,1},{1,2},{2,3},{3,0},{16,17},{17,18},{18,19},{19,16}} | collective-permute-start | bytes 1572872 | tf_op jit(solution)/shard_map/ppermute | solution.py:464
  106.4 5.7 %collective-permute-start.20 = (f32[2,8,256]{2,1,0:T(8,128)S(1)}, f32[2,8,256]{2,1,0:T(8,128)S(1)}, u32[]{:S(2)}, u32[]{:S(2)}) collective-permute-start(f32[2,8,256]{2,1,0:T(8,128)S(1)} %get-tuple-element.43.s0), channel_id=1, source_target_pairs={{1,0},{2,1},{3,2},{0,3},{5,4},{6,5},{7,6},{4,7},{9,8},{10,9},{11,1... | collective-permute-start | bytes 49160 | tf_op jit(solution)/shard_map/ppermute | solution.py:464
  106.4 5.7 %collective-permute-start.21 = (f32[2,8,256]{2,1,0:T(8,128)S(1)}, f32[2,8,256]{2,1,0:T(8,128)S(1)}, u32[]{:S(2)}, u32[]{:S(2)}) collective-permute-start(f32[2,8,256]{2,1,0:T(8,128)S(1)} %get-tuple-element.43.s0), channel_id=1, source_target_pairs={{2,0},{3,1},{0,2},{1,3},{6,4},{7,5},{4,6},{5,7},{10,8},{11,9},{8,1... | collective-permute-start | bytes 49160 | tf_op jit(solution)/shard_map/ppermute | solution.py:464
  108.1 5.5 %collective-permute-start.22 = (f32[2,8,256]{2,1,0:T(8,128)S(1)}, f32[2,8,256]{2,1,0:T(8,128)S(1)}, u32[]{:S(2)}, u32[]{:S(2)}) collective-permute-start(f32[2,8,256]{2,1,0:T(8,128)S(1)} %get-tuple-element.43.s0), channel_id=1, source_target_pairs={{3,0},{0,1},{1,2},{2,3},{7,4},{4,5},{5,6},{6,7},{11,8},{8,9},{9,10... | collective-permute-start | bytes 49160 | tf_op jit(solution)/shard_map/ppermute | solution.py:464
  108.5 5.1 %copy-start.6 = (f32[8,4,128]{2,1,0:T(4,128)S(1)}, f32[8,4,128]{2,1,0:T(4,128)}, u32[]{:S(2)}) copy-start(f32[8,4,128]{2,1,0:T(4,128)} %value.1) | copy-start | bytes 49156
  108.5 5.1 %copy-start.10 = (f32[1024]{0:T(1024)S(1)}, f32[1024]{0:T(1024)}, u32[]{:S(2)}) copy-start(f32[1024]{0:T(1024)} %param.23) | copy-start | bytes 12292
  108.5 5.1 %copy-start.12 = (s32[8,4]{0,1:T(4,128)S(1)}, s32[8,4]{0,1:T(4,128)}, u32[]{:S(2)}) copy-start(s32[8,4]{0,1:T(4,128)} %param.20) | copy-start | bytes 388
  108.5 5.1 %copy-start.13 = (s32[8]{0:T(128)S(1)}, s32[8]{0:T(128)}, u32[]{:S(2)}) copy-start(s32[8]{0:T(128)} %counts.1) | copy-start | bytes 100
